TPU v7x, 32 devices: a whole 2x2x4 slice. The times are simulated.
32 devices in a mesh: seq: 16 (over z, y, core), ch: 2 (over x).
Axes of the slice: x: 2, y: 2, z: 4, core: 2. Of those that a mesh axis runs over, the one named last changes fastest.
Arguments:
- ids: int32 [2, 2048], P(None, 'seq'), may hold values from 0 to 15
- live: int32 [2], replicated, may hold values from 1024 to 2048
- embed: float32 [16, 256], replicated, may hold values from -6 to 6
- norm_gain: float32 [2, 2, 256], replicated, may hold values from 0.5 to 1.5
- in_weight: bfloat16 [2, 256, 3, 256], P(None, None, None, 'ch'), may hold values from -0.375 to 0.375
- short_kernel: float32 [2, 3, 3, 256], P(None, None, None, 'ch'), may hold values from -3 to 3
- filter_first: float32 [2, 33, 64], replicated, may hold values from -3 to 3
- filter_second: float32 [2, 64, 256], P(None, None, 'ch'), may hold values from -0.03125 to 0.03125
- skip_gain: float32 [2, 256], P(None, 'ch'), may hold values from -4 to 4
- out_weight: bfloat16 [2, 256, 256], P(None, 'ch'), may hold values from -0.375 to 0.375
- up_weight: bfloat16 [2, 256, 1024], P(None, None, 'ch'), may hold values from -0.375 to 0.375
- down_weight: bfloat16 [2, 1024, 256], P(None, 'ch'), may hold values from -0.375 to 0.375
- cotangent: float32 [2, 2048, 256], P(None, 'seq'), may hold values from -6 to 6
Outputs:
- block_out: float32 [2, 2048, 256], P(None, 'seq')
- grad_embed: float32 [16, 256], replicated
- grad_norm_gain: float32 [2, 2, 256], replicated
- grad_in_weight: float32 [2, 256, 3, 256], P(None, None, None, 'ch')
- grad_short_kernel: float32 [2, 3, 3, 256], P(None, None, None, 'ch')
- grad_filter_first: float32 [2, 33, 64], replicated
- grad_filter_second: float32 [2, 64, 256], P(None, None, 'ch')
- grad_skip_gain: float32 [2, 256], P(None, 'ch')
- grad_out_weight: float32 [2, 256, 256], P(None, 'ch')
- grad_up_weight: float32 [2, 256, 1024], P(None, None, 'ch')
- grad_down_weight: float32 [2, 1024, 256], P(None, 'ch')
All inputs are finite; a program needn't handle non-finite values.
Results may differ from a plain program's by a relative error of at most 0.012.
Values sent between devices are 32-bit elements; how exact they have to be, the bound alone decides.
No kernel may reach another device: no remote copies, remote signals or barrier semaphores. Data moves between devices by JAX's collectives and lax.ppermute only.
A program may use at most 128 MiB of HBM per device.

v0:
```python
import math

import jax
import jax.numpy as jnp
from jax import lax
from jax.sharding import PartitionSpec as P

D = 256
FEAT = 33


precise = lax.Precision.HIGHEST
epsilon = 1e-05


def passed_along(value, axis, steps):
    count = lax.axis_size(axis)
    leading, last = (max(0, -steps), min(count, count - steps))
    return lax.ppermute(value, axis, [(source, source + steps) for source in range(leading, last)])


def layer_norm(inputs, gain_vec):
    center = inputs - jnp.mean(inputs, axis=-1, keepdims=True)
    spread = jnp.mean(center * center, axis=-1, keepdims=True)
    return center * lax.rsqrt(spread + epsilon) * gain_vec


def position_features(length):
    places = jnp.arange(length, dtype=jnp.int32)
    band_ids = jnp.arange(1, (FEAT - 1) // 2 + 1, dtype=jnp.int32)
    turn_counts = places[:, None] * band_ids[None, :] % length
    angles = turn_counts.astype(jnp.float32) * (2.0 * math.pi / length)
    ramp_vals = places.astype(jnp.float32)[:, None] / length
    return jnp.concatenate([ramp_vals, jnp.cos(angles), jnp.sin(angles)], axis=1)


def decay_rates(channels):
    return 0.3 * 10.0 ** (channels.astype(jnp.float32) / (D - 1))


def dft_tables(blocks, block_len):
    doubled = 2 * blocks
    span_total = doubled * block_len
    frequency = jnp.arange(doubled, dtype=jnp.int32)
    places = jnp.arange(blocks, dtype=jnp.int32)
    inner_idx = jnp.arange(block_len, dtype=jnp.int32)
    outer_angle = (frequency[:, None] * places[None, :] % doubled).astype(jnp.float32) * (
        2.0 * math.pi / doubled
    )
    twist_angle = (frequency[:, None] * inner_idx[None, :] % span_total).astype(jnp.float32) * (
        2.0 * math.pi / span_total
    )
    inner_angle = (inner_idx[:, None] * inner_idx[None, :] % block_len).astype(jnp.float32) * (
        2.0 * math.pi / block_len
    )
    return (
        jnp.cos(outer_angle),
        jnp.sin(outer_angle),
        jnp.cos(twist_angle),
        jnp.sin(twist_angle),
        jnp.cos(inner_angle),
        jnp.sin(inner_angle),
    )


def along_block(values, table):
    return jnp.einsum("...kb,bj->...kj", values, table, precision=precise)


def to_spectrum(signal, tables):
    outer_cos, outer_sin, twist_cos, twist_sin, inner_cos, inner_sin = tables
    first_re = jnp.einsum("kp,...pb->...kb", outer_cos, signal, precision=precise)
    first_im = -jnp.einsum("kp,...pb->...kb", outer_sin, signal, precision=precise)
    turned_re = first_re * twist_cos + first_im * twist_sin
    turned_im = first_im * twist_cos - first_re * twist_sin
    spec_re = along_block(turned_re, inner_cos) + along_block(turned_im, inner_sin)
    spec_im = along_block(turned_im, inner_cos) - along_block(turned_re, inner_sin)
    return (spec_re, spec_im)


def from_spectrum(spec_re, spec_im, tables):
    outer_cos, outer_sin, twist_cos, twist_sin, inner_cos, inner_sin = tables
    back_re = along_block(spec_re, inner_cos) - along_block(spec_im, inner_sin)
    back_im = along_block(spec_re, inner_sin) + along_block(spec_im, inner_cos)
    turned_re = back_re * twist_cos - back_im * twist_sin
    turned_im = back_re * twist_sin + back_im * twist_cos
    scale_back = 1.0 / (outer_cos.shape[0] * inner_cos.shape[0])
    signal = jnp.einsum("kp,...kb->...pb", outer_cos, turned_re, precision=precise) - jnp.einsum(
        "kp,...kb->...pb", outer_sin, turned_im, precision=precise
    )
    return signal * scale_back


def causal_filter(received, filt_spec, skip_part, tables):
    item_count, chan_count, length = received.shape
    blocks = tables[0].shape[1]
    spec_re, spec_im = to_spectrum(
        received.reshape(item_count, chan_count, blocks, length // blocks), tables
    )
    prod_re = spec_re * filt_spec[0] - spec_im * filt_spec[1]
    prod_im = spec_re * filt_spec[1] + spec_im * filt_spec[0]
    result_sig = from_spectrum(prod_re, prod_im, tables).reshape(item_count, chan_count, length)
    return result_sig + skip_part[:, None] * received


def filter_backward(grad_cols, moved_in, filt_spec, skip_part, tables):
    item_count, chan_count, length = grad_cols.shape
    blocks = tables[0].shape[1]
    grad_re, grad_im = to_spectrum(
        grad_cols.reshape(item_count, chan_count, blocks, length // blocks), tables
    )
    input_re, input_im = to_spectrum(
        moved_in.reshape(item_count, chan_count, blocks, length // blocks), tables
    )
    back_re = grad_re * filt_spec[0] + grad_im * filt_spec[1]
    back_im = grad_im * filt_spec[0] - grad_re * filt_spec[1]
    grad_u_cols = (
        from_spectrum(back_re, back_im, tables).reshape(item_count, chan_count, length)
        + skip_part[:, None] * grad_cols
    )
    corr_re = grad_re * input_re + grad_im * input_im
    corr_im = grad_im * input_re - grad_re * input_im
    grad_filt = jnp.sum(from_spectrum(corr_re, corr_im, tables), axis=0).reshape(chan_count, length)
    grad_skip_part = jnp.sum(grad_cols * moved_in, axis=(0, 2))
    return (grad_u_cols, grad_filt, grad_skip_part)


def local_filter(first, second, features, select, group_idx, chan_local):
    hidden_pre = jnp.dot(features, first, precision=precise)
    hidden_act = jnp.sin(hidden_pre)
    chan_width = second.shape[1]
    second_part = jnp.dot(second, select, precision=precise)
    channel_ids = group_idx * chan_width + chan_local
    length = features.shape[0]
    ramp_vals = jnp.arange(length, dtype=jnp.int32).astype(jnp.float32) / length
    decay_part = jnp.exp(-decay_rates(channel_ids)[:, None] * ramp_vals[None, :])
    filt_cols = jnp.einsum("hc,th->ct", second_part, hidden_act, precision=precise) * decay_part
    return (filt_cols, hidden_pre, hidden_act, second_part, decay_part)


def filter_mlp_backward(grad_filt, features, filter_parts):
    hidden_pre, hidden_act, second_part, decay_part = filter_parts
    grad_shaped = grad_filt * decay_part
    grad_second_part = jnp.einsum("ct,th->hc", grad_shaped, hidden_act, precision=precise)
    grad_act = jnp.einsum("ct,hc->th", grad_shaped, second_part, precision=precise)
    grad_first = jnp.einsum(
        "tf,th->fh", features, grad_act * jnp.cos(hidden_pre), precision=precise
    )
    return (grad_first, grad_second_part)


def embed_lookup(ids, live, embed, seq_rank):
    tok_rows = ids.shape[1]
    places = seq_rank * tok_rows + jnp.arange(tok_rows, dtype=jnp.int32)
    keep_mask = (places[None, :] < live[:, None]).astype(jnp.float32)
    vocab_ids = jnp.arange(embed.shape[0], dtype=jnp.int32)
    onehot = (ids[:, :, None] == vocab_ids[None, None, :]).astype(jnp.float32) * keep_mask[
        :, :, None
    ]
    stream = jnp.einsum("mtv,vd->mtd", onehot, embed, precision=precise)
    return (stream, onehot, keep_mask)


def channel_total(partial_sum):
    return lax.psum(partial_sum, "ch")


def input_total(partial_sum):
    return lax.psum(partial_sum, "ch")


def layer_forward(stream, params, filt_spec, skip_part, tables):
    norm_gains, w_in, kernel, w_out, w_up, w_down = params
    normed = layer_norm(stream, norm_gains[0]).astype(jnp.bfloat16)
    mixed_in = jnp.einsum("mtd,dgc->mtgc", normed, w_in, preferred_element_type=jnp.float32)
    rim_rows = passed_along(mixed_in[:, -2:], "seq", 1)
    padded = jnp.concatenate([rim_rows, mixed_in], axis=1)
    micro_count, tok_rows = (mixed_in.shape[0], mixed_in.shape[1])
    chan_width = mixed_in.shape[3]
    gate_vals = (
        kernel[0] * mixed_in
        + kernel[1] * padded[:, 1 : tok_rows + 1]
        + kernel[2] * padded[:, 0:tok_rows]
    )
    product_in = gate_vals[:, :, 2] * gate_vals[:, :, 1]
    flat_rows = jnp.swapaxes(product_in, 1, 2).reshape(1, micro_count * chan_width, tok_rows)
    received = lax.all_to_all(flat_rows, "seq", split_axis=1, concat_axis=2, tiled=True)
    result_sig = causal_filter(received, filt_spec, skip_part, tables)
    conv_flat = lax.all_to_all(result_sig, "seq", split_axis=2, concat_axis=1, tiled=True)
    conv_out = jnp.swapaxes(conv_flat.reshape(micro_count, chan_width, tok_rows), 1, 2)
    gated_out = (conv_out * gate_vals[:, :, 0]).astype(jnp.bfloat16)
    mid_state = stream + channel_total(
        jnp.einsum("mtc,cd->mtd", gated_out, w_out, preferred_element_type=jnp.float32)
    )
    normed_mid = layer_norm(mid_state, norm_gains[1]).astype(jnp.bfloat16)
    pre_act = jnp.einsum("mtd,df->mtf", normed_mid, w_up, preferred_element_type=jnp.float32)
    hidden = jax.nn.gelu(pre_act).astype(jnp.bfloat16)
    new_stream = mid_state + channel_total(
        jnp.einsum("mtf,fd->mtd", hidden, w_down, preferred_element_type=jnp.float32)
    )
    kept_vals = (
        stream,
        normed,
        mixed_in,
        padded,
        gate_vals,
        received,
        conv_out,
        gated_out,
        mid_state,
        normed_mid,
        pre_act,
        hidden,
    )
    return (new_stream, kept_vals)


def layer_backward(grad_stream, kept_vals, params, filt_spec, skip_part, tables):
    norm_gains, w_in, kernel, w_out, w_up, w_down = params
    (
        stream,
        normed,
        mixed_in,
        padded,
        gate_vals,
        moved_in,
        conv_out,
        gated_out,
        mid_state,
        normed_mid,
        pre_act,
        hidden,
    ) = kept_vals
    micro_count, tok_rows = (mixed_in.shape[0], mixed_in.shape[1])
    chan_width = mixed_in.shape[3]
    grad_low = grad_stream.astype(jnp.bfloat16)
    grad_down = jnp.einsum("mtf,mtd->fd", hidden, grad_low, preferred_element_type=jnp.float32)
    grad_hidden = jnp.einsum("mtd,fd->mtf", grad_low, w_down, preferred_element_type=jnp.float32)
    _, gelu_back = jax.vjp(jax.nn.gelu, pre_act)
    grad_pre = gelu_back(grad_hidden)[0].astype(jnp.bfloat16)
    grad_up = jnp.einsum("mtd,mtf->df", normed_mid, grad_pre, preferred_element_type=jnp.float32)
    grad_normed_mid = input_total(
        jnp.einsum("mtf,df->mtd", grad_pre, w_up, preferred_element_type=jnp.float32)
    )
    _, norm_back_mid = jax.vjp(layer_norm, mid_state, norm_gains[1])
    grad_mid_norm, grad_gain_mid = norm_back_mid(grad_normed_mid)
    grad_mid = grad_stream + grad_mid_norm
    grad_mid_low = grad_mid.astype(jnp.bfloat16)
    grad_out = jnp.einsum(
        "mtc,mtd->cd", gated_out, grad_mid_low, preferred_element_type=jnp.float32
    )
    grad_gated = jnp.einsum("mtd,cd->mtc", grad_mid_low, w_out, preferred_element_type=jnp.float32)
    grad_conv = grad_gated * gate_vals[:, :, 0]
    grad_first_gate = grad_gated * conv_out
    grad_flat = jnp.swapaxes(grad_conv, 1, 2).reshape(1, micro_count * chan_width, tok_rows)
    grad_cols = lax.all_to_all(grad_flat, "seq", split_axis=1, concat_axis=2, tiled=True)
    grad_u_cols, grad_filt, grad_skip_part = filter_backward(
        grad_cols, moved_in, filt_spec, skip_part, tables
    )
    grad_back_flat = lax.all_to_all(grad_u_cols, "seq", split_axis=2, concat_axis=1, tiled=True)
    grad_product = jnp.swapaxes(grad_back_flat.reshape(micro_count, chan_width, tok_rows), 1, 2)
    grad_gates = jnp.stack(
        [grad_first_gate, grad_product * gate_vals[:, :, 2], grad_product * gate_vals[:, :, 1]],
        axis=2,
    )
    rim_back = passed_along(grad_gates[:, :2], "seq", -1)
    extended = jnp.concatenate([grad_gates, rim_back], axis=1)
    grad_mixed = (
        kernel[0] * grad_gates
        + kernel[1] * extended[:, 1 : tok_rows + 1]
        + kernel[2] * extended[:, 2 : tok_rows + 2]
    )
    grad_kernel = jnp.stack(
        [
            jnp.sum(grad_gates * mixed_in, axis=(0, 1)),
            jnp.sum(grad_gates * padded[:, 1 : tok_rows + 1], axis=(0, 1)),
            jnp.sum(grad_gates * padded[:, 0:tok_rows], axis=(0, 1)),
        ]
    )
    grad_mixed_low = grad_mixed.astype(jnp.bfloat16)
    grad_in = jnp.einsum(
        "mtd,mtgc->dgc", normed, grad_mixed_low, preferred_element_type=jnp.float32
    )
    grad_normed = input_total(
        jnp.einsum("mtgc,dgc->mtd", grad_mixed_low, w_in, preferred_element_type=jnp.float32)
    )
    _, norm_back_in = jax.vjp(layer_norm, stream, norm_gains[0])
    grad_stream_norm, grad_gain_in = norm_back_in(grad_normed)
    grad_before = grad_mid + grad_stream_norm
    layer_grads = (
        jnp.stack([grad_gain_in, grad_gain_mid]),
        grad_in,
        grad_kernel,
        grad_skip_part,
        grad_out,
        grad_up,
        grad_down,
    )
    return (grad_before, layer_grads, grad_filt)


def local(
    ids,
    live,
    embed,
    norm_gain,
    in_weight,
    short_kernel,
    filter_first,
    filter_second,
    skip_gain,
    out_weight,
    up_weight,
    down_weight,
    cotangent,
):
    seq_count = lax.axis_size("seq")
    seq_rank = lax.axis_index("seq")
    group_idx = lax.axis_index("ch")
    micro_count = ids.shape[0]
    tok_rows = ids.shape[1]
    length = tok_rows * seq_count
    chan_width = in_weight.shape[3]
    own_rows = micro_count * chan_width // seq_count
    layer_count = in_weight.shape[0]
    row_start = seq_rank * own_rows
    row_ids = row_start + jnp.arange(own_rows, dtype=jnp.int32)
    chan_local = row_ids % chan_width
    first_rows = (row_ids < chan_width).astype(jnp.float32)
    select = (jnp.arange(chan_width, dtype=jnp.int32)[:, None] == chan_local[None, :]).astype(
        jnp.float32
    )
    tables = dft_tables(seq_count, tok_rows)
    features = position_features(length)
    ramp_row = jnp.arange(length, dtype=jnp.int32).astype(jnp.float32) / length
    stream, onehot, keep_mask = embed_lookup(ids, live, embed, seq_rank)
    filters = []
    for level_idx in range(layer_count):
        filt_cols, hidden_pre, hidden_act, second_part, decay_part = local_filter(
            filter_first[level_idx],
            filter_second[level_idx],
            features,
            select,
            group_idx,
            chan_local,
        )
        filt_spec = to_spectrum(filt_cols.reshape(own_rows, seq_count, tok_rows), tables)
        skip_part = jnp.dot(skip_gain[level_idx], select, precision=precise)
        penalty_grad = 0.5 * length * ramp_row[None, :] * filt_cols * first_rows[:, None]
        params = (
            norm_gain[level_idx],
            in_weight[level_idx],
            short_kernel[level_idx],
            out_weight[level_idx],
            up_weight[level_idx],
            down_weight[level_idx],
        )
        filters.append(
            (
                params,
                filt_spec,
                skip_part,
                (hidden_pre, hidden_act, second_part, decay_part),
                penalty_grad,
            )
        )
    stored = []
    for level_idx in range(layer_count):
        params, filt_spec, skip_part, _, _ = filters[level_idx]
        layer_input = stream
        stream, kept_vals = layer_forward(stream, params, filt_spec, skip_part, tables)
        stored.append(layer_input)
    block_out = stream * keep_mask[:, :, None]
    grad_stream = cotangent * keep_mask[:, :, None]
    collected = [None] * layer_count
    first_grads = [None] * layer_count
    grad_embed = None
    for level_idx in reversed(range(layer_count)):
        params, filt_spec, skip_part, filter_parts, penalty_grad = filters[level_idx]
        _, kept_vals = layer_forward(stored[level_idx], params, filt_spec, skip_part, tables)
        grad_stream, layer_grads, grad_filt = layer_backward(
            grad_stream, kept_vals, params, filt_spec, skip_part, tables
        )
        grad_first, grad_second_part = filter_mlp_backward(
            grad_filt + penalty_grad, features, filter_parts
        )
        first_grads[level_idx] = grad_first
        grad_second = jnp.dot(grad_second_part, select.T, precision=precise)
        grad_skip = jnp.dot(layer_grads[3], select.T, precision=precise)
        gain_grad, in_grad, kernel_grad, _, out_grad, up_grad, down_grad = layer_grads
        if level_idx == 0:
            embed_part = jnp.einsum("mtv,mtd->vd", onehot, grad_stream, precision=precise)
            summed = lax.psum(
                (
                    gain_grad,
                    in_grad,
                    kernel_grad,
                    grad_second,
                    grad_skip,
                    out_grad,
                    up_grad,
                    down_grad,
                    embed_part,
                ),
                "seq",
            )
            collected[level_idx] = summed[:8]
            grad_embed = summed[8]
        else:
            collected[level_idx] = lax.psum(
                (
                    gain_grad,
                    in_grad,
                    kernel_grad,
                    grad_second,
                    grad_skip,
                    out_grad,
                    up_grad,
                    down_grad,
                ),
                "seq",
            )
    stacked = [
        jnp.stack([collected[level_idx][member] for level_idx in range(layer_count)])
        for member in range(8)
    ]
    filter_grads = lax.psum(jnp.stack(first_grads), ("seq", "ch"))
    return (
        block_out,
        grad_embed,
        stacked[0],
        stacked[1],
        stacked[2],
        filter_grads,
        stacked[3],
        stacked[4],
        stacked[5],
        stacked[6],
        stacked[7],
    )


def solution(mesh):
    in_specs = (
        P(None, "seq"),
        P(),
        P(),
        P(),
        P(None, None, None, "ch"),
        P(None, None, None, "ch"),
        P(),
        P(None, None, "ch"),
        P(None, "ch"),
        P(None, "ch", None),
        P(None, None, "ch"),
        P(None, "ch", None),
        P(None, "seq", None),
    )
    out_specs = (
        P(None, "seq", None),
        P(),
        P(),
        P(None, None, None, "ch"),
        P(None, None, None, "ch"),
        P(),
        P(None, None, "ch"),
        P(None, "ch"),
        P(None, "ch", None),
        P(None, None, "ch"),
        P(None, "ch", None),
    )
    return jax.shard_map(local, mesh=mesh, in_specs=in_specs, out_specs=out_specs, check_vma=False)
```

profile of v0, /device:TPU:0, one launch (start us, length us, event | category | flops | bytes accessed | tf_op | source)
XLA Modules:
  0.0 690.6 jit_solution(3131744000247618550)
XLA Ops:
  30.7 7.5 %all-to-all-start = ((f32[1,256,128]{2,0,1:T(1,128)}), f32[1,256,128]{2,0,1:T(1,128)S(1)}, u32[]{:S(2)}, u32[]{:S(2)}) async-start(f32[1,256,128]{2,0,1:T(1,128)} %bitcast.10), calls=%async_computation | async-start | bytes 262144 | tf_op jit(solution)/shard_map/all_to_all | solution.py:187
  38.8 7.3 %all-to-all-done = f32[1,256,128]{2,0,1:T(1,128)S(1)} async-done(((f32[1,256,128]{2,0,1:T(1,128)}), f32[1,256,128]{2,0,1:T(1,128)S(1)}, u32[]{:S(2)}, u32[]{:S(2)}) %all-to-all-start) | async-done | bytes 131104 | tf_op jit(solution)/shard_map/all_to_all | solution.py:187
  54.9 10.2 %reduce.2 = f32[2048,16]{1,0:T(8,128)} reduce(f32[2048,1,16]{2,1,0:T(1,128)S(1)} %bitcast.733, f32[]{:T(128)} %broadcast.909), dimensions={1}, to_apply=%bitcast.639.reduce_sub_computation | reduce | bytes 262148
  70.9 12.4 %all-reduce.13.cloned.1.call-start = ((), (), s32[]{:S(2)}) async-start(), calls=%async_computation.8 | async-start | bytes 524288 | tf_op jit(solution)/shard_map/psum | solution.py:165
  91.7 22.7 %all-reduce.13.cloned.1.call-done = f32[2,128,256]{2,1,0:T(8,128)} async-done(((f32[2,128,256]{2,1,0:T(8,128)}), f32[2,128,256]{2,1,0:T(8,128)}) %all-reduce.13.cloned.1.call-update) | async-done | bytes 262160 | tf_op jit(solution)/shard_map/psum | solution.py:165
  120.3 22.0 %all-reduce.15.cloned.1.call-done = f32[2,128,256]{2,1,0:T(8,128)} async-done(((f32[2,128,256]{2,1,0:T(8,128)}), f32[2,128,256]{2,1,0:T(8,128)}) %all-reduce.15.cloned.1.call-update) | async-done | bytes 262160 | tf_op jit(solution)/shard_map/psum | solution.py:165
  150.1 7.9 %all-to-all-start.2 = ((f32[1,256,128]{2,0,1:T(1,128)}), f32[1,256,128]{2,0,1:T(1,128)S(1)}, u32[]{:S(2)}, u32[]{:S(2)}) async-start(f32[1,256,128]{2,0,1:T(1,128)} %bitcast.57), calls=%async_computation.2 | async-start | bytes 262144 | tf_op jit(solution)/shard_map/all_to_all | solution.py:187
  158.7 7.2 %all-to-all-done.2 = f32[1,256,128]{2,0,1:T(1,128)S(1)} async-done(((f32[1,256,128]{2,0,1:T(1,128)}), f32[1,256,128]{2,0,1:T(1,128)S(1)}, u32[]{:S(2)}, u32[]{:S(2)}) %all-to-all-start.2) | async-done | bytes 131104 | tf_op jit(solution)/shard_map/all_to_all | solution.py:187
  174.7 10.2 %reduce.4 = f32[2048,16]{1,0:T(8,128)} reduce(f32[2048,1,16]{2,1,0:T(1,128)S(1)} %bitcast.734, f32[]{:T(128)} %broadcast.909), dimensions={1}, to_apply=%bitcast.641.reduce_sub_computation | reduce | bytes 262148
  186.6 10.9 %all_to_all.152 = f32[16,1,2048]{2,1,0:T(1,128)S(1)} all-to-all(f32[16,1,2048]{2,1,0:T(1,128)S(1)} %reshape.941), channel_id=1, replica_groups=mesh['seq'=16,'ch'=2] {'seq'}, dimensions={0} | all-to-all | bytes 262144 | tf_op jit(solution)/shard_map/all_to_all | solution.py:189
  204.2 19.5 %all-reduce.17.cloned.1.call-done = f32[2,128,256]{2,1,0:T(8,128)} async-done(((f32[2,128,256]{2,1,0:T(8,128)}), f32[2,128,256]{2,1,0:T(8,128)}) %all-reduce.17.cloned.1.call-update) | async-done | bytes 262160 | tf_op jit(solution)/shard_map/psum | solution.py:165
  231.0 21.0 %all-reduce.19.cloned.1.call-done = f32[2,128,256]{2,1,0:T(8,128)} async-done(((f32[2,128,256]{2,1,0:T(8,128)}), f32[2,128,256]{2,1,0:T(8,128)}) %all-reduce.19.cloned.1.call-update) | async-done | bytes 262160 | tf_op jit(solution)/shard_map/psum | solution.py:169
  257.7 5.6 all-to-all-start.4
  291.3 10.4 %reduce.6 = f32[2048,16]{1,0:T(8,128)} reduce(f32[2048,1,16]{2,1,0:T(1,128)S(1)} %bitcast.735, f32[]{:T(128)} %broadcast.909), dimensions={1}, to_apply=%bitcast.643.reduce_sub_computation | reduce | bytes 262148
  327.8 20.1 %all-reduce.21.cloned.1.call-done = f32[2,128,256]{2,1,0:T(8,128)} async-done(((f32[2,128,256]{2,1,0:T(8,128)}), f32[2,128,256]{2,1,0:T(8,128)}) %all-reduce.21.cloned.1.call-update) | async-done | bytes 262160 | tf_op jit(solution)/shard_map/psum | solution.py:169
  356.1 20.4 %all-reduce.23.cloned.1.call-done = f32[2,128,256]{2,1,0:T(8,128)} async-done(((f32[2,128,256]{2,1,0:T(8,128)}), f32[2,128,256]{2,1,0:T(8,128)}) %all-reduce.23.cloned.1.call-update) | async-done | bytes 262160 | tf_op jit(solution)/shard_map/psum | solution.py:169
  382.0 5.8 all-to-all-start.6
  389.9 5.8 all-to-all-done.6
  409.2 9.5 %reduce.8 = f32[2048,16]{1,0:T(8,128)S(1)} reduce(f32[2048,1,16]{2,1,0:T(1,128)S(1)} %bitcast.736, f32[]{:T(128)} %broadcast.909), dimensions={1}, to_apply=%bitcast.645.reduce_sub_computation | reduce | bytes 262148
  424.2 7.1 %all-to-all-done.7 = f32[16,1,2048]{2,1,0:T(1,128)S(1)} async-done(((f32[16,1,2048]{2,1,0:T(1,128)}), f32[16,1,2048]{2,1,0:T(1,128)S(1)}, u32[]{:S(2)}, u32[]{:S(2)}) %all-to-all-start.7) | async-done | bytes 131104 | tf_op jit(solution)/shard_map/all_to_all | solution.py:260
  444.7 24.5 %all-reduce.29.cloned.1.call-done = (f32[2,128,256]{2,1,0:T(8,128)}, f32[2,128,256]{2,1,0:T(8,128)}) async-done(((f32[2,128,256]{2,1,0:T(8,128)}, f32[2,128,256]{2,1,0:T(8,128)}), (f32[2,128,256]{2,1,0:T(8,128)}, f32[2,128,256]{2,1,0:T(8,128)})) %all-reduce.29.cloned.1.call-update) | async-done | bytes 524304 | tf_op jit(solution)/shard_map/psum | solution.py:165
  483.1 39.7 %psum.203 = f32[2,33,64]{2,1,0:T(8,128)S(1)} all-reduce(f32[2,33,64]{2,1,0:T(8,128)S(1)} %pad_maximum_fusion.16), channel_id=1, replica_groups=mesh['seq'=16,'ch'=2] {'seq','ch'}, use_global_device_ids=true, to_apply=%region_41.42 | all-reduce | flops 4224 | bytes 33792 | tf_op jit(solution)/shard_map/psum | solution.py:427
  524.3 39.0 %all-reduce.25.cloned.1.call-done = (f32[16,256]{1,0:T(8,128)}, f32[1,2,256]{2,1,0:T(2,128)}, f32[1,2,256]{2,1,0:T(2,128)}, f32[1,3,3,128]{3,2,1,0:T(4,128)}, f3...) async-done(((f32[16,256]{1,0:T(8,128)}, f32[1,2,256]{2,1,0:T(2,128)}, ...) | async-done | bytes 96272 | tf_op jit(solution)/shard_map/psum | solution.py:393
  566.5 110.5 %all-reduce.27.cloned.1.call-done = (f32[1,256,3,128]{3,1,2,0:T(8,128)}, f32[1,256,3,128]{3,1,2,0:T(8,128)}, f32[1,128,256]{2,1,0:T(8,128)}, f32[1,128,256]{2,1,...) async-done(((f32[1,256,3,128]{3,1,2,0:T(8,128)}, f32[1,256,3,128]{3,1,2,0:T(8,128)}, ...) | async-done | bytes 3145744 | tf_op jit(solution)/shard_map/psum | solution.py:410
  (602 shorter events, 216.7 us)
Async XLA Ops:
  12.1 16.5 %collective-permute-start = (f32[2,2,3,128]{3,1,2,0:T(2,128)S(1)}, f32[2,2,3,128]{3,1,2,0:T(2,128)S(1)}, u32[]{:S(2)}, u32[]{:S(2)}) collective-permute-start(f32[2,2,3,128]{3,1,2,0:T(2,128)S(1)} %slice.234), channel_id=1, source_target_pairs={{0,2},{2,4},{4,6},{6,8},{8,10},{10,12},{12,14},{14,16},{16,18},{18... | collective-permute-start | bytes 18440 | tf_op jit(solution)/shard_map/ppermute | solution.py:19
  30.7 15.4 %all-to-all-start = ((f32[1,256,128]{2,0,1:T(1,128)}), f32[1,256,128]{2,0,1:T(1,128)S(1)}, u32[]{:S(2)}, u32[]{:S(2)}) async-start(f32[1,256,128]{2,0,1:T(1,128)} %bitcast.10), calls=%async_computation | async-start | bytes 262144 | tf_op jit(solution)/shard_map/all_to_all | solution.py:187
  67.4 16.8 %all-to-all-start.1 = ((f32[16,1,2048]{2,1,0:T(1,128)}), f32[16,1,2048]{2,1,0:T(1,128)S(1)}, u32[]{:S(2)}, u32[]{:S(2)}) async-start(f32[16,1,2048]{2,1,0:T(1,128)} %reshape.939), calls=%async_computation.1 | async-start | bytes 262144 | tf_op jit(solution)/shard_map/all_to_all | solution.py:189
  70.9 43.4 %all-reduce.13.cloned.1.call-start = ((), (), s32[]{:S(2)}) async-start(), calls=%async_computation.8 | async-start | bytes 524288 | tf_op jit(solution)/shard_map/psum | solution.py:165
  89.7 52.6 %all-reduce.15.cloned.1.call-start = ((), (), s32[]{:S(2)}) async-start(), calls=%async_computation.9 | async-start | bytes 524288 | tf_op jit(solution)/shard_map/psum | solution.py:165
  119.6 28.2 %copy-start.117 = (f32[3,128]{1,0:T(4,128)}, f32[3,128]{1,0:T(4,128)S(1)}, u32[]{:S(2)}) copy-start(f32[3,128]{1,0:T(4,128)S(1)} %get-tuple-element.168) | copy-start | bytes 4612
  119.6 28.2 %copy-start.119 = (f32[3,128]{1,0:T(4,128)}, f32[3,128]{1,0:T(4,128)S(1)}, u32[]{:S(2)}) copy-start(f32[3,128]{1,0:T(4,128)S(1)} %get-tuple-element.169) | copy-start | bytes 4612
  120.2 48.6 %copy-start.27 = (f32[16,32,128]{2,1,0:T(8,128)}, f32[16,32,128]{2,1,0:T(8,128)S(1)}, u32[]{:S(2)}) copy-start(f32[16,32,128]{2,1,0:T(8,128)S(1)} %convolution_subtract_fusion.7) | copy-start | bytes 786436
  145.0 2.8 collective-permute-start.1
  150.1 15.8 %all-to-all-start.2 = ((f32[1,256,128]{2,0,1:T(1,128)}), f32[1,256,128]{2,0,1:T(1,128)S(1)}, u32[]{:S(2)}, u32[]{:S(2)}) async-start(f32[1,256,128]{2,0,1:T(1,128)} %bitcast.57), calls=%async_computation.2 | async-start | bytes 262144 | tf_op jit(solution)/shard_map/all_to_all | solution.py:187
  158.0 65.6 %all-reduce.17.cloned.1.call-start = ((), (), s32[]{:S(2)}) async-start(), calls=%async_computation.10 | async-start | bytes 524288 | tf_op jit(solution)/shard_map/psum | solution.py:165
  203.6 48.3 %all-reduce.19.cloned.1.call-start = ((), (), s32[]{:S(2)}) async-start(), calls=%async_computation.11 | async-start | bytes 524288 | tf_op jit(solution)/shard_map/psum | solution.py:169
  257.7 13.6 %all-to-all-start.4 = ((f32[1,256,128]{2,0,1:T(1,128)}), f32[1,256,128]{2,0,1:T(1,128)S(1)}, u32[]{:S(2)}, u32[]{:S(2)}) async-start(f32[1,256,128]{2,0,1:T(1,128)} %bitcast.95), calls=%async_computation.4 | async-start | bytes 262144 | tf_op jit(solution)/shard_map/all_to_all | solution.py:256
  304.0 11.6 %all-to-all-start.5 = ((f32[16,1,2048]{2,1,0:T(1,128)}), f32[16,1,2048]{2,1,0:T(1,128)S(1)}, u32[]{:S(2)}, u32[]{:S(2)}) async-start(f32[16,1,2048]{2,1,0:T(1,128)} %reshape.943), calls=%async_computation.5 | async-start | bytes 262144 | tf_op jit(solution)/shard_map/all_to_all | solution.py:260
  307.6 40.2 %all-reduce.21.cloned.1.call-start = ((), (), s32[]{:S(2)}) async-start(), calls=%async_computation.12 | async-start | bytes 524288 | tf_op jit(solution)/shard_map/psum | solution.py:169
  320.8 3.1 collective-permute-start.2
  326.0 50.5 %all-reduce.23.cloned.1.call-start = ((), (), s32[]{:S(2)}) async-start(), calls=%async_computation.13 | async-start | bytes 524288 | tf_op jit(solution)/shard_map/psum | solution.py:169
  382.0 13.8 %all-to-all-start.6 = ((f32[1,256,128]{2,0,1:T(1,128)}), f32[1,256,128]{2,0,1:T(1,128)S(1)}, u32[]{:S(2)}, u32[]{:S(2)}) async-start(f32[1,256,128]{2,0,1:T(1,128)} %bitcast.124), calls=%async_computation.6 | async-start | bytes 262144 | tf_op jit(solution)/shard_map/all_to_all | solution.py:256
  419.8 11.5 %all-to-all-start.7 = ((f32[16,1,2048]{2,1,0:T(1,128)}), f32[16,1,2048]{2,1,0:T(1,128)S(1)}, u32[]{:S(2)}, u32[]{:S(2)}) async-start(f32[16,1,2048]{2,1,0:T(1,128)} %reshape.945), calls=%async_computation.7 | async-start | bytes 262144 | tf_op jit(solution)/shard_map/all_to_all | solution.py:260
  423.5 45.8 %all-reduce.29.cloned.1.call-start = ((), (), s32[]{:S(2)}) async-start(), calls=%async_computation.16 | async-start | bytes 1048576 | tf_op jit(solution)/shard_map/psum | solution.py:165
  436.6 3.1 collective-permute-start.3
  441.8 121.6 %all-reduce.25.cloned.1.call-start = ((), (), s32[]{:S(2)}) async-start(), calls=%async_computation.14 | async-start | bytes 198656 | tf_op jit(solution)/shard_map/psum | solution.py:393
  474.4 202.6 %all-reduce.27.cloned.1.call-start = ((), (), s32[]{:S(2)}) async-start(), calls=%async_computation.15 | async-start | bytes 6291456 | tf_op jit(solution)/shard_map/psum | solution.py:410
  482.5 41.0 %copy-start.76 = (f32[2,128,256]{2,1,0:T(8,128)S(1)}, f32[2,128,256]{2,1,0:T(8,128)}, u32[]{:S(2)}) copy-start(f32[2,128,256]{2,1,0:T(8,128)} %get-tuple-element.108) | copy-start | bytes 786436
  (154 other events, 416.0 us)
Sparse Core Ops, SparseCore 0:
  89.8 24.4 all-reduce.12
  119.0 23.1 all-reduce.14
  203.7 19.8 all-reduce.16
  228.7 23.1 all-reduce.18
  326.1 21.7 all-reduce.20
  353.3 23.1 all-reduce.22
  441.9 27.3 all-reduce.28
  475.8 87.4 all-reduce.24
  569.0 107.9 all-reduce.26
where the time goes:
time: 699 us; the launch traced here: 691 us
  waiting for transfers between devices  340 us (49%)
  matrix products  88.6 us (13%)
  other arithmetic  71.9 us (10%)
  local copies, waits for them, and re-layouts  66.3 us (9%)
  starting transfers between devices  57 us (8%)
  blocking collectives  50.7 us (7%)
  between operations  16.7 us (2%)
    psum x2, waiting for transfers between devices, local(): lax.psum((gain_grad, in_grad, kernel_grad, grad_second, grad_skip, out_gr...  149 us
    psum x4, waiting for transfers between devices, channel_total(): return lax.psum(partial_sum, 'ch')  88.7 us
    psum x3, waiting for transfers between devices, input_total(): return lax.psum(partial_sum, 'ch')  61.4 us
    unnamed x334, local copies, waits for them, and re-layouts  50.7 us
    unnamed x4, other arithmetic  40.4 us
    psum x1, blocking collectives, local(): filter_grads = lax.psum(jnp.stack(first_grads), ('seq', 'ch'))  39.7 us
    dot_general x48, matrix products, along_block(): return jnp.einsum('...kb,bj->...kj', values, table, precision=precise)  35.5 us
    all_to_all x2, starting transfers between devices, layer_forward(): lax.all_to_all(flat_rows, 'seq', split_axis=1, concat_axis=2, tiled=True)  15.4 us
  transfers between devices with their start and end apart: 20, of which 17 were waited for; matrix products, arithmetic and copies ran while one was open for 7% of the time, Pallas kernels for 0%

commit v1 on v0

--- a/solution.py
+++ b/solution.py
@@ -1,8 +1,12 @@
+import functools
 import math
 
 import jax
 import jax.numpy as jnp
+import numpy as np
 from jax import lax
+from jax.experimental import pallas as pl
+from jax.experimental.pallas import tpu as pltpu
 from jax.sharding import PartitionSpec as P
 
 D = 256
@@ -440,6 +444,1097 @@
     )
 
 
+HALO = 16
+ROOT_HALF = math.sqrt(0.5)
+GELU_A = math.sqrt(2.0 / math.pi)
+GELU_B = 0.044715
+BLOCKS = 8
+BLOCK = 256
+KINDS = 9
+VMEM_LIMIT = 20 * 2**20
+f32 = jnp.float32
+bf16 = jnp.bfloat16
+
+
+def run(body, outs, scalars, *arrays, scratch=()):
+    vmem = pl.BlockSpec(memory_space=pltpu.VMEM)
+    smem = pl.BlockSpec(memory_space=pltpu.SMEM)
+    single = not isinstance(outs, (list, tuple))
+    shapes = [outs] if single else list(outs)
+    result = pl.pallas_call(
+        body,
+        out_shape=shapes,
+        in_specs=[smem] + [vmem] * len(arrays),
+        out_specs=[vmem] * len(shapes),
+        scratch_shapes=list(scratch),
+        compiler_params=pltpu.CompilerParams(vmem_limit_bytes=VMEM_LIMIT),
+    )(scalars, *arrays)
+    return result[0] if single else result
+
+
+def arr(*shape, kind=f32):
+    return jax.ShapeDtypeStruct(shape, kind)
+
+
+def mm(a, b):
+    return jnp.dot(a, b, preferred_element_type=f32)
+
+
+def mm_nt(a, b):
+    return lax.dot_general(a, b, (((1,), (1,)), ((), ())), preferred_element_type=f32)
+
+
+def mm_tn(a, b):
+    return lax.dot_general(a, b, (((0,), (0,)), ((), ())), preferred_element_type=f32)
+
+
+def split(a):
+    high = a.astype(bf16)
+    return high, (a - high.astype(f32)).astype(bf16)
+
+
+def mm3(a, b):
+    a_high, a_low = split(a)
+    b_high, b_low = split(b)
+    return mm(a_high, b_high) + (mm(a_low, b_high) + mm(a_high, b_low))
+
+
+def unit(rows):
+    center = rows - jnp.mean(rows, axis=-1, keepdims=True)
+    scale = lax.rsqrt(jnp.mean(center * center, axis=-1, keepdims=True) + epsilon)
+    return center * scale, scale
+
+
+def unit_back(grad, normal, scale):
+    inner = jnp.mean(grad * normal, axis=-1, keepdims=True)
+    return scale * (grad - jnp.mean(grad, axis=-1, keepdims=True) - normal * inner)
+
+
+def at(start, size, unit_rows=16):
+    return pl.ds(pl.multiple_of(start, unit_rows), size)
+
+
+def dft_table():
+    turns = np.outer(np.arange(BLOCK), np.arange(BLOCK)) % BLOCK
+    angle = 2.0 * np.pi * turns / BLOCK
+    return np.concatenate([np.cos(angle), np.sin(angle)], axis=1).astype(np.float32)
+
+
+def twiddle_table():
+    angle = 2.0 * np.pi * np.outer(np.arange(1, KINDS), np.arange(BLOCK)) / (2 * BLOCKS * BLOCK)
+    pair = np.stack([np.cos(angle), np.sin(angle)], axis=1).astype(np.float32)
+    return np.broadcast_to(pair[..., None], (KINDS - 1, 2, BLOCK, 128)).copy()
+
+
+def feature_table(length):
+    places = np.arange(length)
+    turns = np.outer(places, np.arange(1, (FEAT - 1) // 2 + 1)) % length
+    angle = 2.0 * np.pi * turns / length
+    ramp = places[:, None] / length
+    return np.concatenate([ramp, np.cos(angle), np.sin(angle)], axis=1).astype(np.float32)
+
+
+def rate_table():
+    return (0.3 * 10.0 ** (np.arange(D) / (D - 1))).astype(np.float32).reshape(2, 1, D // 2)
+
+
+def four_real(a, b, c, d):
+    s, m, t, n = a + c, a - c, b + d, b - d
+    hn, ht = ROOT_HALF * n, ROOT_HALF * t
+    return (s + t, s - t, (a + hn, -(ht + c)), (m, -n), (a - hn, c - ht))
+
+
+def turn(k):
+    angle = 2.0 * math.pi * k / (2 * BLOCKS)
+    return math.cos(angle), math.sin(angle)
+
+
+def put_pair(stage, kind, row, re, im):
+    rows = re.shape[0]
+    re, im = re.astype(bf16), im.astype(bf16)
+    stage[kind, pl.ds(row, rows), 0:128] = re
+    stage[kind, pl.ds(row, rows), 128:256] = im
+    stage[kind, pl.ds(row + BLOCK, rows), 0:128] = im
+    stage[kind, pl.ds(row + BLOCK, rows), 128:256] = -re
+
+
+def put_pair_back(stage, kind, row, re, im):
+    rows = re.shape[0]
+    re, im = re.astype(bf16), im.astype(bf16)
+    stage[kind, pl.ds(row, rows), 0:128] = re
+    stage[kind, pl.ds(row, rows), 128:256] = im
+    stage[kind, pl.ds(row + BLOCK, rows), 0:128] = -im
+    stage[kind, pl.ds(row + BLOCK, rows), 128:256] = re
+
+
+def all_kinds(dft, stage, out):
+    def one(kind, carry):
+        out[kind] = mm(dft[...], stage[kind])
+        return carry
+
+    lax.fori_loop(0, KINDS, one, 0)
+
+
+def to_freq(load, dft, twiddle, stage, out):
+    def chunk(step, carry):
+        row = pl.multiple_of(step * 16, 16)
+        u = [load(p, row) for p in range(BLOCKS)]
+        e0, e4, e1, e2, e3 = four_real(u[0], u[2], u[4], u[6])
+        o0, o4, o1, o2, o3 = four_real(u[1], u[3], u[5], u[7])
+
+        def put(kind, re, im):
+            c, s = twiddle[kind - 1, 0, pl.ds(row, 16), :], twiddle[kind - 1, 1, pl.ds(row, 16), :]
+            put_pair(stage, kind, row, re * c + im * s, im * c - re * s)
+
+        put_pair(stage, 0, row, e0 + o0, jnp.zeros_like(e0))
+        last = e0 - o0
+        c, s = twiddle[7, 0, pl.ds(row, 16), :], twiddle[7, 1, pl.ds(row, 16), :]
+        put_pair(stage, 8, row, last * c, -(last * s))
+        put(4, e4, -o4)
+        for k, (er, ei), (orr, oi) in ((1, e1, o1), (2, e2, o2), (3, e3, o3)):
+            c, s = turn(k)
+            wr, wi = orr * c + oi * s, oi * c - orr * s
+            put(k, er + wr, ei + wi)
+            put(8 - k, er - wr, wi - ei)
+        return carry
+
+    lax.fori_loop(0, BLOCK // 16, chunk, 0)
+    all_kinds(dft, stage, out)
+
+
+def from_freq(dft, twiddle, stage, back, store):
+    all_kinds(dft, stage, back)
+
+    def chunk(step, carry):
+        row = pl.multiple_of(step * 16, 16)
+
+        def get(kind):
+            re = back[kind, pl.ds(row, 16), 0:128]
+            im = back[kind, pl.ds(row, 16), 128:256]
+            c, s = twiddle[kind - 1, 0, pl.ds(row, 16), :], twiddle[kind - 1, 1, pl.ds(row, 16), :]
+            return re * c - im * s, re * s + im * c
+
+        first = 0.5 * back[0, pl.ds(row, 16), 0:128]
+        last = 0.5 * get(8)[0]
+        mid_re, mid_im = get(4)
+        even, odd = {}, {}
+        for k in (1, 2, 3):
+            ar, ai = get(k)
+            br, bi = get(8 - k)
+            even[k] = (ar + br, ai - bi)
+            c, s = turn(k)
+            dr, di = ar - br, ai + bi
+            odd[k] = (dr * c - di * s, dr * s + di * c)
+        for shift, base, extra, part in (
+            (0, first + last, mid_re, even),
+            (1, first - last, -mid_im, odd),
+        ):
+            (r1, i1), (r2, i2), (r3, i3) = part[1], part[2], part[3]
+            plus, minus = base + extra, base - extra
+            diff, both = ROOT_HALF * (r1 - r3), ROOT_HALF * (i1 + i3)
+            store(shift, row, plus + (r1 + r2 + r3))
+            store(shift + 2, row, minus - i2 + (diff - both))
+            store(shift + 4, row, plus - r2 - (i1 - i3))
+            store(shift + 6, row, minus + i2 - (diff + both))
+        return carry
+
+    lax.fori_loop(0, BLOCK // 16, chunk, 0)
+
+
+def times(first, second, stage, conj):
+    def chunk(step, carry):
+        row = pl.multiple_of(step * 16, 16)
+        for kind in range(KINDS):
+            fr = first[kind, pl.ds(row, 16), 0:128]
+            fi = first[kind, pl.ds(row, 16), 128:256]
+            ur = second[kind, pl.ds(row, 16), 0:128]
+            ui = second[kind, pl.ds(row, 16), 128:256]
+            if conj:
+                put_pair_back(stage, kind, row, fr * ur + fi * ui, fr * ui - fi * ur)
+            else:
+                put_pair_back(stage, kind, row, fr * ur - fi * ui, fr * ui + fi * ur)
+        return carry
+
+    lax.fori_loop(0, BLOCK // 16, chunk, 0)
+
+
+SPECTRUM = (KINDS, BLOCK, 256)
+
+
+def stage_scratch():
+    return pltpu.VMEM((KINDS, 2 * BLOCK, 256), bf16)
+
+
+def spec_scratch():
+    return pltpu.VMEM(SPECTRUM, f32)
+
+
+PACK_SECOND = 48
+PACK_SHORT = 176
+PACK_SKIP = 194
+PACK_ROWS = 200
+
+
+def pack_kernel(s, embed, gain, in_own, second, short, skip, out):
+    normal, _ = unit(embed[...])
+    low = (normal * gain[0, 0:1, :]).astype(bf16)
+    for g in range(3):
+        out[16 * g : 16 * g + 16, :] = mm(low, in_own[0, g])
+    for l in range(2):
+        out[PACK_SECOND + 64 * l : PACK_SECOND + 64 * l + 64, :] = second[l]
+        for k in range(3):
+            row = PACK_SHORT + 9 * l + 3 * k
+            out[row : row + 3, :] = short[l, k]
+    out[PACK_SKIP : PACK_SKIP + 2, :] = skip[...]
+    out[PACK_SKIP + 2 : PACK_ROWS, :] = jnp.zeros((PACK_ROWS - PACK_SKIP - 2, 128), f32)
+
+
+def table_kernel(s, own, peer, embed, mine_out, other_out, conv_table, gate_table):
+    first = s[0] == 0
+    mine = jnp.where(first, own[...], peer[...])
+    other = jnp.where(first, peer[...], own[...])
+    mine_out[...] = mine
+    other_out[...] = other
+
+    def fill(table, lanes, parts):
+        whole = jnp.concatenate(parts, axis=0)
+        high, low = split(whole)
+        table[0:48, lanes] = high
+        table[48:96, lanes] = low
+        table[96:128, lanes] = jnp.zeros((32, 128), bf16)
+
+    def gate(pack, g):
+        parts = []
+        for k in range(3):
+            row = PACK_SHORT + 3 * k + g
+            parts.append(pack[16 * g : 16 * g + 16] * pack[row : row + 1])
+        return parts
+
+    fill(conv_table, slice(0, 128), gate(mine, 1))
+    fill(conv_table, slice(128, 256), gate(mine, 2))
+    fill(gate_table, slice(0, 128), gate(mine, 0))
+    fill(gate_table, slice(128, 256), gate(other, 0))
+    zero = jnp.zeros((16, 128), f32)
+    fill(gate_table, slice(256, 384), [embed[:, 0:128], zero, zero])
+    fill(gate_table, slice(384, 512), [embed[:, 128:256], zero, zero])
+
+
+def onehot_kernel(s, ids, out, turned, work):
+    live = s[2]
+    count, width = ids.shape
+    work[0:HALO, :] = jnp.zeros((HALO, 128), f32)
+    work[HALO + count * width : 2 * HALO + count * width, :] = jnp.zeros((HALO, 128), f32)
+    vocab = lax.broadcasted_iota(jnp.int32, (128, width), 0) % 16
+    place = lax.broadcasted_iota(jnp.int32, (128, width), 1)
+    for i in range(count):
+        token = jnp.broadcast_to(ids[i : i + 1, :], (128, width))
+        hit = (token == vocab) & (place + i * width < live)
+        work[HALO + width * i : HALO + width * (i + 1), :] = jnp.where(hit, 1.0, 0.0).T
+    lane = lax.broadcasted_iota(jnp.int32, (width, 128), 1) % 48 // 16
+    used = lax.broadcasted_iota(jnp.int32, (width, 128), 1) < 96
+    half = count // 2
+    for i in range(count):
+        row = HALO + width * i
+        now = work[row : row + width, :]
+        one = work[row - 1 : row - 1 + width, :]
+        two = work[row - 2 : row - 2 + width, :]
+        picked = jnp.where(lane == 0, now, jnp.where(lane == 1, one, two))
+        picked = jnp.where(used, picked, 0.0)
+        out[row : row + width, :] = picked.astype(bf16)
+        turned[i // half, :, width * (i % half) : width * (i % half + 1)] = picked.T.astype(bf16)
+    out[0:HALO, :] = jnp.zeros((HALO, 128), bf16)
+    out[HALO + count * width : 2 * HALO + count * width, :] = jnp.zeros((HALO, 128), bf16)
+
+
+def sine_kernel(s, feats, firsts, sine, cosine, turned):
+    both = jnp.concatenate([firsts[0], firsts[1]], axis=1)
+    count = feats.shape[0] // 256
+
+    def chunk(i, carry):
+        rows = at(256 * i, 256)
+        angle = jnp.dot(feats[rows, :], both, precision=precise, preferred_element_type=f32)
+        act = jnp.sin(angle)
+        sine[rows, :] = act
+        cosine[rows, :] = jnp.cos(angle)
+        turned[:, at(256 * i, 256, 256)] = act.T.astype(bf16)
+        return carry
+
+    lax.fori_loop(0, count, chunk, 0)
+
+
+def decay_of(rates, start, rows, length):
+    place = (lax.broadcasted_iota(jnp.int32, (rows, 1), 0) + start).astype(f32) / length
+    return jnp.exp(-place * rates), place
+
+
+def filter_kernel(s, sine, mine, rates, dft, twiddle, filt0, filt1, freq0, freq1, stage, work):
+    length = sine.shape[0]
+    rate = rates[s[3]]
+    zero = jnp.zeros((64, 128), f32)
+    left = jnp.concatenate([mine[PACK_SECOND : PACK_SECOND + 64], zero], axis=0)
+    right = jnp.concatenate([zero, mine[PACK_SECOND + 64 : PACK_SECOND + 128]], axis=0)
+    weights = jnp.concatenate([left, right], axis=1)
+
+    def chunk(i, carry):
+        rows = at(256 * i, 256)
+        decay, _ = decay_of(rate, 256 * i, 256, length)
+        both = mm3(sine[rows, :], weights)
+        filt0[rows, :] = both[:, 0:128] * decay
+        filt1[rows, :] = both[:, 128:256] * decay
+        return carry
+
+    lax.fori_loop(0, length // 256, chunk, 0)
+    for filt, freq in ((filt0, freq0), (filt1, freq1)):
+        to_freq(lambda p, row: filt[pl.ds(BLOCK * p + row, 16), :] * (1.0 / length), dft, twiddle, stage, freq)
+
+
+def causal(load, skip_row, freq_filt, dft, twiddle, spec, stage, work, line):
+    to_freq(load, dft, twiddle, stage, spec)
+    times(freq_filt, spec, stage, False)
+
+    def store(p, row, value):
+        line[pl.ds(HALO + BLOCK * p + row, 16), :] = value + skip_row * load(p, row)
+
+    from_freq(dft, twiddle, stage, work, store)
+
+
+def hand_out(s, line, keep, send):
+    half = (line.shape[0] - 2 * HALO) // 2
+    span = half + 2 * HALO
+    k = s[0]
+    line[0:HALO, :] = jnp.zeros((HALO, 128), f32)
+    line[HALO + 2 * half :, :] = jnp.zeros((HALO, 128), f32)
+    keep[...] = line[at(half * k, span), :]
+    send[...] = line[at(half * (1 - k), span), :]
+
+
+def conv_first_kernel(s, onehot, conv_table, mine, freq_filt, dft, twiddle, keep, send, spec, product, stage, work, line):
+    def chunk(i, carry):
+        rows = at(256 * i, 256)
+        pair = mm(onehot[at(256 * i + HALO, 256), :], conv_table[...])
+        product[rows, :] = pair[:, 0:128] * pair[:, 128:256]
+        return carry
+
+    lax.fori_loop(0, product.shape[0] // 256, chunk, 0)
+    skip_row = mine[PACK_SKIP : PACK_SKIP + 1, :]
+    causal(lambda p, row: product[pl.ds(BLOCK * p + row, 16), :], skip_row, freq_filt, dft, twiddle, spec, stage, work, line)
+    hand_out(s, line, keep, send)
+
+
+def join_rows(s, whole, kept, received):
+    half = kept.shape[0]
+    whole[at(half * s[0], half), :] = kept[...]
+    whole[at(half * (1 - s[0]), half), :] = received[...]
+
+
+def conv_second_kernel(s, kept, received, mine, freq_filt, dft, twiddle, keep, send, spec, product, stage, work, line):
+    join_rows(s, product, kept, received)
+    skip_row = mine[PACK_SKIP + 1 : PACK_SKIP + 2, :]
+    causal(lambda p, row: product[pl.ds(BLOCK * p + row, 16), :], skip_row, freq_filt, dft, twiddle, spec, stage, work, line)
+    hand_out(s, line, keep, send)
+
+
+def gelu_parts(p):
+    squared = p * p
+    th = jnp.tanh(GELU_A * p * (1.0 + GELU_B * squared))
+    half = 0.5 * (1.0 + th)
+    slope = half + 0.5 * p * (1.0 - th * th) * (GELU_A + (3.0 * GELU_A * GELU_B) * squared)
+    return p * half, slope
+
+
+def gelu_only(p):
+    return 0.5 * p * (1.0 + jnp.tanh(GELU_A * p * (1.0 + GELU_B * (p * p))))
+
+
+CHUNK = 352
+
+
+def forward_first_kernel(
+    s, onehot, gate_table, conv_mine, conv_other, gain, w_out, w_up, w_down, w_in, mine, other,
+    keep, send, mid_out, stream_out, gates, mixed,
+):
+    span = mid_out.shape[0]
+    half = span - 2 * HALO
+    k = s[0]
+    taps = [
+        jnp.concatenate([pack[PACK_SHORT + 9 + 3 * t + g : PACK_SHORT + 10 + 3 * t + g, :] for g in range(3) for pack in (mine, other)], axis=1)
+        for t in range(3)
+    ]
+
+    def chunk(i, carry):
+        rows = at(CHUNK * i, CHUNK)
+        looked = mm(onehot[at(half * k + CHUNK * i, CHUNK), :], gate_table[...])
+        conv = jnp.concatenate([conv_mine[rows, :], conv_other[rows, :]], axis=1)
+        gated = (conv * looked[:, 0:256]).astype(bf16)
+        mid = looked[:, 256:512] + mm(gated, w_out[...])
+        mid_out[rows, :] = mid
+        normal, _ = unit(mid)
+        low = (normal * gain[0, 1:2, :]).astype(bf16)
+        hidden = gelu_only(mm(low, w_up[...])).astype(bf16)
+        stream = mid + mm(hidden, w_down[...])
+        stream_out[rows, :] = stream
+        normal, _ = unit(stream)
+        low = (normal * gain[1, 0:1, :]).astype(bf16)
+        mixed[rows, :] = mm(low, w_in[...])
+        return carry
+
+    lax.fori_loop(0, span // CHUNK, chunk, 0)
+    gates[0:HALO, :] = jnp.zeros((HALO, 768), f32)
+    step = 80
+    for start in range(HALO, span, step):
+        stop = start + step
+        gates[start:stop, :] = (
+            taps[0] * mixed[start:stop, :]
+            + taps[1] * mixed[start - 1 : stop - 1, :]
+            + taps[2] * mixed[start - 2 : stop - 2, :]
+        )
+    own = slice(HALO, HALO + half)
+    keep[...] = gates[own, 256:384] * gates[own, 512:640]
+    send[...] = gates[own, 384:512] * gates[own, 640:768]
+
+
+def turn_back_kernel(
+    s, conv_mine, conv_other, gates, stream, cot, gain, w_out, w_up, w_down,
+    keep, send, grad_x0, grad_mid, block_out, hidden_out, low_out, normed_out, pre_out, gated_out, mid_low_out, gain_out,
+    cot_rows, conv_grads,
+):
+    span = stream.shape[0]
+    half = span - 2 * HALO
+    k = s[0]
+    live = s[2]
+    cot_rows[0:HALO, :] = jnp.zeros((HALO, 256), f32)
+    cot_rows[HALO : HALO + half, :] = cot[at(half * k, half), :]
+    cot_rows[HALO + half :, :] = jnp.where(k == 0, cot[half : half + HALO, :], 0.0)
+    gain_out[...] = jnp.zeros_like(gain_out)
+
+    def chunk(i, carry):
+        rows = at(CHUNK * i, CHUNK)
+        local_row = lax.broadcasted_iota(jnp.int32, (CHUNK, 1), 0) + CHUNK * i
+        keep_mask = (local_row + (half * k - HALO) < live).astype(f32)
+        own_mask = ((local_row >= HALO) & (local_row < HALO + half)).astype(f32)
+        x0 = gates[rows, 0:256]
+        conv = jnp.concatenate([conv_mine[rows, :], conv_other[rows, :]], axis=1)
+        gated = (conv * x0).astype(bf16)
+        gated_out[rows, :] = gated
+        mid = stream[rows, :] + mm(gated, w_out[...])
+        normal, scale = unit(mid)
+        gain_row = gain[1, 1:2, :]
+        low = (normal * gain_row).astype(bf16)
+        normed_out[rows, :] = low
+        act, slope = gelu_parts(mm(low, w_up[...]))
+        hidden = act.astype(bf16)
+        hidden_out[rows, :] = hidden
+        block_out[rows, :] = (mid + mm(hidden, w_down[...])) * keep_mask
+        grad = cot_rows[rows, :] * keep_mask
+        grad_low = grad.astype(bf16)
+        low_out[rows, :] = grad_low
+        grad_pre = (slope * mm_nt(grad_low, w_down[...])).astype(bf16)
+        pre_out[rows, :] = grad_pre
+        grad_normed = mm_nt(grad_pre, w_up[...])
+        gain_out[0:1, :] += jnp.sum(grad_normed * normal * own_mask, axis=0, keepdims=True)
+        mid_grad = grad + unit_back(grad_normed * gain_row, normal, scale)
+        grad_mid[rows, :] = mid_grad
+        mid_low = mid_grad.astype(bf16)
+        mid_low_out[rows, :] = mid_low
+        grad_gated = mm_nt(mid_low, w_out[...])
+        conv_grads[rows, :] = grad_gated * x0
+        grad_x0[rows, :] = grad_gated * conv
+        return carry
+
+    lax.fori_loop(0, span // CHUNK, chunk, 0)
+    own = slice(HALO, HALO + half)
+    keep[...] = conv_grads[own, 0:128]
+    send[...] = conv_grads[own, 128:256]
+
+
+def conv_back_kernel(s, kept, received, mine, freq_filt, dft, twiddle, keep, send, spec, grads, stage, work, line):
+    join_rows(s, grads, kept, received)
+    skip_row = mine[PACK_SKIP + 1 : PACK_SKIP + 2, :]
+    load = lambda p, row: grads[pl.ds(BLOCK * p + row, 16), :]
+    to_freq(load, dft, twiddle, stage, spec)
+    times(freq_filt, spec, stage, True)
+
+    def store(p, row, value):
+        line[pl.ds(HALO + BLOCK * p + row, 16), :] = value + skip_row * load(p, row)
+
+    from_freq(dft, twiddle, stage, work, store)
+    hand_out(s, line, keep, send)
+
+
+def conv_back_first_kernel(
+    s, kept, received, mine, freq_filt, dft, twiddle, onehot, turned, conv_table, spec, grads, by_token, stage, work, line
+):
+    length = grads.shape[0]
+    join_rows(s, grads, kept, received)
+    skip_row = mine[PACK_SKIP : PACK_SKIP + 1, :]
+    load = lambda p, row: grads[pl.ds(BLOCK * p + row, 16), :]
+    to_freq(load, dft, twiddle, stage, spec)
+    times(freq_filt, spec, stage, True)
+
+    def store(p, row, value):
+        line[pl.ds(BLOCK * p + row, 16), :] = value + skip_row * load(p, row)
+
+    from_freq(dft, twiddle, stage, work, store)
+    by_token[...] = jnp.zeros_like(by_token)
+    width = turned.shape[2]
+    for i in range(length // width):
+        rows = slice(width * i, width * (i + 1))
+        pair = mm(onehot[HALO + width * i : HALO + width * (i + 1), :], conv_table[...])
+        back = line[rows, :]
+        gate_grads = jnp.concatenate([back * pair[:, 128:256], back * pair[:, 0:128]], axis=1).astype(bf16)
+        by_token[...] += mm(turned[i], gate_grads)[0:48, :]
+
+
+def filter_back_kernel(
+    level, s, spec_grad, spec_in, grads, product, filt, cosine, sine_turned, mine, rates, feats_turned, dft, twiddle,
+    second_out, first_out, skip_out, stage, work, line, inner,
+):
+    length = filt.shape[0]
+    times(spec_in, spec_grad, stage, True)
+
+    def store(p, row, value):
+        line[pl.ds(BLOCK * p + row, 16), :] = value
+
+    from_freq(dft, twiddle, stage, work, store)
+    rate = rates[s[3]]
+    second = mine[PACK_SECOND + 64 * level : PACK_SECOND + 64 * level + 64, :].astype(bf16)
+    weight = jnp.where(s[1] == 0, 0.5 * length, 0.0)
+    skip_out[...] = jnp.zeros_like(skip_out)
+    second_out[...] = jnp.zeros_like(second_out)
+    first_out[...] = jnp.zeros_like(first_out)
+    for i in range(length // 512):
+        rows = slice(512 * i, 512 * (i + 1))
+        decay, place = decay_of(rate, 512 * i, 512, length)
+        shaped = ((line[rows, :] * (1.0 / length) + (weight * place) * filt[rows, :]) * decay).astype(bf16)
+        skip_out[...] += jnp.sum((grads[rows, :] * product[rows, :]).reshape(64, 8, 128), axis=0)
+        second_out[...] += mm(sine_turned[64 * level : 64 * level + 64, rows], shaped)
+        inner = (mm_nt(shaped, second) * cosine[rows, 64 * level : 64 * level + 64]).astype(bf16)
+        first_out[...] += mm(feats_turned[:, rows], inner)
+
+
+def back_gates_kernel(
+    s, prod_mine, prod_other, grad_x0, gates, mixed, grad_mid, stream, gain, mine, other, w_in,
+    grad_stream, normed_out, mixed_low, short_out, gain_out, line,
+):
+    span = stream.shape[0]
+    half = span - 2 * HALO
+    taps = [
+        jnp.concatenate([pack[PACK_SHORT + 9 + 3 * t + g : PACK_SHORT + 10 + 3 * t + g, :] for g in range(3) for pack in (mine, other)], axis=1)
+        for t in range(3)
+    ]
+    step = 128
+    for start in list(range(HALO, HALO + half, step)) + [HALO + half]:
+        stop = start + (step if start < HALO + half else HALO)
+        product = jnp.concatenate([prod_mine[start:stop, :], prod_other[start:stop, :]], axis=1)
+        line[start:stop, 0:256] = grad_x0[start:stop, :]
+        line[start:stop, 256:512] = product * gates[start:stop, 512:768]
+        line[start:stop, 512:768] = product * gates[start:stop, 256:512]
+    short_out[...] = jnp.zeros_like(short_out)
+    gain_out[...] = jnp.zeros_like(gain_out)
+    step = 64
+    for start in range(HALO, HALO + half, step):
+        stop = start + step
+        values = mixed[start:stop, :]
+        total = None
+        for t in range(3):
+            shifted = line[start + t : stop + t, :]
+            part = taps[t] * shifted
+            total = part if total is None else total + part
+            short_out[t] += jnp.sum((shifted * values).reshape(step // 8, 8, 768), axis=0)
+        mixed_low[start - HALO : stop - HALO, :] = total.astype(bf16)
+
+    def chunk(i, carry):
+        rows = at(256 * i, 256)
+        wide = at(256 * i + HALO, 256)
+        normal, scale = unit(stream[wide, :])
+        gain_row = gain[1, 0:1, :]
+        normed_out[rows, :] = (normal * gain_row).astype(bf16)
+        grad_normed = mm_nt(mixed_low[rows, :], w_in[...])
+        gain_out[0:1, :] += jnp.sum(grad_normed * normal, axis=0, keepdims=True)
+        grad_stream[rows, :] = grad_mid[wide, :] + unit_back(grad_normed * gain_row, normal, scale)
+        return carry
+
+    lax.fori_loop(0, half // 256, chunk, 0)
+
+
+def back_first_kernel(
+    s, grad_stream, mid, onehot, turned, gate_table, conv_mine, conv_other, gain, w_out, w_up, w_down,
+    keep, send, hidden_out, low_out, normed_out, pre_out, gated_out, mid_low_out, by_token, gain_out,
+):
+    half = grad_stream.shape[0]
+    k = s[0]
+    by_token[...] = jnp.zeros_like(by_token)
+    gain_out[...] = jnp.zeros_like(gain_out)
+
+    def chunk(i, carry):
+        rows = at(256 * i, 256)
+        wide = at(256 * i + HALO, 256)
+        hot = onehot[at(half * k + 256 * i + HALO, 256), :]
+        x0 = mm(hot, gate_table[:, 0:256])
+        conv = jnp.concatenate([conv_mine[wide, :], conv_other[wide, :]], axis=1)
+        gated_out[rows, :] = (conv * x0).astype(bf16)
+        normal, scale = unit(mid[wide, :])
+        gain_row = gain[0, 1:2, :]
+        low = (normal * gain_row).astype(bf16)
+        normed_out[rows, :] = low
+        act, slope = gelu_parts(mm(low, w_up[...]))
+        hidden_out[rows, :] = act.astype(bf16)
+        grad = grad_stream[rows, :]
+        grad_low = grad.astype(bf16)
+        low_out[rows, :] = grad_low
+        grad_pre = (slope * mm_nt(grad_low, w_down[...])).astype(bf16)
+        pre_out[rows, :] = grad_pre
+        grad_normed = mm_nt(grad_pre, w_up[...])
+        gain_out[0:1, :] += jnp.sum(grad_normed * normal, axis=0, keepdims=True)
+        mid_grad = grad + unit_back(grad_normed * gain_row, normal, scale)
+        mid_low = mid_grad.astype(bf16)
+        mid_low_out[rows, :] = mid_low
+        grad_gated = mm_nt(mid_low, w_out[...])
+        conv_grad = grad_gated * x0
+        keep[rows, :] = conv_grad[:, 0:128]
+        send[rows, :] = conv_grad[:, 128:256]
+        flips = turned[k, :, at(256 * i, 256, 256)]
+        rest = mid_grad - mid_low.astype(f32)
+        gate_grads = jnp.concatenate([(grad_gated * conv).astype(bf16), mid_low, rest.astype(bf16)], axis=1)
+        by_token[...] += mm(flips, gate_grads)[0:48, :]
+        return carry
+
+    lax.fori_loop(0, half // 256, chunk, 0)
+
+
+R_OUT, R_UP, R_DOWN, R_IN = 128, 512, 512, 384
+
+
+def send_weights_kernel(level, with_in, s, w_out, w_up, w_down, w_in, out):
+    k = s[0]
+    first = k == 0
+    pick = lambda a, b: jnp.where(first, a.astype(f32), b.astype(f32))
+    out[0:128, :] = pick(w_out[level, :, 0:128], w_out[level, :, 128:256])
+    for j in range(2):
+        lanes = slice(128 * j, 128 * j + 128)
+        out[128 + 256 * j : 384 + 256 * j, :] = pick(
+            w_up[level, :, 128 * j : 128 * j + 128], w_up[level, :, 256 + 128 * j : 384 + 128 * j]
+        )
+        out[640 + 256 * j : 896 + 256 * j, :] = pick(w_down[level, 0:256, lanes], w_down[level, 256:512, lanes])
+    if with_in:
+        for g in range(3):
+            out[1152 + 128 * g : 1280 + 128 * g, :] = pick(w_in[level, g, 0:128, :], w_in[level, g, 128:256, :])
+
+
+def join_weights_kernel(level, with_in, s, w_out, w_up, w_down, w_in, first_part, second_part, out_full, up_full, down_full, *in_full):
+    k = s[0]
+    first = k == 0
+    low = lambda ref, a, b: ref[a:b, :].astype(bf16)
+    pick = lambda a, b: jnp.where(first, a, b)
+    mine_out = w_out[level]
+    a, b = first_part[0:128, :], second_part[0:128, :]
+    peer_out = jnp.concatenate([pick(a, b), pick(b, a)], axis=1).astype(bf16)
+    out_full[0:128, :] = pick(mine_out.astype(f32), peer_out.astype(f32)).astype(bf16)
+    out_full[128:256, :] = pick(peer_out.astype(f32), mine_out.astype(f32)).astype(bf16)
+    up_a, up_b = w_up[level, :, 0:256].astype(f32), w_up[level, :, 256:512].astype(f32)
+    up_full[:, 0:256] = pick(up_a, up_b).astype(bf16)
+    up_full[:, 256:512] = pick(up_b, up_a).astype(bf16)
+    down_a, down_b = w_down[level, 0:256, :].astype(f32), w_down[level, 256:512, :].astype(f32)
+    down_full[0:256, :] = pick(down_a, down_b).astype(bf16)
+    down_full[256:512, :] = pick(down_b, down_a).astype(bf16)
+    for n, part in enumerate((first_part, second_part)):
+        for j in range(2):
+            up_full[:, 512 + 256 * n + 128 * j : 640 + 256 * n + 128 * j] = low(part, 128 + 256 * j, 384 + 256 * j)
+            down_full[512 + 256 * n : 768 + 256 * n, 128 * j : 128 * j + 128] = low(part, 640 + 256 * j, 896 + 256 * j)
+    if with_in:
+        (full,) = in_full
+        for g in range(3):
+            own = w_in[level, g].astype(f32)
+            a, b = first_part[1152 + 128 * g : 1280 + 128 * g, :], second_part[1152 + 128 * g : 1280 + 128 * g, :]
+            peer = jnp.concatenate([pick(a, b), pick(b, a)], axis=0)
+            full[:, 256 * g : 256 * g + 128] = pick(own, peer).astype(bf16)
+            full[:, 256 * g + 128 : 256 * g + 256] = pick(peer, own).astype(bf16)
+
+
+def put_wide_grads(s, keep, send, row, gated, mid_low, normed, grad_pre, hidden, grad_low):
+    k = s[0]
+    first = k == 0
+    out = mm_tn(gated, mid_low)
+    for m in range(2):
+        a, b = out[128 * m : 128 * m + 128, 0:128], out[128 * m : 128 * m + 128, 128:256]
+        half = m + k - 2 * m * k
+        keep[half, row : row + 128, :] = jnp.where(first, a, b)
+        send[half, row : row + 128, :] = jnp.where(first, b, a)
+    for j in range(4):
+        target = (keep, send)[j % 2]
+        up = mm_tn(normed, grad_pre[:, 256 * j : 256 * j + 256])
+        down = mm_tn(hidden[:, 256 * j : 256 * j + 256], grad_low)
+        for n in range(2):
+            lanes = slice(128 * n, 128 * n + 128)
+            target[j // 2, row + 128 + 256 * n : row + 384 + 256 * n, :] = up[:, lanes]
+            target[j // 2, row + 640 + 256 * n : row + 896 + 256 * n, :] = down[:, lanes]
+
+
+def wide_grads_kernel(pad, s, gated, mid_low, normed, grad_pre, hidden, grad_low, keep, send):
+    stop = gated.shape[0] - pad
+    own = lambda ref: ref[pad:stop, :]
+    put_wide_grads(s, keep, send, 0, own(gated), own(mid_low), own(normed), own(grad_pre), own(hidden), own(grad_low))
+
+
+def wide_and_in_grads_kernel(s, gated, mid_low, normed, grad_pre, hidden, grad_low, normed_in, mixed_low, keep, send):
+    k = s[0]
+    first = k == 0
+    put_wide_grads(
+        s, keep, send, 0, gated[...], mid_low[...], normed[...], grad_pre[...], hidden[...], grad_low[...]
+    )
+    for g in range(3):
+        both = mm_tn(normed_in[...], mixed_low[:, 256 * g : 256 * g + 256])
+        for m in range(2):
+            block = both[:, 128 * m : 128 * m + 128]
+            half = m + k - 2 * m * k
+            row = 1152 + 128 * g
+            keep[half, row : row + 128, :] = jnp.where(first, block[0:128], block[128:256])
+            send[half, row : row + 128, :] = jnp.where(first, block[128:256], block[0:128])
+
+
+def add_kernel(s, kept, received, own_out, peer_out):
+    own_out[...] = kept[0] + received[0]
+    peer_out[...] = kept[1] + received[1]
+
+
+def add_one_kernel(s, kept, received, out):
+    out[...] = kept[...] + received[...]
+
+
+def spread_grads_kernel(with_in, s, kept, received, out, up, down, *w_in):
+    first = s[0] == 0
+    a, b = kept, received
+    pick = lambda x, y: jnp.where(first, x, y)
+
+    def both(row, rows):
+        x, y = a[row : row + rows, :], b[row : row + rows, :]
+        return pick(x, y), pick(y, x)
+
+    x, y = both(0, 128)
+    out[:, 0:128] = x
+    out[:, 128:256] = y
+    for j in range(2):
+        lanes = slice(128 * j, 128 * j + 128)
+        x, y = both(128 + 256 * j, 256)
+        up[:, 128 * j : 128 * j + 128] = x
+        up[:, 256 + 128 * j : 384 + 128 * j] = y
+        x, y = both(640 + 256 * j, 256)
+        down[0:256, lanes] = x
+        down[256:512, lanes] = y
+    if with_in:
+        for g in range(3):
+            x, y = both(1152 + 128 * g, 128)
+            w_in[0][g, 0:128, :] = x
+            w_in[0][g, 128:256, :] = y
+
+
+F_GAIN1, F_GAIN0, F_EMBED, F_FIRST, F_SKIPPAD, F_SHORT, F_TOKEN = 0, 8, 16, 32, 72, 80, 112
+F_ROWS = 160
+C_SECOND1, C_SECOND0, C_SKIP, C_TOKEN = 0, 64, 128, 136
+C_ROWS = 232
+
+
+def small_kernel(
+    s, gain_mid1, gain_in1, gain_mid0, by_token0, by_token12, first1, first0, short1, second1, second0, skip1, skip0, flat, mine
+):
+    k = s[0]
+    flat[...] = jnp.zeros_like(flat)
+    flat[F_GAIN1 : F_GAIN1 + 8, :] = gain_mid1[...]
+    flat[F_GAIN0 : F_GAIN0 + 8, :] = gain_mid0[...]
+    flat[F_GAIN1 + 1 : F_GAIN1 + 2, :] = gain_in1[0:1, :]
+    flat[F_EMBED : F_EMBED + 16, :] = by_token0[0:16, 256:512] + by_token0[0:16, 512:768]
+    flat[F_FIRST : F_FIRST + 40, 0:64] = first0[...]
+    flat[F_FIRST : F_FIRST + 40, 128:192] = first1[...]
+    swap = lambda v: jnp.where(k == 0, v, jnp.concatenate([v[:, 128:256], v[:, 0:128]], axis=1))
+    for t in range(3):
+        total = jnp.sum(short1[t], axis=0, keepdims=True)
+        for g in range(3):
+            flat[F_SHORT + 3 * t + g : F_SHORT + 3 * t + g + 1, :] = swap(total[:, 256 * g : 256 * g + 256])
+    flat[F_TOKEN : F_TOKEN + 48, :] = swap(by_token0[:, 0:256])
+    mine[C_SECOND1 : C_SECOND1 + 64, :] = second1[...]
+    mine[C_SECOND0 : C_SECOND0 + 64, :] = second0[...]
+    mine[C_SKIP : C_SKIP + 8, :] = jnp.zeros((8, 128), f32)
+    mine[C_SKIP : C_SKIP + 1, :] = jnp.sum(skip0[...], axis=0, keepdims=True)
+    mine[C_SKIP + 1 : C_SKIP + 2, :] = jnp.sum(skip1[...], axis=0, keepdims=True)
+    mine[C_TOKEN : C_TOKEN + 48, :] = by_token12[:, 0:128]
+    mine[C_TOKEN + 48 : C_TOKEN + 96, :] = by_token12[:, 128:256]
+
+
+def chip_kernel(s, flat, flat_in, mine, mine_in, out):
+    first = s[0] == 0
+    total = flat[...] + flat_in[...]
+    out[0:F_ROWS, :] = total
+    out[F_ROWS : F_ROWS + C_ROWS, 0:128] = jnp.where(first, mine[...], mine_in[...])
+    out[F_ROWS : F_ROWS + C_ROWS, 128:256] = jnp.where(first, mine_in[...], mine[...])
+
+
+def last_kernel(
+    s, here, there, embed, gain, own, peer, w_own, w_first, w_second,
+    embed_out, gain_out, in_out, short_out, first_out, second_out, skip_out,
+):
+    first = s[0] == 0
+    pick = lambda x, y: jnp.where(first, x, y)
+
+    def plain(row, rows):
+        return here[row : row + rows, :] + there[row : row + rows, :]
+
+    def halves(row, rows):
+        left = here[row : row + rows, 0:128] + there[row : row + rows, 128:256]
+        right = here[row : row + rows, 128:256] + there[row : row + rows, 0:128]
+        return left, right
+
+    gains1 = plain(F_GAIN1, 8)
+    gains0 = plain(F_GAIN0, 8)
+    gain_out[1, 0:1, :] = gains1[1:2, :]
+    gain_out[1, 1:2, :] = gains1[0:1, :]
+    gain_out[0, 1:2, :] = gains0[0:1, :]
+    firsts = plain(F_FIRST, 40)
+    first_out[0] = firsts[0:33, 0:64]
+    first_out[1] = firsts[0:33, 128:192]
+    short = halves(F_SHORT, 16)[0]
+    for t in range(3):
+        short_out[1, t] = short[3 * t : 3 * t + 3, :]
+    mine_rows = lambda row, rows: halves(F_ROWS + row, rows)
+    second_out[1] = mine_rows(C_SECOND1, 64)[0]
+    second_out[0] = mine_rows(C_SECOND0, 64)[0]
+    skip_out[...] = mine_rows(C_SKIP, 8)[0][0:2]
+    tokens = [halves(F_TOKEN, 48), mine_rows(C_TOKEN, 48), mine_rows(C_TOKEN + 48, 48)]
+    normal, scale = unit(embed[...])
+    gain_row = gain[0, 0:1, :]
+    low = (normal * gain_row).astype(bf16)
+    grad_normed = jnp.zeros((16, 256), f32)
+    for g in range(3):
+        for h, pack in ((0, own), (1, peer)):
+            grads = tokens[g][h]
+            table = pack[16 * g : 16 * g + 16, :]
+            summed = jnp.zeros((16, 128), f32)
+            for t in range(3):
+                row = PACK_SHORT + 3 * t + g
+                part = grads[16 * t : 16 * t + 16, :]
+                summed += pack[row : row + 1, :] * part
+                if h == 0:
+                    short_out[0, t, g : g + 1, :] = jnp.sum(table * part, axis=0, keepdims=True)
+            if h == 0:
+                in_out[g] = lax.dot_general(
+                    low.astype(f32), summed, (((0,), (0,)), ((), ())), precision=precise, preferred_element_type=f32
+                )
+                weight = w_own[0, g].astype(f32)
+            else:
+                rows = slice(128 * g, 128 * g + 128)
+                a, b = w_first[rows, :], w_second[rows, :]
+                weight = jnp.concatenate([pick(a, b), pick(b, a)], axis=0)
+            grad_normed += lax.dot_general(
+                summed, weight, (((1,), (1,)), ((), ())), precision=precise, preferred_element_type=f32
+            )
+    gain_out[0, 0:1, :] = jnp.sum(grad_normed * normal, axis=0, keepdims=True)
+    embed_out[...] = plain(F_EMBED, 16) + unit_back(grad_normed * gain_row, normal, scale)
+
+
+def send_in_kernel(s, w_in, out):
+    first = s[0] == 0
+    for g in range(3):
+        a, b = w_in[0, g, 0:128, :].astype(f32), w_in[0, g, 128:256, :].astype(f32)
+        out[128 * g : 128 * g + 128, :] = jnp.where(first, a, b)
+
+
+def block_send_kernel(s, block_out, mine, other):
+    spot = s[4]
+    mine[...] = block_out[at(HALO + 128 * spot, 128), :]
+    near = spot + 1 - 2 * s[0]
+    other[...] = block_out[at(HALO + 128 * near, 128), :]
+
+
+def block_pick_kernel(s, mine, received, out):
+    out[...] = jnp.where(s[5] == 1, mine[...], received[...])
+
+
+def block_join_kernel(s, here, there, out):
+    first = s[1] == 0
+    out[0] = jnp.where(first, here[...], there[...])
+    out[1] = jnp.where(first, there[...], here[...])
+
+
+def chip_local(
+    ids, live, embed, norm_gain, in_weight, short_kernel, filter_first, filter_second, skip_gain,
+    out_weight, up_weight, down_weight, cotangent,
+):
+    count = lax.axis_size("seq")
+    rank = lax.axis_index("seq")
+    group = lax.axis_index("ch")
+    width = ids.shape[1]
+    length = width * count
+    half = length // 2
+    span = half + 2 * HALO
+    core = rank % 2
+    swaps = [(i, i ^ 1) for i in range(count)]
+    across = lambda v: lax.ppermute(v, "ch", [(0, 1), (1, 0)])
+    beside = lambda v: lax.ppermute(v, "seq", swaps)
+    half_ranks = count // 2
+    holder = (rank // half_ranks == core).astype(jnp.int32)
+    s = jnp.stack([core, group, live[group], group ^ core, rank % half_ranks, holder]).astype(jnp.int32)
+    dft = jnp.asarray(dft_table()).astype(bf16)
+    twiddle = jnp.asarray(twiddle_table())
+    feats = jnp.asarray(feature_table(length))
+    feats_turned = jnp.asarray(np.pad(feature_table(length).T, ((0, 40 - FEAT), (0, 0)))).astype(bf16)
+    rates = jnp.asarray(rate_table())
+
+    in_own = jnp.swapaxes(in_weight, 1, 2)
+    pack = run(pack_kernel, arr(PACK_ROWS, 128), s, embed, norm_gain, in_own, filter_second, short_kernel, skip_gain)
+    pack_in = across(pack)
+    own_ids = lax.dynamic_index_in_dim(ids, group, 0, True)
+    all_ids = lax.all_to_all(jnp.broadcast_to(own_ids, (count, width)), "seq", split_axis=0, concat_axis=0, tiled=True)
+    cot = lax.all_gather(lax.dynamic_index_in_dim(cotangent, group, 0, False), "seq", axis=0, tiled=True)
+
+    sine, cosine, sine_turned = run(
+        sine_kernel, [arr(length, 128), arr(length, 128), arr(128, length, kind=bf16)], s, feats, filter_first
+    )
+    weights = []
+    for level, with_in in ((0, False), (1, True)):
+        rows = 1536 if with_in else 1152
+        part = run(
+            functools.partial(send_weights_kernel, level, with_in), arr(rows, 128), s, out_weight, up_weight, down_weight, in_own
+        )
+        part_in = across(part)
+        other_in = beside(part_in)
+        shapes = [arr(256, 256, kind=bf16), arr(256, 1024, kind=bf16), arr(1024, 256, kind=bf16)]
+        if with_in:
+            shapes.append(arr(256, 768, kind=bf16))
+        weights.append(
+            run(
+                functools.partial(join_weights_kernel, level, with_in), shapes, s, out_weight, up_weight, down_weight, in_own,
+                part_in, other_in,
+            )
+        )
+    (w_out0, w_up0, w_down0), (w_out1, w_up1, w_down1, w_in1) = weights
+    first_in = across(run(send_in_kernel, arr(384, 128), s, in_own))
+    first_in_other = beside(first_in)
+
+    mine, other, conv_table, gate_table = run(
+        table_kernel,
+        [arr(PACK_ROWS, 128), arr(PACK_ROWS, 128), arr(128, 256, kind=bf16), arr(128, 512, kind=bf16)],
+        s, pack, pack_in, embed,
+    )
+    filt0, filt1, freq0, freq1 = run(
+        filter_kernel, [arr(length, 128), arr(length, 128), arr(*SPECTRUM), arr(*SPECTRUM)], s, sine, mine, rates, dft, twiddle,
+        scratch=[stage_scratch(), spec_scratch()],
+    )
+    onehot, turned = run(
+        onehot_kernel, [arr(length + 2 * HALO, 128, kind=bf16), arr(2, 128, half, kind=bf16)], s, all_ids,
+        scratch=[pltpu.VMEM((length + 2 * HALO, 128), f32)],
+    )
+    line = pltpu.VMEM((length + 2 * HALO, 128), f32)
+    conv_scratch = [stage_scratch(), spec_scratch(), line]
+
+    conv_mine0, sent, spec0, product0 = run(
+        conv_first_kernel, [arr(span, 128), arr(span, 128), arr(*SPECTRUM), arr(length, 128)],
+        s, onehot, conv_table, mine, freq0, dft, twiddle, scratch=conv_scratch,
+    )
+    conv_other0 = beside(sent)
+    kept, sent, mid0, stream1, gates1, mixed1 = run(
+        forward_first_kernel,
+        [arr(half, 128), arr(half, 128), arr(span, 256), arr(span, 256), arr(span, 768), arr(span, 768)],
+        s, onehot, gate_table, conv_mine0, conv_other0, norm_gain, w_out0, w_up0, w_down0, w_in1, mine, other,
+    )
+    received = beside(sent)
+    conv_mine1, sent, spec1, product1 = run(
+        conv_second_kernel, [arr(span, 128), arr(span, 128), arr(*SPECTRUM), arr(length, 128)],
+        s, kept, received, mine, freq1, dft, twiddle, scratch=conv_scratch,
+    )
+    conv_other1 = beside(sent)
+    low = lambda *shape: arr(*shape, kind=bf16)
+    (kept, sent, grad_x0, grad_mid1, block, hidden, grad_low, normed, grad_pre, gated, mid_low, gain_mid1) = run(
+        turn_back_kernel,
+        [
+            arr(half, 128), arr(half, 128), arr(span, 256), arr(span, 256), arr(span, 256), low(span, 1024), low(span, 256),
+            low(span, 256), low(span, 1024), low(span, 256), low(span, 256), arr(8, 256),
+        ],
+        s, conv_mine1, conv_other1, gates1, stream1, cot, norm_gain, w_out1, w_up1, w_down1,
+        scratch=[pltpu.VMEM((span, 256), f32), pltpu.VMEM((span, 256), f32)],
+    )
+    received = beside(sent)
+    grads_keep, grads_send = run(
+        functools.partial(wide_grads_kernel, HALO), [arr(2, 1152, 128), arr(2, 1152, 128)],
+        s, gated, mid_low, normed, grad_pre, hidden, grad_low,
+    )
+    block_mine, block_other = run(block_send_kernel, [arr(width, 256), arr(width, 256)], s, block)
+    block_here = run(block_pick_kernel, arr(width, 256), s, block_mine, beside(block_other))
+    block_out = run(block_join_kernel, arr(2, width, 256), s, block_here, across(block_here))
+
+    prod_mine, sent, spec_grad1, grads1 = run(
+        conv_back_kernel, [arr(span, 128), arr(span, 128), arr(*SPECTRUM), arr(length, 128)],
+        s, kept, received, mine, freq1, dft, twiddle, scratch=conv_scratch,
+    )
+    prod_other = beside(sent)
+    filter_shapes = [arr(64, 128), arr(40, 64), arr(8, 128)]
+    filter_scratch = [stage_scratch(), spec_scratch(), pltpu.VMEM((length, 128), f32), pltpu.VMEM((8, 128), f32)]
+    second1, first1, skip1 = run(
+        functools.partial(filter_back_kernel, 1), filter_shapes, s, spec_grad1, spec1, grads1, product1, filt1, cosine,
+        sine_turned, mine, rates, feats_turned, dft, twiddle, scratch=filter_scratch,
+    )
+
+    def reduce_wide(keep, send, with_in):
+        rows = keep.shape[1]
+        own, peer = run(add_kernel, [arr(rows, 128), arr(rows, 128)], s, keep, beside(send))
+        total = run(add_one_kernel, arr(rows, 128), s, own, across(peer))
+        shapes = [arr(128, 256), arr(256, 512), arr(512, 256)] + ([arr(3, 256, 128)] if with_in else [])
+        return run(functools.partial(spread_grads_kernel, with_in), shapes, s, total, beside(total))
+
+    grad_out1, grad_up1, grad_down1 = reduce_wide(grads_keep, grads_send, False)
+    grad_stream1, normed_in, mixed_low, short1, gain_in1 = run(
+        back_gates_kernel,
+        [arr(half, 256), low(half, 256), low(half, 768), arr(3, 8, 768), arr(8, 256)],
+        s, prod_mine, prod_other, grad_x0, gates1, mixed1, grad_mid1, stream1, norm_gain, mine, other, w_in1,
+        scratch=[pltpu.VMEM((span, 768), f32)],
+    )
+    (kept, sent, hidden, grad_low, normed, grad_pre, gated, mid_low, by_token0, gain_mid0) = run(
+        back_first_kernel,
+        [
+            arr(half, 128), arr(half, 128), low(half, 1024), low(half, 256), low(half, 256), low(half, 1024), low(half, 256),
+            low(half, 256), arr(48, 768), arr(8, 256),
+        ],
+        s, grad_stream1, mid0, onehot, turned, gate_table, conv_mine0, conv_other0, norm_gain, w_out0, w_up0, w_down0,
+    )
+    received = beside(sent)
+    grads_keep, grads_send = run(
+        wide_and_in_grads_kernel, [arr(2, 1536, 128), arr(2, 1536, 128)],
+        s, gated, mid_low, normed, grad_pre, hidden, grad_low, normed_in, mixed_low,
+    )
+    grad_out0, grad_up0, grad_down0, grad_in1 = reduce_wide(grads_keep, grads_send, True)
+    spec_grad0, grads0, by_token12 = run(
+        conv_back_first_kernel, [arr(*SPECTRUM), arr(length, 128), arr(48, 256)],
+        s, kept, received, mine, freq0, dft, twiddle, onehot, turned, conv_table, scratch=conv_scratch,
+    )
+    second0, first0, skip0 = run(
+        functools.partial(filter_back_kernel, 0), filter_shapes, s, spec_grad0, spec0, grads0, product0, filt0, cosine,
+        sine_turned, mine, rates, feats_turned, dft, twiddle, scratch=filter_scratch,
+    )
+    flat, parts = run(
+        small_kernel, [arr(F_ROWS, 256), arr(C_ROWS, 128)],
+        s, gain_mid1, gain_in1, gain_mid0, by_token0, by_token12, first1, first0, short1, second1, second0, skip1, skip0,
+    )
+    here = run(chip_kernel, arr(F_ROWS + C_ROWS, 256), s, flat, beside(flat), parts, beside(parts))
+    grad_embed, grad_gain, grad_in0, grad_short, grad_first, grad_second, grad_skip = run(
+        last_kernel,
+        [
+            arr(16, 256), arr(2, 2, 256), arr(3, 256, 128), arr(2, 3, 3, 128), arr(2, FEAT, 64), arr(2, 64, 128), arr(2, 128),
+        ],
+        s, here, across(here), embed, norm_gain, pack, pack_in, in_own, first_in, first_in_other,
+    )
+    return (
+        block_out,
+        grad_embed,
+        grad_gain,
+        jnp.swapaxes(jnp.stack([grad_in0, grad_in1]), 1, 2),
+        grad_short,
+        grad_first,
+        grad_second,
+        grad_skip,
+        jnp.stack([grad_out0, grad_out1]),
+        jnp.stack([grad_up0, grad_up1]),
+        jnp.stack([grad_down0, grad_down1]),
+    )
+
+
 def solution(mesh):
     in_specs = (
         P(None, "seq"),
@@ -469,4 +1564,9 @@
         P(None, None, "ch"),
         P(None, "ch", None),
     )
-    return jax.shard_map(local, mesh=mesh, in_specs=in_specs, out_specs=out_specs, check_vma=False)
+
+    def either(*args):
+        length = args[0].shape[1] * lax.axis_size("seq")
+        return (chip_local if length == BLOCKS * BLOCK else local)(*args)
+
+    return jax.shard_map(either, mesh=mesh, in_specs=in_specs, out_specs=out_specs, check_vma=False)

time: 699 us -> 268 us (0.38); the launches traced: 691 us -> 267 us
  waiting for transfers between devices: 340 us -> 81.8 us
  Pallas kernels: 0 us -> 105 us
  matrix products: 88.6 us -> 0 us
  other arithmetic: 71.9 us -> 3.76 us
  blocking collectives: 50.7 us -> 0 us
  starting transfers between devices: 57 us -> 20.6 us
  local copies, waits for them, and re-layouts: 66.3 us -> 40 us
    psum x9 -> x0, waiting for transfers between devices: 300 us -> none  [the longest x2 149 us: local(): lax.psum((gain_grad, in_grad, kernel_grad, grad_second, grad_skip, out_gr...]
    pallas_call x0 -> x34, Pallas kernels: none -> 105 us  [run(): pl.pallas_call(body, out_shape=shapes, in_specs=[smem] + [vmem] * len(arr...]
    dot_general x116 -> x0, matrix products: 88.6 us -> none  [the longest x48 35.5 us: along_block(): return jnp.einsum('...kb,bj->...kj', values, table, precision=precise)]
    ppermute x4 -> x24, waiting for transfers between devices: 1.98 us -> 81.8 us  [the longest x8 72.6 us: chip_local(): across = lambda v: lax.ppermute(v, 'ch', [(0, 1), (1, 0)])]
    unnamed x4 -> x0, other arithmetic: 40.4 us -> none
    psum x1 -> x0, blocking collectives: 39.7 us -> none  [local(): filter_grads = lax.psum(jnp.stack(first_grads), ('seq', 'ch'))]
    all_to_all x7 -> x1, waiting for transfers between devices: 37.8 us -> 0.01 us  [chip_local(): lax.all_to_all(jnp.broadcast_to(own_ids, (count, width)), 'seq', split_ax...]
    all_to_all x7 -> x1, starting transfers between devices: 37.6 us -> 6.57 us  [chip_local(): lax.all_to_all(jnp.broadcast_to(own_ids, (count, width)), 'seq', split_ax...]
  transfers between devices with their start and end apart: 20 -> 26, of which waited for: 17 -> 12; matrix products, arithmetic and copies ran while one was open for 7% -> 1% of each run, Pallas kernels for 0% -> 28%
where the time goes in v1:
time: 268 us; the launch traced here: 267 us
  Pallas kernels  105 us (39%)
  waiting for transfers between devices  81.8 us (31%)
  local copies, waits for them, and re-layouts  40 us (15%)
  starting transfers between devices  20.6 us (8%)
  between operations  15.2 us (6%)
  other arithmetic  3.76 us (1%)
    pallas_call x34, Pallas kernels, run(): pl.pallas_call(body, out_shape=shapes, in_specs=[smem] + [vmem] * len(arr...  105 us
    ppermute x8, waiting for transfers between devices, chip_local(): across = lambda v: lax.ppermute(v, 'ch', [(0, 1), (1, 0)])  72.6 us
    unnamed x178, local copies, waits for them, and re-layouts  36.8 us
    ppermute x8, starting transfers between devices, chip_local(): across = lambda v: lax.ppermute(v, 'ch', [(0, 1), (1, 0)])  11.4 us
    ppermute x16, waiting for transfers between devices, chip_local(): beside = lambda v: lax.ppermute(v, 'seq', swaps)  9.23 us
    all_to_all x1, starting transfers between devices, chip_local(): lax.all_to_all(jnp.broadcast_to(own_ids, (count, width)), 'seq', split_ax...  6.57 us
  transfers between devices with their start and end apart: 26, of which 12 were waited for; matrix products, arithmetic and copies ran while one was open for 1% of the time, Pallas kernels for 28%

profile of v1, /device:TPU:0, one launch (start us, length us, event | category | flops | bytes accessed | tf_op | source)
XLA Modules:
  0.0 266.8 jit_solution(7071081995649743745)
XLA Ops:
  15.5 3.0 %collective-permute-start.4 = (f32[1536,128]{1,0:T(8,128)S(1)}, f32[1536,128]{1,0:T(8,128)}, u32[]{:S(2)}, u32[]{:S(2)}) collective-permute-start(f32[1536,128]{1,0:T(8,128)S(1)} %shard_map.265), channel_id=1, source_target_pairs={{0,1},{1,0},{2,3},{3,2},{4,5},{5,4},{6,7},{7,6},{8,9},{9,8},{10,11... | collective-permute-start | bytes 2359304 | tf_op jit(solution)/shard_map/ppermute | solution.py:1370
  19.2 17.8 %collective-permute-done.4.first_part = f32[1536,128]{1,0:T(8,128)} collective-permute-done((f32[1536,128]{1,0:T(8,128)S(1)}, f32[1536,128]{1,0:T(8,128)}, u32[]{:S(2)}, u32[]{:S(2)}) %collective-permute-start.4) | collective-permute-done | bytes 786464 | tf_op jit(solution)/shard_map/ppermute | solution.py:1370
  40.0 9.7 %collective-permute-done.2.first_part = f32[1152,128]{1,0:T(8,128)} collective-permute-done((f32[1152,128]{1,0:T(8,128)S(1)}, f32[1152,128]{1,0:T(8,128)}, u32[]{:S(2)}, u32[]{:S(2)}) %collective-permute-start.2) | collective-permute-done | bytes 589856 | tf_op jit(solution)/shard_map/ppermute | solution.py:1370
  50.3 6.6 %all-to-all-start = ((s32[16,1,128]{2,1,0:T(1,128)}), s32[16,1,128]{2,1,0:T(1,128)S(1)}, u32[]{:S(2)}, u32[]{:S(2)}) async-start(s32[16,1,128]{2,1,0:T(1,128)} %broadcast_in_dim.2), calls=%async_computation | async-start | bytes 16384 | tf_op jit(solution)/shard_map/all_to_all | solution.py:1385
  58.1 6.6 %shard_map.260 = (f32[2048,128]{1,0:T(8,128)S(1)}, f32[2048,128]{1,0:T(8,128)S(1)}, bf16[128,2048]{1,0:T(8,128)(2,1)S(1)}) custom-call(s32[6]{0:T(128)S(1)} %stack.63.s, f32[2048,33]{1,0:T(8,128)S(1)} %copy-done.54, f32[2,33,64]{2,1,0:T(8,128)S(1)} %copy.34.firsts), custom_call_target="tpu_custom_call" | custom-call | tf_op jit(solution)/shard_map/pallas_call | solution.py:464
  72.7 8.4 %shard_map.261 = (f32[2048,128]{1,0:T(8,128)S(1)}, f32[2048,128]{1,0:T(8,128)S(1)}, f32[9,256,256]{2,1,0:T(8,128)S(1)}, f32[9,256,256]{2,1,0:T(8,128)S(1)}) custom-call(s32[6]{0:T(128)S(1)} %stack.63.s, f32[2048,128]{1,0:T(8,128)S(1)} %copy-done.56, f32[200,128]{1,0:T(8,128)S(1)} %get-tuple-element.114.mine, f32[2,1,128]{2,1,0:T(1,128)S(1)} %copy-done.82, ...), custom_call_target="tpu_custom_call" | custom-call | tf_op jit(solution)/shard_map/pallas_call | solution.py:464
  83.1 8.3 %shard_map.262 = (f32[1056,128]{1,0:T(8,128)S(1)}, f32[1056,128]{1,0:T(8,128)S(1)}, f32[9,256,256]{2,1,0:T(8,128)S(1)}, f32[2048,128]{1,0:T(8,128)S(1)}) custom-call(s32[6]{0:T(128)S(1)} %stack.63.s, bf16[2080,128]{1,0:T(8,128)(2,1)S(1)} %get-tuple-element.111.onehot, bf16[128,256]{1,0:T(8,128)(2,1)S(1)} %get-tuple-element.113.conv_table, ...), custom_call_target="tpu_custom_call" | custom-call | tf_op jit(solution)/shard_map/pallas_call | solution.py:464
  91.9 2.4 shard_map.264
  94.3 2.1 shard_map.266
  98.1 7.6 %shard_map.267 = (f32[1024,128]{1,0:T(8,128)S(1)}, f32[1024,128]{1,0:T(8,128)S(1)}, f32[1056,256]{1,0:T(8,128)S(1)}, f32[1056,256]{1,0:T(8,128)S(1)}, f32[1056,768]{1,0:T(8,128)S(1)}, /*index=5*/f32[1056,768]{1,0:T(8,128)S(1)}) custom-call(s32[6]{0:T(128)S(1)} %stack.63.s, bf16[2080,128]{1,0:T(8,128)(2,1)S(1)} %get-tuple-element.111.onehot, ...), custom_call_target="tpu_custom_call" | custom-call | tf_op jit(solution)/shard_map/pallas_call | solution.py:464
  113.2 6.9 %shard_map.268 = (f32[1056,128]{1,0:T(8,128)S(1)}, f32[1056,128]{1,0:T(8,128)S(1)}, f32[9,256,256]{2,1,0:T(8,128)S(1)}, f32[2048,128]{1,0:T(8,128)S(1)}) custom-call(s32[6]{0:T(128)S(1)} %stack.63.s, f32[1024,128]{1,0:T(8,128)S(1)} %get-tuple-element.124.kept, f32[1024,128]{1,0:T(8,128)S(1)} %collective-permute-done.6.received, ...), custom_call_target="tpu_custom_call" | custom-call | tf_op jit(solution)/shard_map/pallas_call | solution.py:464
  135.8 7.0 %shard_map.269 = (f32[1024,128]{1,0:T(8,128)S(1)}, f32[1024,128]{1,0:T(8,128)S(1)}, f32[1056,256]{1,0:T(8,128)S(1)}, f32[1056,256]{1,0:T(8,128)S(1)}, f32[1056,2...) custom-call(s32[6]{0:T(128)S(1)} %stack.63.s, ...), custom_call_target="tpu_custom_call" | custom-call | tf_op jit(solution)/shard_map/pallas_call | solution.py:464
  144.8 7.0 %shard_map.273 = (f32[1056,128]{1,0:T(8,128)S(1)}, f32[1056,128]{1,0:T(8,128)S(1)}, f32[9,256,256]{2,1,0:T(8,128)S(1)}, f32[2048,128]{1,0:T(8,128)S(1)}) custom-call(s32[6]{0:T(128)S(1)} %stack.63.s, f32[1024,128]{1,0:T(8,128)S(1)} %get-tuple-element.138.kept, f32[1024,128]{1,0:T(8,128)S(1)} %collective-permute-done.10.received, ...), custom_call_target="tpu_custom_call" | custom-call | tf_op jit(solution)/shard_map/pallas_call | solution.py:464
  154.0 6.0 %shard_map.274 = (f32[1024,256]{1,0:T(8,128)S(1)}, bf16[1024,256]{1,0:T(8,128)(2,1)S(1)}, bf16[1024,768]{1,0:T(8,128)(2,1)S(1)}, f32[3,8,768]{2,1,0:T(8,128)S(1)}, f32[8,256]{1,0:T(8,128)S(1)}) custom-call(s32[6]{0:T(128)S(1)} %stack.63.s, f32[1056,128]{1,0:T(8,128)S(1)} %get-tuple-element.140.prod_mine, f32[1056,128]{1,0:T(8,128)S(1)} %collective-permute-done.11.prod_other, ...), custom_call_target="tpu_custom_call" | custom-call | tf_op jit(solution)/shard_map/pallas_call | solution.py:464
  160.0 7.2 %shard_map.275 = (f32[1024,128]{1,0:T(8,128)S(1)}, f32[1024,128]{1,0:T(8,128)S(1)}, bf16[1024,1024]{1,0:T(8,128)(2,1)S(1)}, bf16[1024,256]{1,0:T(8,128)(2,1)S(1)...) custom-call(s32[6]{0:T(128)S(1)} %stack.63.s, ...), custom_call_target="tpu_custom_call" | custom-call | tf_op jit(solution)/shard_map/pallas_call | solution.py:464
  167.2 2.5 shard_map.283
  177.2 17.2 %collective-permute-done.19.received = f32[1536,128]{1,0:T(8,128)S(1)} collective-permute-done((f32[1536,128]{1,0:T(8,128)S(1)}, f32[1536,128]{1,0:T(8,128)S(1)}, u32[]{:S(2)}, u32[]{:S(2)}) %collective-permute-start.19) | collective-permute-done | bytes 786464 | tf_op jit(solution)/shard_map/ppermute | solution.py:1370
  195.1 11.1 %collective-permute-done.22.received = f32[1152,128]{1,0:T(8,128)S(1)} collective-permute-done((f32[1152,128]{1,0:T(8,128)S(1)}, f32[1152,128]{1,0:T(8,128)S(1)}, u32[]{:S(2)}, u32[]{:S(2)}) %collective-permute-start.22) | collective-permute-done | bytes 589856 | tf_op jit(solution)/shard_map/ppermute | solution.py:1370
  207.0 4.8 %shard_map.277 = (f32[64,128]{1,0:T(8,128)S(1)}, f32[40,64]{1,0:T(8,128)S(1)}, f32[8,128]{1,0:T(8,128)S(1)}) custom-call(s32[6]{0:T(128)S(1)} %stack.63.s, f32[9,256,256]{2,1,0:T(8,128)S(1)} %get-tuple-element.154.spec_grad, f32[9,256,256]{2,1,0:T(8,128)S(1)} %copy-done.26, f32[2048,128]{1,0:T(8,128)S(1)} %get-tuple-element.156.grads, ...), custom_call_target="tpu_custom_call" | custom-call | tf_op jit(solution)/shard_map/pallas_call | solution.py:464
  211.9 7.9 %shard_map.276 = (f32[9,256,256]{2,1,0:T(8,128)S(1)}, f32[2048,128]{1,0:T(8,128)S(1)}, f32[48,256]{1,0:T(8,128)S(1)}) custom-call(s32[6]{0:T(128)S(1)} %stack.63.s, f32[1024,128]{1,0:T(8,128)S(1)} %get-tuple-element.151.kept, f32[1024,128]{1,0:T(8,128)S(1)} %collective-permute-done.12.received, f32[200,128]{1,0:T(8,128)S(1)} %get-tuple-element.114.mine, ...), custom_call_target="tpu_custom_call" | custom-call | tf_op jit(solution)/shard_map/pallas_call | solution.py:464
  219.8 4.8 %shard_map.278 = (f32[64,128]{1,0:T(8,128)S(1)}, f32[40,64]{1,0:T(8,128)S(1)}, f32[8,128]{1,0:T(8,128)S(1)}) custom-call(s32[6]{0:T(128)S(1)} %stack.63.s, f32[9,256,256]{2,1,0:T(8,128)S(1)} %get-tuple-element.162.spec_grad, f32[9,256,256]{2,1,0:T(8,128)S(1)} %copy-done.24, f32[2048,128]{1,0:T(8,128)S(1)} %get-tuple-element.164.grads, ...), custom_call_target="tpu_custom_call" | custom-call | tf_op jit(solution)/shard_map/pallas_call | solution.py:464
  231.0 12.3 %collective-permute-done.16.w_first = f32[384,128]{1,0:T(8,128)S(1)} collective-permute-done((f32[384,128]{1,0:T(8,128)S(1)}, f32[384,128]{1,0:T(8,128)S(1)}, u32[]{:S(2)}, u32[]{:S(2)}) %collective-permute-start.16) | collective-permute-done | bytes 196640 | tf_op jit(solution)/shard_map/ppermute | solution.py:1370
  245.4 4.4 %collective-permute-done.9.there = f32[128,256]{1,0:T(8,128)S(1)} collective-permute-done((f32[128,256]{1,0:T(8,128)S(1)}, f32[128,256]{1,0:T(8,128)S(1)}, u32[]{:S(2)}, u32[]{:S(2)}) %collective-permute-start.9) | collective-permute-done | bytes 131104 | tf_op jit(solution)/shard_map/ppermute | solution.py:1370
  251.2 2.5 shard_map.282
  (250 shorter events, 77.7 us)
Async XLA Ops:
  7.2 118.7 %all-gather.3.cloned.1.call-start = ((), (), s32[]{:S(2)}) async-start(), calls=%async_computation.1 | async-start | bytes 2228224 | tf_op jit(solution)/shard_map/all_gather | solution.py:1386
  15.5 21.5 %collective-permute-start.4 = (f32[1536,128]{1,0:T(8,128)S(1)}, f32[1536,128]{1,0:T(8,128)}, u32[]{:S(2)}, u32[]{:S(2)}) collective-permute-start(f32[1536,128]{1,0:T(8,128)S(1)} %shard_map.265), channel_id=1, source_target_pairs={{0,1},{1,0},{2,3},{3,2},{4,5},{5,4},{6,7},{7,6},{8,9},{9,8},{10,11... | collective-permute-start | bytes 2359304 | tf_op jit(solution)/shard_map/ppermute | solution.py:1370
  19.1 30.5 %collective-permute-start.2 = (f32[1152,128]{1,0:T(8,128)S(1)}, f32[1152,128]{1,0:T(8,128)}, u32[]{:S(2)}, u32[]{:S(2)}) collective-permute-start(f32[1152,128]{1,0:T(8,128)S(1)} %shard_map.263), channel_id=1, source_target_pairs={{0,1},{1,0},{2,3},{3,2},{4,5},{5,4},{6,7},{7,6},{8,9},{9,8},{10,11... | collective-permute-start | bytes 1769480 | tf_op jit(solution)/shard_map/ppermute | solution.py:1370
  37.0 57.3 %collective-permute-start.5 = (f32[1536,128]{1,0:T(8,128)}, f32[1536,128]{1,0:T(8,128)}, u32[]{:S(2)}, u32[]{:S(2)}) collective-permute-start(f32[1536,128]{1,0:T(8,128)} %collective-permute-done.4.first_part), channel_id=1, source_target_pairs={{0,2},{2,0},{4,6},{6,4},{8,10},{10,8},{12,14},{14,12},{16,18},{18,... | collective-permute-start | bytes 2359304 | tf_op jit(solution)/shard_map/ppermute | solution.py:1371
  37.9 31.3 %collective-permute-start = (f32[200,128]{1,0:T(8,128)S(1)}, f32[200,128]{1,0:T(8,128)S(1)}, u32[]{:S(2)}, u32[]{:S(2)}) collective-permute-start(f32[200,128]{1,0:T(8,128)S(1)} %shard_map.258.own), channel_id=1, source_target_pairs={{0,1},{1,0},{2,3},{3,2},{4,5},{5,4},{6,7},{7,6},{8,9},{9,8},{10,11... | collective-permute-start | bytes 307208 | tf_op jit(solution)/shard_map/ppermute | solution.py:1370
  49.7 42.2 %collective-permute-start.3 = (f32[1152,128]{1,0:T(8,128)}, f32[1152,128]{1,0:T(8,128)}, u32[]{:S(2)}, u32[]{:S(2)}) collective-permute-start(f32[1152,128]{1,0:T(8,128)} %collective-permute-done.2.first_part), channel_id=1, source_target_pairs={{0,2},{2,0},{4,6},{6,4},{8,10},{10,8},{12,14},{14,12},{16,18},{18,... | collective-permute-start | bytes 1769480 | tf_op jit(solution)/shard_map/ppermute | solution.py:1371
  50.3 17.2 %all-to-all-start = ((s32[16,1,128]{2,1,0:T(1,128)}), s32[16,1,128]{2,1,0:T(1,128)S(1)}, u32[]{:S(2)}, u32[]{:S(2)}) async-start(s32[16,1,128]{2,1,0:T(1,128)} %broadcast_in_dim.2), calls=%async_computation | async-start | bytes 16384 | tf_op jit(solution)/shard_map/all_to_all | solution.py:1385
  91.4 6.7 %collective-permute-start.1 = (f32[1056,128]{1,0:T(8,128)S(1)}, f32[1056,128]{1,0:T(8,128)S(1)}, u32[]{:S(2)}, u32[]{:S(2)}) collective-permute-start(f32[1056,128]{1,0:T(8,128)S(1)} %get-tuple-element.118), channel_id=1, source_target_pairs={{0,2},{2,0},{4,6},{6,4},{8,10},{10,8},{12,14},{14,12},{16,18},{18,... | collective-permute-start | bytes 1622024 | tf_op jit(solution)/shard_map/ppermute | solution.py:1371
  111.2 1.9 collective-permute-start.6
  123.2 1.9 collective-permute-start.7
  142.8 2.0 collective-permute-start.10
  151.9 2.0 collective-permute-start.11
  169.7 3.5 %collective-permute-start.18 = (f32[2,1536,128]{2,1,0:T(8,128)S(1)}, f32[2,1536,128]{2,1,0:T(8,128)S(1)}, u32[]{:S(2)}, u32[]{:S(2)}) collective-permute-start(f32[2,1536,128]{2,1,0:T(8,128)S(1)} %get-tuple-element.187), channel_id=1, source_target_pairs={{0,2},{2,0},{4,6},{6,4},{8,10},{10,8},{12,14},{14,12},{16,18},{18,... | collective-permute-start | bytes 4718600 | tf_op jit(solution)/shard_map/ppermute | solution.py:1371
  171.9 3.5 %collective-permute-start.21 = (f32[2,1152,128]{2,1,0:T(8,128)S(1)}, f32[2,1152,128]{2,1,0:T(8,128)S(1)}, u32[]{:S(2)}, u32[]{:S(2)}) collective-permute-start(f32[2,1152,128]{2,1,0:T(8,128)S(1)} %get-tuple-element.203), channel_id=1, source_target_pairs={{0,2},{2,0},{4,6},{6,4},{8,10},{10,8},{12,14},{14,12},{16,18},{18,... | collective-permute-start | bytes 3538952 | tf_op jit(solution)/shard_map/ppermute | solution.py:1371
  173.9 20.4 %collective-permute-start.19 = (f32[1536,128]{1,0:T(8,128)S(1)}, f32[1536,128]{1,0:T(8,128)S(1)}, u32[]{:S(2)}, u32[]{:S(2)}) collective-permute-start(f32[1536,128]{1,0:T(8,128)S(1)} %get-tuple-element.189), channel_id=1, source_target_pairs={{0,1},{1,0},{2,3},{3,2},{4,5},{5,4},{6,7},{7,6},{8,9},{9,8},{10,11... | collective-permute-start | bytes 2359304 | tf_op jit(solution)/shard_map/ppermute | solution.py:1370
  176.2 30.0 %collective-permute-start.22 = (f32[1152,128]{1,0:T(8,128)S(1)}, f32[1152,128]{1,0:T(8,128)S(1)}, u32[]{:S(2)}, u32[]{:S(2)}) collective-permute-start(f32[1152,128]{1,0:T(8,128)S(1)} %get-tuple-element.205), channel_id=1, source_target_pairs={{0,1},{1,0},{2,3},{3,2},{4,5},{5,4},{6,7},{7,6},{8,9},{9,8},{10,11... | collective-permute-start | bytes 1769480 | tf_op jit(solution)/shard_map/ppermute | solution.py:1370
  177.1 34.7 %collective-permute-start.12 = (f32[1024,128]{1,0:T(8,128)S(1)}, f32[1024,128]{1,0:T(8,128)S(1)}, u32[]{:S(2)}, u32[]{:S(2)}) collective-permute-start(f32[1024,128]{1,0:T(8,128)S(1)} %get-tuple-element.152), channel_id=1, source_target_pairs={{0,2},{2,0},{4,6},{6,4},{8,10},{10,8},{12,14},{14,12},{16,18},{18,... | collective-permute-start | bytes 1572872 | tf_op jit(solution)/shard_map/ppermute | solution.py:1371
  195.0 60.6 %collective-permute-start.20 = (f32[1536,128]{1,0:T(8,128)S(1)}, f32[1536,128]{1,0:T(8,128)S(1)}, u32[]{:S(2)}, u32[]{:S(2)}) collective-permute-start(f32[1536,128]{1,0:T(8,128)S(1)} %shard_map.285.kept), channel_id=1, source_target_pairs={{0,2},{2,0},{4,6},{6,4},{8,10},{10,8},{12,14},{14,12},{16,18},{18,... | collective-permute-start | bytes 2359304 | tf_op jit(solution)/shard_map/ppermute | solution.py:1371
  206.8 48.1 %collective-permute-start.23 = (f32[1152,128]{1,0:T(8,128)S(1)}, f32[1152,128]{1,0:T(8,128)S(1)}, u32[]{:S(2)}, u32[]{:S(2)}) collective-permute-start(f32[1152,128]{1,0:T(8,128)S(1)} %shard_map.289.kept), channel_id=1, source_target_pairs={{0,2},{2,0},{4,6},{6,4},{8,10},{10,8},{12,14},{14,12},{16,18},{18,... | collective-permute-start | bytes 1769480 | tf_op jit(solution)/shard_map/ppermute | solution.py:1371
  227.6 23.5 %collective-permute-start.15 = (f32[392,256]{1,0:T(8,128)S(1)}, f32[392,256]{1,0:T(8,128)S(1)}, u32[]{:S(2)}, u32[]{:S(2)}) collective-permute-start(f32[392,256]{1,0:T(8,128)S(1)} %shard_map.280.here), channel_id=1, source_target_pairs={{0,1},{1,0},{2,3},{3,2},{4,5},{5,4},{6,7},{7,6},{8,9},{9,8},{10,11... | collective-permute-start | bytes 1204232 | tf_op jit(solution)/shard_map/ppermute | solution.py:1370
  229.7 13.6 %collective-permute-start.16 = (f32[384,128]{1,0:T(8,128)S(1)}, f32[384,128]{1,0:T(8,128)S(1)}, u32[]{:S(2)}, u32[]{:S(2)}) collective-permute-start(f32[384,128]{1,0:T(8,128)S(1)} %shard_map.281), channel_id=1, source_target_pairs={{0,1},{1,0},{2,3},{3,2},{4,5},{5,4},{6,7},{7,6},{8,9},{9,8},{10,11... | collective-permute-start | bytes 589832 | tf_op jit(solution)/shard_map/ppermute | solution.py:1370
  230.9 12.4 %collective-permute-start.8 = (f32[128,256]{1,0:T(8,128)S(1)}, f32[128,256]{1,0:T(8,128)S(1)}, u32[]{:S(2)}, u32[]{:S(2)}) collective-permute-start(f32[128,256]{1,0:T(8,128)S(1)} %get-tuple-element.136), channel_id=1, source_target_pairs={{0,2},{2,0},{4,6},{6,4},{8,10},{10,8},{12,14},{14,12},{16,18},{18,... | collective-permute-start | bytes 393224 | tf_op jit(solution)/shard_map/ppermute | solution.py:1371
  243.3 7.8 %collective-permute-start.17 = (f32[384,128]{1,0:T(8,128)S(1)}, f32[384,128]{1,0:T(8,128)S(1)}, u32[]{:S(2)}, u32[]{:S(2)}) collective-permute-start(f32[384,128]{1,0:T(8,128)S(1)} %collective-permute-done.16.w_first), channel_id=1, source_target_pairs={{0,2},{2,0},{4,6},{6,4},{8,10},{10,8},{12,14},{14,12},{16,18},{18,... | collective-permute-start | bytes 589832 | tf_op jit(solution)/shard_map/ppermute | solution.py:1371
  243.9 6.0 %collective-permute-start.9 = (f32[128,256]{1,0:T(8,128)S(1)}, f32[128,256]{1,0:T(8,128)S(1)}, u32[]{:S(2)}, u32[]{:S(2)}) collective-permute-start(f32[128,256]{1,0:T(8,128)S(1)} %shard_map.271.here), channel_id=1, source_target_pairs={{0,1},{1,0},{2,3},{3,2},{4,5},{5,4},{6,7},{7,6},{8,9},{9,8},{10,11... | collective-permute-start | bytes 393224 | tf_op jit(solution)/shard_map/ppermute | solution.py:1370
  (89 other events, 1009.3 us)
Sparse Core Ops, SparseCore 0:
  10.8 43.9 all-gather.2

commit v2 on v1

--- a/solution.py
+++ b/solution.py
@@ -452,23 +452,61 @@
 BLOCK = 256
 KINDS = 9
 VMEM_LIMIT = 20 * 2**20
+FLOPS = 10**10
 f32 = jnp.float32
 bf16 = jnp.bfloat16
 
 
-def run(body, outs, scalars, *arrays, scratch=()):
+class Numbers:
+    def __init__(self, table):
+        self.table = table
+
+    def __getitem__(self, row):
+        return self.table[row, 0]
+
+
+CORE, GROUP, LIVE, WHICH, SPOT, HOLDER, BIT1, BIT2, BIT3 = range(9)
+NUMBER_ROWS = 16
+
+
+def number_table(count):
+    rows = np.zeros((count, 2, NUMBER_ROWS, 128), np.int32)
+    half = count // 2
+    for rank in range(count):
+        for group in range(2):
+            core = rank % 2
+            values = (core, group, 0, group ^ core, rank % half, int(rank // half == core), rank // 2 % 2, rank // 4 % 2, rank // 8 % 2)
+            for row, value in enumerate(values):
+                rows[rank, group, row] = value
+    return rows
+
+
+def numbers_kernel(s, live, out):
+    out[...] = s.table[...]
+    out[LIVE : LIVE + 1, :] = jnp.broadcast_to(jnp.where(s[GROUP] == 0, live[0:1, 0:1], live[0:1, 1:2]), (1, 128))
+
+
+def run(body, outs, scalars, *arrays, scratch=(), after=(), hbm=()):
     vmem = pl.BlockSpec(memory_space=pltpu.VMEM)
-    smem = pl.BlockSpec(memory_space=pltpu.SMEM)
+    far = pl.BlockSpec(memory_space=pl.ANY)
     single = not isinstance(outs, (list, tuple))
     shapes = [outs] if single else list(outs)
+    used, waits = 1 + len(arrays), len(after)
+
+    def call(table, *refs):
+        body(Numbers(table), *refs[: used - 1], *refs[used - 1 + waits :])
+
+    inner = getattr(body, "func", body)
     result = pl.pallas_call(
-        body,
+        call,
         out_shape=shapes,
-        in_specs=[smem] + [vmem] * len(arrays),
+        in_specs=[vmem] + [far if i in hbm else vmem for i in range(len(arrays))] + [far] * waits,
         out_specs=[vmem] * len(shapes),
         scratch_shapes=list(scratch),
         compiler_params=pltpu.CompilerParams(vmem_limit_bytes=VMEM_LIMIT),
-    )(scalars, *arrays)
+        cost_estimate=pl.CostEstimate(flops=FLOPS, bytes_accessed=1, transcendentals=0),
+        name=inner.__name__,
+    )(scalars, *arrays, *after)
     return result[0] if single else result
 
 
@@ -690,7 +728,7 @@
 
 
 def table_kernel(s, own, peer, embed, mine_out, other_out, conv_table, gate_table):
-    first = s[0] == 0
+    first = s[CORE] == 0
     mine = jnp.where(first, own[...], peer[...])
     other = jnp.where(first, peer[...], own[...])
     mine_out[...] = mine
@@ -720,14 +758,14 @@
 
 
 def onehot_kernel(s, ids, out, turned, work):
-    live = s[2]
-    count, width = ids.shape
+    live = s[LIVE]
+    count, _, width = ids.shape
     work[0:HALO, :] = jnp.zeros((HALO, 128), f32)
     work[HALO + count * width : 2 * HALO + count * width, :] = jnp.zeros((HALO, 128), f32)
     vocab = lax.broadcasted_iota(jnp.int32, (128, width), 0) % 16
     place = lax.broadcasted_iota(jnp.int32, (128, width), 1)
     for i in range(count):
-        token = jnp.broadcast_to(ids[i : i + 1, :], (128, width))
+        token = jnp.broadcast_to(ids[i, 0:1, :], (128, width))
         hit = (token == vocab) & (place + i * width < live)
         work[HALO + width * i : HALO + width * (i + 1), :] = jnp.where(hit, 1.0, 0.0).T
     lane = lax.broadcasted_iota(jnp.int32, (width, 128), 1) % 48 // 16
@@ -746,6 +784,20 @@
     out[HALO + count * width : 2 * HALO + count * width, :] = jnp.zeros((HALO, 128), bf16)
 
 
+def sine_and_cosine(angle):
+    turns = jnp.round(angle * (2.0 / math.pi))
+    x = ((angle - turns * 1.5703125) - turns * 4.837512969970703125e-4) - turns * 7.549789948768648e-8
+    z = x * x
+    sin = ((-1.9515295891e-4 * z + 8.3321608736e-3) * z - 1.6666654611e-1) * z * x + x
+    cos = ((2.443315711809948e-5 * z - 1.388731625493765e-3) * z + 4.166664568298827e-2) * z * z - 0.5 * z + 1.0
+    quarter = turns.astype(jnp.int32) & 3
+    odd = (quarter & 1) == 1
+    first, second = jnp.where(odd, cos, sin), jnp.where(odd, sin, cos)
+    first = jnp.where(quarter >= 2, -first, first)
+    second = jnp.where((quarter == 1) | (quarter == 2), -second, second)
+    return first, second
+
+
 def sine_kernel(s, feats, firsts, sine, cosine, turned):
     both = jnp.concatenate([firsts[0], firsts[1]], axis=1)
     count = feats.shape[0] // 256
@@ -753,9 +805,8 @@
     def chunk(i, carry):
         rows = at(256 * i, 256)
         angle = jnp.dot(feats[rows, :], both, precision=precise, preferred_element_type=f32)
-        act = jnp.sin(angle)
+        act, cosine[rows, :] = sine_and_cosine(angle)
         sine[rows, :] = act
-        cosine[rows, :] = jnp.cos(angle)
         turned[:, at(256 * i, 256, 256)] = act.T.astype(bf16)
         return carry
 
@@ -769,7 +820,7 @@
 
 def filter_kernel(s, sine, mine, rates, dft, twiddle, filt0, filt1, freq0, freq1, stage, work):
     length = sine.shape[0]
-    rate = rates[s[3]]
+    rate = rates[s[WHICH]]
     zero = jnp.zeros((64, 128), f32)
     left = jnp.concatenate([mine[PACK_SECOND : PACK_SECOND + 64], zero], axis=0)
     right = jnp.concatenate([zero, mine[PACK_SECOND + 64 : PACK_SECOND + 128]], axis=0)
@@ -801,7 +852,7 @@
 def hand_out(s, line, keep, send):
     half = (line.shape[0] - 2 * HALO) // 2
     span = half + 2 * HALO
-    k = s[0]
+    k = s[CORE]
     line[0:HALO, :] = jnp.zeros((HALO, 128), f32)
     line[HALO + 2 * half :, :] = jnp.zeros((HALO, 128), f32)
     keep[...] = line[at(half * k, span), :]
@@ -823,8 +874,8 @@
 
 def join_rows(s, whole, kept, received):
     half = kept.shape[0]
-    whole[at(half * s[0], half), :] = kept[...]
-    whole[at(half * (1 - s[0]), half), :] = received[...]
+    whole[at(half * s[CORE], half), :] = kept[...]
+    whole[at(half * (1 - s[CORE]), half), :] = received[...]
 
 
 def conv_second_kernel(s, kept, received, mine, freq_filt, dft, twiddle, keep, send, spec, product, stage, work, line):
@@ -855,7 +906,7 @@
 ):
     span = mid_out.shape[0]
     half = span - 2 * HALO
-    k = s[0]
+    k = s[CORE]
     taps = [
         jnp.concatenate([pack[PACK_SHORT + 9 + 3 * t + g : PACK_SHORT + 10 + 3 * t + g, :] for g in range(3) for pack in (mine, other)], axis=1)
         for t in range(3)
@@ -894,17 +945,17 @@
 
 
 def turn_back_kernel(
-    s, conv_mine, conv_other, gates, stream, cot, gain, w_out, w_up, w_down,
+    s, conv_mine, conv_other, gates, stream, cot_near, cot_far, cot_rim, gain, w_out, w_up, w_down,
     keep, send, grad_x0, grad_mid, block_out, hidden_out, low_out, normed_out, pre_out, gated_out, mid_low_out, gain_out,
     cot_rows, conv_grads,
 ):
     span = stream.shape[0]
     half = span - 2 * HALO
-    k = s[0]
-    live = s[2]
+    k = s[CORE]
+    live = s[LIVE]
     cot_rows[0:HALO, :] = jnp.zeros((HALO, 256), f32)
-    cot_rows[HALO : HALO + half, :] = cot[at(half * k, half), :]
-    cot_rows[HALO + half :, :] = jnp.where(k == 0, cot[half : half + HALO, :], 0.0)
+    cot_rows[HALO : HALO + half, :] = jnp.where(s[HOLDER] == 1, cot_near[...], cot_far[...]).reshape(half, 256)
+    cot_rows[HALO + half :, :] = jnp.where(k == 0, cot_rim[...], 0.0)
     gain_out[...] = jnp.zeros_like(gain_out)
 
     def chunk(i, carry):
@@ -961,33 +1012,14 @@
     hand_out(s, line, keep, send)
 
 
-def conv_back_first_kernel(
-    s, kept, received, mine, freq_filt, dft, twiddle, onehot, turned, conv_table, spec, grads, by_token, stage, work, line
-):
-    length = grads.shape[0]
+def grad_freq_kernel(s, kept, received, dft, twiddle, spec, grads, stage):
     join_rows(s, grads, kept, received)
-    skip_row = mine[PACK_SKIP : PACK_SKIP + 1, :]
-    load = lambda p, row: grads[pl.ds(BLOCK * p + row, 16), :]
-    to_freq(load, dft, twiddle, stage, spec)
-    times(freq_filt, spec, stage, True)
-
-    def store(p, row, value):
-        line[pl.ds(BLOCK * p + row, 16), :] = value + skip_row * load(p, row)
-
-    from_freq(dft, twiddle, stage, work, store)
-    by_token[...] = jnp.zeros_like(by_token)
-    width = turned.shape[2]
-    for i in range(length // width):
-        rows = slice(width * i, width * (i + 1))
-        pair = mm(onehot[HALO + width * i : HALO + width * (i + 1), :], conv_table[...])
-        back = line[rows, :]
-        gate_grads = jnp.concatenate([back * pair[:, 128:256], back * pair[:, 0:128]], axis=1).astype(bf16)
-        by_token[...] += mm(turned[i], gate_grads)[0:48, :]
-
-
-def filter_back_kernel(
+    to_freq(lambda p, row: grads[pl.ds(BLOCK * p + row, 16), :], dft, twiddle, stage, spec)
+
+
+def filter_back(
     level, s, spec_grad, spec_in, grads, product, filt, cosine, sine_turned, mine, rates, feats_turned, dft, twiddle,
-    second_out, first_out, skip_out, stage, work, line, inner,
+    second_out, first_out, skip_out, stage, work, line,
 ):
     length = filt.shape[0]
     times(spec_in, spec_grad, stage, True)
@@ -996,9 +1028,9 @@
         line[pl.ds(BLOCK * p + row, 16), :] = value
 
     from_freq(dft, twiddle, stage, work, store)
-    rate = rates[s[3]]
+    rate = rates[s[WHICH]]
     second = mine[PACK_SECOND + 64 * level : PACK_SECOND + 64 * level + 64, :].astype(bf16)
-    weight = jnp.where(s[1] == 0, 0.5 * length, 0.0)
+    weight = jnp.where(s[GROUP] == 0, 0.5 * length, 0.0)
     skip_out[...] = jnp.zeros_like(skip_out)
     second_out[...] = jnp.zeros_like(second_out)
     first_out[...] = jnp.zeros_like(first_out)
@@ -1010,6 +1042,36 @@
         second_out[...] += mm(sine_turned[64 * level : 64 * level + 64, rows], shaped)
         inner = (mm_nt(shaped, second) * cosine[rows, 64 * level : 64 * level + 64]).astype(bf16)
         first_out[...] += mm(feats_turned[:, rows], inner)
+
+
+def filter_back_kernel(s, *refs):
+    filter_back(1, s, *refs)
+
+
+def token_back_kernel(
+    s, spec_grad, spec_in, grads, product, filt, cosine, sine_turned, mine, rates, feats_turned, dft, twiddle,
+    freq_filt, onehot, turned, conv_table, second_out, first_out, skip_out, by_token, stage, work, line,
+):
+    length = grads.shape[0]
+    skip_row = mine[PACK_SKIP : PACK_SKIP + 1, :]
+    times(freq_filt, spec_grad, stage, True)
+
+    def store(p, row, value):
+        line[pl.ds(BLOCK * p + row, 16), :] = value + skip_row * grads[pl.ds(BLOCK * p + row, 16), :]
+
+    from_freq(dft, twiddle, stage, work, store)
+    by_token[...] = jnp.zeros_like(by_token)
+    width = turned.shape[2]
+    for i in range(length // width):
+        rows = slice(width * i, width * (i + 1))
+        pair = mm(onehot[HALO + width * i : HALO + width * (i + 1), :], conv_table[...])
+        back = line[rows, :]
+        gate_grads = jnp.concatenate([back * pair[:, 128:256], back * pair[:, 0:128]], axis=1).astype(bf16)
+        by_token[...] += mm(turned[i], gate_grads)[0:48, :]
+    filter_back(
+        0, s, spec_grad, spec_in, grads, product, filt, cosine, sine_turned, mine, rates, feats_turned, dft, twiddle,
+        second_out, first_out, skip_out, stage, work, line,
+    )
 
 
 def back_gates_kernel(
@@ -1062,7 +1124,7 @@
     keep, send, hidden_out, low_out, normed_out, pre_out, gated_out, mid_low_out, by_token, gain_out,
 ):
     half = grad_stream.shape[0]
-    k = s[0]
+    k = s[CORE]
     by_token[...] = jnp.zeros_like(by_token)
     gain_out[...] = jnp.zeros_like(gain_out)
 
@@ -1105,32 +1167,55 @@
 R_OUT, R_UP, R_DOWN, R_IN = 128, 512, 512, 384
 
 
-def send_weights_kernel(level, with_in, s, w_out, w_up, w_down, w_in, out):
-    k = s[0]
-    first = k == 0
+def send_weights_kernel(s, w_out, w_up, w_down, w_in, part0, part1, raw_out, raw_up, raw_down, raw_in, done):
+    copies = [
+        pltpu.make_async_copy(far, near, done.at[i])
+        for i, (far, near) in enumerate(((w_out, raw_out), (w_up, raw_up), (w_down, raw_down), (w_in, raw_in)))
+    ]
+    for copy in copies:
+        copy.start()
+    for copy in copies:
+        copy.wait()
+    first = s[CORE] == 0
     pick = lambda a, b: jnp.where(first, a.astype(f32), b.astype(f32))
-    out[0:128, :] = pick(w_out[level, :, 0:128], w_out[level, :, 128:256])
-    for j in range(2):
-        lanes = slice(128 * j, 128 * j + 128)
-        out[128 + 256 * j : 384 + 256 * j, :] = pick(
-            w_up[level, :, 128 * j : 128 * j + 128], w_up[level, :, 256 + 128 * j : 384 + 128 * j]
-        )
-        out[640 + 256 * j : 896 + 256 * j, :] = pick(w_down[level, 0:256, lanes], w_down[level, 256:512, lanes])
-    if with_in:
+    for level, out in ((0, part0), (1, part1)):
+        out[0:128, :] = pick(raw_out[level, :, 0:128], raw_out[level, :, 128:256])
+        for j in range(2):
+            lanes = slice(128 * j, 128 * j + 128)
+            out[128 + 256 * j : 384 + 256 * j, :] = pick(
+                raw_up[level, :, 128 * j : 128 * j + 128], raw_up[level, :, 256 + 128 * j : 384 + 128 * j]
+            )
+            out[640 + 256 * j : 896 + 256 * j, :] = pick(raw_down[level, 0:256, lanes], raw_down[level, 256:512, lanes])
         for g in range(3):
-            out[1152 + 128 * g : 1280 + 128 * g, :] = pick(w_in[level, g, 0:128, :], w_in[level, g, 128:256, :])
-
-
-def join_weights_kernel(level, with_in, s, w_out, w_up, w_down, w_in, first_part, second_part, out_full, up_full, down_full, *in_full):
-    k = s[0]
-    first = k == 0
+            out[1152 + 128 * g : 1280 + 128 * g, :] = pick(raw_in[1 - level, g, 0:128, :], raw_in[1 - level, g, 128:256, :])
+
+
+def ids_kernel(s, ids, out):
+    row = jnp.where(s[GROUP] == 0, ids[0:1, :], ids[1:2, :])
+    out[0] = jnp.broadcast_to(row, out.shape[1:])
+
+
+def pick_kernel(s, values, out):
+    out[0] = values[s[GROUP]]
+
+
+def rim_kernel(s, near, far_rows, out):
+    out[...] = jnp.where(s[HOLDER] == 1, near[0, 0:HALO, :], far_rows[0, 0:HALO, :])
+
+
+def relay_kernel(s, value, out):
+    out[...] = value[...]
+
+
+def join_weights_kernel(level, s, w_out, w_up, w_down, w_in, first_part, second_part, out_full, up_full, down_full, *in_full):
+    first = s[CORE] == 0
     low = lambda ref, a, b: ref[a:b, :].astype(bf16)
     pick = lambda a, b: jnp.where(first, a, b)
     mine_out = w_out[level]
     a, b = first_part[0:128, :], second_part[0:128, :]
-    peer_out = jnp.concatenate([pick(a, b), pick(b, a)], axis=1).astype(bf16)
-    out_full[0:128, :] = pick(mine_out.astype(f32), peer_out.astype(f32)).astype(bf16)
-    out_full[128:256, :] = pick(peer_out.astype(f32), mine_out.astype(f32)).astype(bf16)
+    peer_out = jnp.concatenate([pick(a, b), pick(b, a)], axis=1)
+    out_full[0:128, :] = pick(mine_out.astype(f32), peer_out).astype(bf16)
+    out_full[128:256, :] = pick(peer_out, mine_out.astype(f32)).astype(bf16)
     up_a, up_b = w_up[level, :, 0:256].astype(f32), w_up[level, :, 256:512].astype(f32)
     up_full[:, 0:256] = pick(up_a, up_b).astype(bf16)
     up_full[:, 256:512] = pick(up_b, up_a).astype(bf16)
@@ -1141,55 +1226,47 @@
         for j in range(2):
             up_full[:, 512 + 256 * n + 128 * j : 640 + 256 * n + 128 * j] = low(part, 128 + 256 * j, 384 + 256 * j)
             down_full[512 + 256 * n : 768 + 256 * n, 128 * j : 128 * j + 128] = low(part, 640 + 256 * j, 896 + 256 * j)
-    if with_in:
+    if in_full:
         (full,) = in_full
         for g in range(3):
-            own = w_in[level, g].astype(f32)
+            own = w_in[1 - level, g].astype(f32)
             a, b = first_part[1152 + 128 * g : 1280 + 128 * g, :], second_part[1152 + 128 * g : 1280 + 128 * g, :]
             peer = jnp.concatenate([pick(a, b), pick(b, a)], axis=0)
             full[:, 256 * g : 256 * g + 128] = pick(own, peer).astype(bf16)
             full[:, 256 * g + 128 : 256 * g + 256] = pick(peer, own).astype(bf16)
 
 
-def put_wide_grads(s, keep, send, row, gated, mid_low, normed, grad_pre, hidden, grad_low):
-    k = s[0]
+def wide_grads_kernel(pad, s, gated, mid_low, normed, grad_pre, hidden, grad_low, keep, send):
+    k = s[CORE]
     first = k == 0
-    out = mm_tn(gated, mid_low)
+    stop = gated.shape[0] - pad
+    own = lambda ref: ref[pad:stop, :]
+    out = mm_tn(own(gated), own(mid_low))
     for m in range(2):
         a, b = out[128 * m : 128 * m + 128, 0:128], out[128 * m : 128 * m + 128, 128:256]
         half = m + k - 2 * m * k
-        keep[half, row : row + 128, :] = jnp.where(first, a, b)
-        send[half, row : row + 128, :] = jnp.where(first, b, a)
+        keep[half, 0:128, :] = jnp.where(first, a, b)
+        send[half, 0:128, :] = jnp.where(first, b, a)
     for j in range(4):
         target = (keep, send)[j % 2]
-        up = mm_tn(normed, grad_pre[:, 256 * j : 256 * j + 256])
-        down = mm_tn(hidden[:, 256 * j : 256 * j + 256], grad_low)
+        up = mm_tn(own(normed), grad_pre[pad:stop, 256 * j : 256 * j + 256])
+        down = mm_tn(hidden[pad:stop, 256 * j : 256 * j + 256], own(grad_low))
         for n in range(2):
             lanes = slice(128 * n, 128 * n + 128)
-            target[j // 2, row + 128 + 256 * n : row + 384 + 256 * n, :] = up[:, lanes]
-            target[j // 2, row + 640 + 256 * n : row + 896 + 256 * n, :] = down[:, lanes]
-
-
-def wide_grads_kernel(pad, s, gated, mid_low, normed, grad_pre, hidden, grad_low, keep, send):
-    stop = gated.shape[0] - pad
-    own = lambda ref: ref[pad:stop, :]
-    put_wide_grads(s, keep, send, 0, own(gated), own(mid_low), own(normed), own(grad_pre), own(hidden), own(grad_low))
-
-
-def wide_and_in_grads_kernel(s, gated, mid_low, normed, grad_pre, hidden, grad_low, normed_in, mixed_low, keep, send):
-    k = s[0]
+            target[j // 2, 128 + 256 * n : 384 + 256 * n, :] = up[:, lanes]
+            target[j // 2, 640 + 256 * n : 896 + 256 * n, :] = down[:, lanes]
+
+
+def in_grads_kernel(s, normed_in, mixed_low, keep, send):
+    k = s[CORE]
     first = k == 0
-    put_wide_grads(
-        s, keep, send, 0, gated[...], mid_low[...], normed[...], grad_pre[...], hidden[...], grad_low[...]
-    )
     for g in range(3):
         both = mm_tn(normed_in[...], mixed_low[:, 256 * g : 256 * g + 256])
         for m in range(2):
             block = both[:, 128 * m : 128 * m + 128]
             half = m + k - 2 * m * k
-            row = 1152 + 128 * g
-            keep[half, row : row + 128, :] = jnp.where(first, block[0:128], block[128:256])
-            send[half, row : row + 128, :] = jnp.where(first, block[128:256], block[0:128])
+            keep[half, 128 * g : 128 * g + 128, :] = jnp.where(first, block[0:128], block[128:256])
+            send[half, 128 * g : 128 * g + 128, :] = jnp.where(first, block[128:256], block[0:128])
 
 
 def add_kernel(s, kept, received, own_out, peer_out):
@@ -1201,104 +1278,128 @@
     out[...] = kept[...] + received[...]
 
 
-def spread_grads_kernel(with_in, s, kept, received, out, up, down, *w_in):
-    first = s[0] == 0
-    a, b = kept, received
+def spread_wide_kernel(s, kept1, received1, kept0, received0, out, up, down):
+    first = s[CORE] == 0
     pick = lambda x, y: jnp.where(first, x, y)
-
-    def both(row, rows):
-        x, y = a[row : row + rows, :], b[row : row + rows, :]
-        return pick(x, y), pick(y, x)
-
-    x, y = both(0, 128)
-    out[:, 0:128] = x
-    out[:, 128:256] = y
-    for j in range(2):
-        lanes = slice(128 * j, 128 * j + 128)
-        x, y = both(128 + 256 * j, 256)
-        up[:, 128 * j : 128 * j + 128] = x
-        up[:, 256 + 128 * j : 384 + 128 * j] = y
-        x, y = both(640 + 256 * j, 256)
-        down[0:256, lanes] = x
-        down[256:512, lanes] = y
-    if with_in:
-        for g in range(3):
-            x, y = both(1152 + 128 * g, 128)
-            w_in[0][g, 0:128, :] = x
-            w_in[0][g, 128:256, :] = y
-
-
-F_GAIN1, F_GAIN0, F_EMBED, F_FIRST, F_SKIPPAD, F_SHORT, F_TOKEN = 0, 8, 16, 32, 72, 80, 112
-F_ROWS = 160
-C_SECOND1, C_SECOND0, C_SKIP, C_TOKEN = 0, 64, 128, 136
-C_ROWS = 232
-
-
-def small_kernel(
-    s, gain_mid1, gain_in1, gain_mid0, by_token0, by_token12, first1, first0, short1, second1, second0, skip1, skip0, flat, mine
-):
-    k = s[0]
+    for level, a, b in ((0, kept0, received0), (1, kept1, received1)):
+
+        def both(row, rows):
+            x, y = a[row : row + rows, :], b[row : row + rows, :]
+            return pick(x, y), pick(y, x)
+
+        x, y = both(0, 128)
+        out[level, :, 0:128] = x
+        out[level, :, 128:256] = y
+        for j in range(2):
+            lanes = slice(128 * j, 128 * j + 128)
+            x, y = both(128 + 256 * j, 256)
+            up[level, :, 128 * j : 128 * j + 128] = x
+            up[level, :, 256 + 128 * j : 384 + 128 * j] = y
+            x, y = both(640 + 256 * j, 256)
+            down[level, 0:256, lanes] = x
+            down[level, 256:512, lanes] = y
+
+
+def spread_in_kernel(s, in_first, kept, received, out):
+    first = s[CORE] == 0
+    for g in range(3):
+        x, y = kept[128 * g : 128 * g + 128, :], received[128 * g : 128 * g + 128, :]
+        out[0, g] = in_first[g]
+        out[1, g, 0:128, :] = jnp.where(first, x, y)
+        out[1, g, 128:256, :] = jnp.where(first, y, x)
+
+
+def pair_kernel(bit, s, own, received, out):
+    spot = s[(CORE, BIT1, BIT2, BIT3)[bit]]
+    size = own.shape[0]
+    if bit == 0:
+        for j in range(size):
+            out[2 * j + spot] = own[j]
+            out[2 * j + 1 - spot] = received[j]
+    else:
+        out[pl.ds(size * spot, size)] = own[...]
+        out[pl.ds(size * (1 - spot), size)] = received[...]
+
+
+E_GAIN1, E_GAIN0, E_EMBED, E_FIRST, E_SHORT, E_TOKEN, E_ROWS = 0, 8, 16, 32, 72, 88, 136
+EM_SECOND, EM_SKIP, EM_ROWS = 0, 64, 72
+L_TOKEN, L_SECOND, L_SKIP, L_ROWS = 0, 96, 160, 168
+FIRST_ROWS = 40
+
+
+def early_kernel(s, gain_mid1, gain_in1, gain_mid0, by_token0, first1, short1, second1, skip1, flat, mine):
+    k = s[CORE]
     flat[...] = jnp.zeros_like(flat)
-    flat[F_GAIN1 : F_GAIN1 + 8, :] = gain_mid1[...]
-    flat[F_GAIN0 : F_GAIN0 + 8, :] = gain_mid0[...]
-    flat[F_GAIN1 + 1 : F_GAIN1 + 2, :] = gain_in1[0:1, :]
-    flat[F_EMBED : F_EMBED + 16, :] = by_token0[0:16, 256:512] + by_token0[0:16, 512:768]
-    flat[F_FIRST : F_FIRST + 40, 0:64] = first0[...]
-    flat[F_FIRST : F_FIRST + 40, 128:192] = first1[...]
+    flat[E_GAIN1 : E_GAIN1 + 8, :] = gain_mid1[...]
+    flat[E_GAIN0 : E_GAIN0 + 8, :] = gain_mid0[...]
+    flat[E_GAIN1 + 1 : E_GAIN1 + 2, :] = gain_in1[0:1, :]
+    flat[E_EMBED : E_EMBED + 16, :] = by_token0[0:16, 256:512] + by_token0[0:16, 512:768]
+    flat[E_FIRST : E_FIRST + FIRST_ROWS, 0:64] = first1[...]
     swap = lambda v: jnp.where(k == 0, v, jnp.concatenate([v[:, 128:256], v[:, 0:128]], axis=1))
     for t in range(3):
         total = jnp.sum(short1[t], axis=0, keepdims=True)
         for g in range(3):
-            flat[F_SHORT + 3 * t + g : F_SHORT + 3 * t + g + 1, :] = swap(total[:, 256 * g : 256 * g + 256])
-    flat[F_TOKEN : F_TOKEN + 48, :] = swap(by_token0[:, 0:256])
-    mine[C_SECOND1 : C_SECOND1 + 64, :] = second1[...]
-    mine[C_SECOND0 : C_SECOND0 + 64, :] = second0[...]
-    mine[C_SKIP : C_SKIP + 8, :] = jnp.zeros((8, 128), f32)
-    mine[C_SKIP : C_SKIP + 1, :] = jnp.sum(skip0[...], axis=0, keepdims=True)
-    mine[C_SKIP + 1 : C_SKIP + 2, :] = jnp.sum(skip1[...], axis=0, keepdims=True)
-    mine[C_TOKEN : C_TOKEN + 48, :] = by_token12[:, 0:128]
-    mine[C_TOKEN + 48 : C_TOKEN + 96, :] = by_token12[:, 128:256]
+            flat[E_SHORT + 3 * t + g : E_SHORT + 3 * t + g + 1, :] = swap(total[:, 256 * g : 256 * g + 256])
+    flat[E_TOKEN : E_TOKEN + 48, :] = swap(by_token0[:, 0:256])
+    mine[EM_SECOND : EM_SECOND + 64, :] = second1[...]
+    mine[EM_SKIP : EM_SKIP + 8, :] = jnp.broadcast_to(jnp.sum(skip1[...], axis=0, keepdims=True), (8, 128))
+
+
+def late_kernel(s, by_token12, second0, skip0, first0, mine, first_out):
+    mine[L_TOKEN : L_TOKEN + 48, :] = by_token12[:, 0:128]
+    mine[L_TOKEN + 48 : L_TOKEN + 96, :] = by_token12[:, 128:256]
+    mine[L_SECOND : L_SECOND + 64, :] = second0[...]
+    mine[L_SKIP : L_SKIP + 8, :] = jnp.broadcast_to(jnp.sum(skip0[...], axis=0, keepdims=True), (8, 128))
+    first_out[:, 0:64] = first0[...]
+    first_out[:, 64:128] = jnp.zeros((FIRST_ROWS, 64), f32)
 
 
 def chip_kernel(s, flat, flat_in, mine, mine_in, out):
-    first = s[0] == 0
+    first = s[CORE] == 0
+    rows = flat.shape[0]
     total = flat[...] + flat_in[...]
-    out[0:F_ROWS, :] = total
-    out[F_ROWS : F_ROWS + C_ROWS, 0:128] = jnp.where(first, mine[...], mine_in[...])
-    out[F_ROWS : F_ROWS + C_ROWS, 128:256] = jnp.where(first, mine_in[...], mine[...])
+    out[0:rows, 0 : total.shape[1]] = total
+    if total.shape[1] == 128:
+        out[0:rows, 128:256] = jnp.zeros((rows, 128), f32)
+    out[rows:, 0:128] = jnp.where(first, mine[...], mine_in[...])
+    out[rows:, 128:256] = jnp.where(first, mine_in[...], mine[...])
 
 
 def last_kernel(
-    s, here, there, embed, gain, own, peer, w_own, w_first, w_second,
+    s, early, early_in, late, late_in, embed, gain, own, peer, w_own, w_first, w_second,
     embed_out, gain_out, in_out, short_out, first_out, second_out, skip_out,
 ):
-    first = s[0] == 0
-    pick = lambda x, y: jnp.where(first, x, y)
-
-    def plain(row, rows):
-        return here[row : row + rows, :] + there[row : row + rows, :]
-
-    def halves(row, rows):
+    pick = lambda x, y: jnp.where(s[CORE] == 0, x, y)
+
+    def plain(pair, row, rows):
+        return pair[0][row : row + rows, :] + pair[1][row : row + rows, :]
+
+    def halves(pair, row, rows):
+        here, there = pair
         left = here[row : row + rows, 0:128] + there[row : row + rows, 128:256]
         right = here[row : row + rows, 128:256] + there[row : row + rows, 0:128]
         return left, right
 
-    gains1 = plain(F_GAIN1, 8)
-    gains0 = plain(F_GAIN0, 8)
+    early, late = (early, early_in), (late, late_in)
+    gains1 = plain(early, E_GAIN1, 8)
+    gains0 = plain(early, E_GAIN0, 8)
     gain_out[1, 0:1, :] = gains1[1:2, :]
     gain_out[1, 1:2, :] = gains1[0:1, :]
     gain_out[0, 1:2, :] = gains0[0:1, :]
-    firsts = plain(F_FIRST, 40)
-    first_out[0] = firsts[0:33, 0:64]
-    first_out[1] = firsts[0:33, 128:192]
-    short = halves(F_SHORT, 16)[0]
+    first_out[0] = plain(late, 0, FIRST_ROWS)[0:33, 0:64]
+    first_out[1] = plain(early, E_FIRST, FIRST_ROWS)[0:33, 0:64]
+    short = halves(early, E_SHORT, 16)[0]
     for t in range(3):
         short_out[1, t] = short[3 * t : 3 * t + 3, :]
-    mine_rows = lambda row, rows: halves(F_ROWS + row, rows)
-    second_out[1] = mine_rows(C_SECOND1, 64)[0]
-    second_out[0] = mine_rows(C_SECOND0, 64)[0]
-    skip_out[...] = mine_rows(C_SKIP, 8)[0][0:2]
-    tokens = [halves(F_TOKEN, 48), mine_rows(C_TOKEN, 48), mine_rows(C_TOKEN + 48, 48)]
+    second_out[1] = halves(early, E_ROWS + EM_SECOND, 64)[0]
+    second_out[0] = halves(late, FIRST_ROWS + L_SECOND, 64)[0]
+    skip_out[0:1, :] = halves(late, FIRST_ROWS + L_SKIP, 8)[0][0:1]
+    skip_out[1:2, :] = halves(early, E_ROWS + EM_SKIP, 8)[0][0:1]
+    tokens = [
+        halves(early, E_TOKEN, 48),
+        halves(late, FIRST_ROWS + L_TOKEN, 48),
+        halves(late, FIRST_ROWS + L_TOKEN + 48, 48),
+    ]
     normal, scale = unit(embed[...])
     gain_row = gain[0, 0:1, :]
     low = (normal * gain_row).astype(bf16)
@@ -1314,42 +1415,32 @@
                 summed += pack[row : row + 1, :] * part
                 if h == 0:
                     short_out[0, t, g : g + 1, :] = jnp.sum(table * part, axis=0, keepdims=True)
+            high, rest = split(summed)
             if h == 0:
-                in_out[g] = lax.dot_general(
-                    low.astype(f32), summed, (((0,), (0,)), ((), ())), precision=precise, preferred_element_type=f32
-                )
-                weight = w_own[0, g].astype(f32)
+                in_out[g] = mm_tn(low, high) + mm_tn(low, rest)
+                weight = w_own[0, g]
             else:
-                rows = slice(128 * g, 128 * g + 128)
+                rows = slice(1152 + 128 * g, 1280 + 128 * g)
                 a, b = w_first[rows, :], w_second[rows, :]
-                weight = jnp.concatenate([pick(a, b), pick(b, a)], axis=0)
-            grad_normed += lax.dot_general(
-                summed, weight, (((1,), (1,)), ((), ())), precision=precise, preferred_element_type=f32
-            )
+                weight = jnp.concatenate([pick(a, b), pick(b, a)], axis=0).astype(bf16)
+            grad_normed += mm_nt(high, weight) + mm_nt(rest, weight)
     gain_out[0, 0:1, :] = jnp.sum(grad_normed * normal, axis=0, keepdims=True)
-    embed_out[...] = plain(F_EMBED, 16) + unit_back(grad_normed * gain_row, normal, scale)
-
-
-def send_in_kernel(s, w_in, out):
-    first = s[0] == 0
-    for g in range(3):
-        a, b = w_in[0, g, 0:128, :].astype(f32), w_in[0, g, 128:256, :].astype(f32)
-        out[128 * g : 128 * g + 128, :] = jnp.where(first, a, b)
+    embed_out[...] = plain(early, E_EMBED, 16) + unit_back(grad_normed * gain_row, normal, scale)
 
 
 def block_send_kernel(s, block_out, mine, other):
-    spot = s[4]
+    spot = s[SPOT]
     mine[...] = block_out[at(HALO + 128 * spot, 128), :]
-    near = spot + 1 - 2 * s[0]
+    near = spot + 1 - 2 * s[CORE]
     other[...] = block_out[at(HALO + 128 * near, 128), :]
 
 
 def block_pick_kernel(s, mine, received, out):
-    out[...] = jnp.where(s[5] == 1, mine[...], received[...])
+    out[...] = jnp.where(s[HOLDER] == 1, mine[...], received[...])
 
 
 def block_join_kernel(s, here, there, out):
-    first = s[1] == 0
+    first = s[GROUP] == 0
     out[0] = jnp.where(first, here[...], there[...])
     out[1] = jnp.where(first, there[...], here[...])
 
@@ -1366,126 +1457,129 @@
     half = length // 2
     span = half + 2 * HALO
     core = rank % 2
-    swaps = [(i, i ^ 1) for i in range(count)]
     across = lambda v: lax.ppermute(v, "ch", [(0, 1), (1, 0)])
-    beside = lambda v: lax.ppermute(v, "seq", swaps)
+    trade = lambda v, bit: lax.ppermute(v, "seq", [(i, i ^ bit) for i in range(count)])
+    beside = lambda v: trade(v, 1)
     half_ranks = count // 2
-    holder = (rank // half_ranks == core).astype(jnp.int32)
-    s = jnp.stack([core, group, live[group], group ^ core, rank % half_ranks, holder]).astype(jnp.int32)
+    table = jnp.asarray(number_table(count))[rank, group]
     dft = jnp.asarray(dft_table()).astype(bf16)
     twiddle = jnp.asarray(twiddle_table())
     feats = jnp.asarray(feature_table(length))
     feats_turned = jnp.asarray(np.pad(feature_table(length).T, ((0, 40 - FEAT), (0, 0)))).astype(bf16)
     rates = jnp.asarray(rate_table())
-
+    low = lambda *shape: arr(*shape, kind=bf16)
+    line = pltpu.VMEM((length + 2 * HALO, 128), f32)
+    conv_scratch = [stage_scratch(), spec_scratch(), line]
+
+    s = run(numbers_kernel, arr(NUMBER_ROWS, 128, kind=jnp.int32), table, live.reshape(1, 2))
+    row_shape = lambda rows: arr(rows, 8, width, kind=jnp.int32)
+    own_ids = run(ids_kernel, row_shape(1), s, ids)
     in_own = jnp.swapaxes(in_weight, 1, 2)
-    pack = run(pack_kernel, arr(PACK_ROWS, 128), s, embed, norm_gain, in_own, filter_second, short_kernel, skip_gain)
+    pack = run(pack_kernel, arr(PACK_ROWS, 128), s, embed, norm_gain, in_own, filter_second, short_kernel, skip_gain, after=(own_ids,))
     pack_in = across(pack)
-    own_ids = lax.dynamic_index_in_dim(ids, group, 0, True)
-    all_ids = lax.all_to_all(jnp.broadcast_to(own_ids, (count, width)), "seq", split_axis=0, concat_axis=0, tiled=True)
-    cot = lax.all_gather(lax.dynamic_index_in_dim(cotangent, group, 0, False), "seq", axis=0, tiled=True)
-
+    parts = run(
+        send_weights_kernel, [arr(1536, 128), arr(1536, 128)], s, out_weight, up_weight, down_weight, in_own, hbm=(0, 1, 2, 3),
+        scratch=[
+            pltpu.VMEM(w.shape, w.dtype) for w in (out_weight, up_weight, down_weight, in_own)
+        ] + [pltpu.SemaphoreType.DMA((4,))], after=(pack,),
+    )
+    parts_in = [across(parts[0])]
+    all_ids = run(functools.partial(pair_kernel, 1), row_shape(2), s, own_ids, trade(own_ids, 2), after=(parts[0],))
+    parts_in.append(across(parts[1]))
+    all_ids = run(functools.partial(pair_kernel, 2), row_shape(4), s, all_ids, trade(all_ids, 4))
     sine, cosine, sine_turned = run(
-        sine_kernel, [arr(length, 128), arr(length, 128), arr(128, length, kind=bf16)], s, feats, filter_first
-    )
-    weights = []
-    for level, with_in in ((0, False), (1, True)):
-        rows = 1536 if with_in else 1152
-        part = run(
-            functools.partial(send_weights_kernel, level, with_in), arr(rows, 128), s, out_weight, up_weight, down_weight, in_own
-        )
-        part_in = across(part)
-        other_in = beside(part_in)
-        shapes = [arr(256, 256, kind=bf16), arr(256, 1024, kind=bf16), arr(1024, 256, kind=bf16)]
-        if with_in:
-            shapes.append(arr(256, 768, kind=bf16))
-        weights.append(
-            run(
-                functools.partial(join_weights_kernel, level, with_in), shapes, s, out_weight, up_weight, down_weight, in_own,
-                part_in, other_in,
-            )
-        )
-    (w_out0, w_up0, w_down0), (w_out1, w_up1, w_down1, w_in1) = weights
-    first_in = across(run(send_in_kernel, arr(384, 128), s, in_own))
-    first_in_other = beside(first_in)
-
+        sine_kernel, [arr(length, 128), arr(length, 128), low(128, length)], s, feats, filter_first, after=(all_ids,)
+    )
+    all_ids = run(functools.partial(pair_kernel, 3), row_shape(8), s, all_ids, trade(all_ids, 8), after=(sine,))
+    all_ids = run(functools.partial(pair_kernel, 0), row_shape(16), s, all_ids, beside(all_ids))
+
+    cot = run(pick_kernel, arr(1, width, 256), s, cotangent, after=(sine,))
+    cot = run(functools.partial(pair_kernel, 1), arr(2, width, 256), s, cot, trade(cot, 2), after=(all_ids,))
+    cot = run(functools.partial(pair_kernel, 2), arr(4, width, 256), s, cot, trade(cot, 4))
+    cot = run(functools.partial(pair_kernel, 0), arr(8, width, 256), s, cot, beside(cot))
+    cot_far = lax.ppermute(cot, "seq", [(i, i ^ 8) for i in range(count) if i % 2 == i // half_ranks])
+
+    onehot, turned = run(
+        onehot_kernel, [low(length + 2 * HALO, 128), low(2, 128, half)], s, all_ids,
+        scratch=[pltpu.VMEM((length + 2 * HALO, 128), f32)],
+    )
     mine, other, conv_table, gate_table = run(
-        table_kernel,
-        [arr(PACK_ROWS, 128), arr(PACK_ROWS, 128), arr(128, 256, kind=bf16), arr(128, 512, kind=bf16)],
-        s, pack, pack_in, embed,
+        table_kernel, [arr(PACK_ROWS, 128), arr(PACK_ROWS, 128), low(128, 256), low(128, 512)], s, pack, pack_in, embed,
     )
     filt0, filt1, freq0, freq1 = run(
         filter_kernel, [arr(length, 128), arr(length, 128), arr(*SPECTRUM), arr(*SPECTRUM)], s, sine, mine, rates, dft, twiddle,
         scratch=[stage_scratch(), spec_scratch()],
     )
-    onehot, turned = run(
-        onehot_kernel, [arr(length + 2 * HALO, 128, kind=bf16), arr(2, 128, half, kind=bf16)], s, all_ids,
-        scratch=[pltpu.VMEM((length + 2 * HALO, 128), f32)],
-    )
-    line = pltpu.VMEM((length + 2 * HALO, 128), f32)
-    conv_scratch = [stage_scratch(), spec_scratch(), line]
-
+    first_part = run(relay_kernel, arr(1536, 128), s, parts_in[0], after=(freq1,))
+    first_beside = beside(first_part)
     conv_mine0, sent, spec0, product0 = run(
         conv_first_kernel, [arr(span, 128), arr(span, 128), arr(*SPECTRUM), arr(length, 128)],
-        s, onehot, conv_table, mine, freq0, dft, twiddle, scratch=conv_scratch,
+        s, onehot, conv_table, mine, freq0, dft, twiddle, scratch=conv_scratch, after=(first_part,),
     )
     conv_other0 = beside(sent)
+    w_out0, w_up0, w_down0, w_in1 = run(
+        functools.partial(join_weights_kernel, 0), [low(256, 256), low(256, 1024), low(1024, 256), low(256, 768)],
+        s, out_weight, up_weight, down_weight, in_own, first_part, first_beside, after=(sent,),
+    )
     kept, sent, mid0, stream1, gates1, mixed1 = run(
         forward_first_kernel,
         [arr(half, 128), arr(half, 128), arr(span, 256), arr(span, 256), arr(span, 768), arr(span, 768)],
         s, onehot, gate_table, conv_mine0, conv_other0, norm_gain, w_out0, w_up0, w_down0, w_in1, mine, other,
     )
     received = beside(sent)
+    second_part = run(relay_kernel, arr(1536, 128), s, parts_in[1], after=(sent,))
+    second_beside = beside(second_part)
     conv_mine1, sent, spec1, product1 = run(
         conv_second_kernel, [arr(span, 128), arr(span, 128), arr(*SPECTRUM), arr(length, 128)],
-        s, kept, received, mine, freq1, dft, twiddle, scratch=conv_scratch,
+        s, kept, received, mine, freq1, dft, twiddle, scratch=conv_scratch, after=(second_part,),
     )
     conv_other1 = beside(sent)
-    low = lambda *shape: arr(*shape, kind=bf16)
+    w_out1, w_up1, w_down1 = run(
+        functools.partial(join_weights_kernel, 1), [low(256, 256), low(256, 1024), low(1024, 256)],
+        s, out_weight, up_weight, down_weight, in_own, second_part, second_beside, after=(sent,),
+    )
+    cot_rim = beside(run(rim_kernel, arr(HALO, 256), s, cot, cot_far, after=(sent,)))
     (kept, sent, grad_x0, grad_mid1, block, hidden, grad_low, normed, grad_pre, gated, mid_low, gain_mid1) = run(
         turn_back_kernel,
         [
             arr(half, 128), arr(half, 128), arr(span, 256), arr(span, 256), arr(span, 256), low(span, 1024), low(span, 256),
             low(span, 256), low(span, 1024), low(span, 256), low(span, 256), arr(8, 256),
         ],
-        s, conv_mine1, conv_other1, gates1, stream1, cot, norm_gain, w_out1, w_up1, w_down1,
+        s, conv_mine1, conv_other1, gates1, stream1, cot, cot_far, cot_rim, norm_gain, w_out1, w_up1, w_down1,
         scratch=[pltpu.VMEM((span, 256), f32), pltpu.VMEM((span, 256), f32)],
     )
     received = beside(sent)
-    grads_keep, grads_send = run(
+    grads_keep1, grads_send1 = run(
         functools.partial(wide_grads_kernel, HALO), [arr(2, 1152, 128), arr(2, 1152, 128)],
         s, gated, mid_low, normed, grad_pre, hidden, grad_low,
     )
     block_mine, block_other = run(block_send_kernel, [arr(width, 256), arr(width, 256)], s, block)
-    block_here = run(block_pick_kernel, arr(width, 256), s, block_mine, beside(block_other))
-    block_out = run(block_join_kernel, arr(2, width, 256), s, block_here, across(block_here))
+    grads_in1 = beside(grads_send1)
+    block_beside = beside(block_other)
 
     prod_mine, sent, spec_grad1, grads1 = run(
         conv_back_kernel, [arr(span, 128), arr(span, 128), arr(*SPECTRUM), arr(length, 128)],
-        s, kept, received, mine, freq1, dft, twiddle, scratch=conv_scratch,
+        s, kept, received, mine, freq1, dft, twiddle, scratch=conv_scratch, after=(grads_send1, block_mine),
     )
     prod_other = beside(sent)
+    own1, peer1 = run(add_kernel, [arr(1152, 128), arr(1152, 128)], s, grads_keep1, grads_in1, after=(sent,))
+    across1 = across(peer1)
     filter_shapes = [arr(64, 128), arr(40, 64), arr(8, 128)]
-    filter_scratch = [stage_scratch(), spec_scratch(), pltpu.VMEM((length, 128), f32), pltpu.VMEM((8, 128), f32)]
+    filter_scratch = [stage_scratch(), spec_scratch(), pltpu.VMEM((length, 128), f32)]
     second1, first1, skip1 = run(
-        functools.partial(filter_back_kernel, 1), filter_shapes, s, spec_grad1, spec1, grads1, product1, filt1, cosine,
-        sine_turned, mine, rates, feats_turned, dft, twiddle, scratch=filter_scratch,
-    )
-
-    def reduce_wide(keep, send, with_in):
-        rows = keep.shape[1]
-        own, peer = run(add_kernel, [arr(rows, 128), arr(rows, 128)], s, keep, beside(send))
-        total = run(add_one_kernel, arr(rows, 128), s, own, across(peer))
-        shapes = [arr(128, 256), arr(256, 512), arr(512, 256)] + ([arr(3, 256, 128)] if with_in else [])
-        return run(functools.partial(spread_grads_kernel, with_in), shapes, s, total, beside(total))
-
-    grad_out1, grad_up1, grad_down1 = reduce_wide(grads_keep, grads_send, False)
+        filter_back_kernel, filter_shapes, s, spec_grad1, spec1, grads1, product1, filt1, cosine,
+        sine_turned, mine, rates, feats_turned, dft, twiddle, scratch=filter_scratch, after=(peer1,),
+    )
     grad_stream1, normed_in, mixed_low, short1, gain_in1 = run(
         back_gates_kernel,
         [arr(half, 256), low(half, 256), low(half, 768), arr(3, 8, 768), arr(8, 256)],
         s, prod_mine, prod_other, grad_x0, gates1, mixed1, grad_mid1, stream1, norm_gain, mine, other, w_in1,
-        scratch=[pltpu.VMEM((span, 768), f32)],
-    )
+        scratch=[pltpu.VMEM((span, 768), f32)], after=(skip1,),
+    )
+    in_keep, in_send = run(in_grads_kernel, [arr(2, 384, 128), arr(2, 384, 128)], s, normed_in, mixed_low)
+    in_beside = beside(in_send)
+    block_here = run(block_pick_kernel, arr(width, 256), s, block_mine, block_beside, after=(in_send,))
+    block_across = across(block_here)
     (kept, sent, hidden, grad_low, normed, grad_pre, gated, mid_low, by_token0, gain_mid0) = run(
         back_first_kernel,
         [
@@ -1493,45 +1587,67 @@
             low(half, 256), arr(48, 768), arr(8, 256),
         ],
         s, grad_stream1, mid0, onehot, turned, gate_table, conv_mine0, conv_other0, norm_gain, w_out0, w_up0, w_down0,
+        after=(in_send, block_here),
     )
     received = beside(sent)
-    grads_keep, grads_send = run(
-        wide_and_in_grads_kernel, [arr(2, 1536, 128), arr(2, 1536, 128)],
-        s, gated, mid_low, normed, grad_pre, hidden, grad_low, normed_in, mixed_low,
-    )
-    grad_out0, grad_up0, grad_down0, grad_in1 = reduce_wide(grads_keep, grads_send, True)
-    spec_grad0, grads0, by_token12 = run(
-        conv_back_first_kernel, [arr(*SPECTRUM), arr(length, 128), arr(48, 256)],
-        s, kept, received, mine, freq0, dft, twiddle, onehot, turned, conv_table, scratch=conv_scratch,
-    )
-    second0, first0, skip0 = run(
-        functools.partial(filter_back_kernel, 0), filter_shapes, s, spec_grad0, spec0, grads0, product0, filt0, cosine,
-        sine_turned, mine, rates, feats_turned, dft, twiddle, scratch=filter_scratch,
-    )
-    flat, parts = run(
-        small_kernel, [arr(F_ROWS, 256), arr(C_ROWS, 128)],
-        s, gain_mid1, gain_in1, gain_mid0, by_token0, by_token12, first1, first0, short1, second1, second0, skip1, skip0,
-    )
-    here = run(chip_kernel, arr(F_ROWS + C_ROWS, 256), s, flat, beside(flat), parts, beside(parts))
+    block_out = run(block_join_kernel, arr(2, width, 256), s, block_here, block_across, after=(sent,))
+    grads_keep0, grads_send0 = run(
+        functools.partial(wide_grads_kernel, 0), [arr(2, 1152, 128), arr(2, 1152, 128)],
+        s, gated, mid_low, normed, grad_pre, hidden, grad_low, after=(block_out,),
+    )
+    grads_in0 = beside(grads_send0)
+    in_own1, in_peer1 = run(add_kernel, [arr(384, 128), arr(384, 128)], s, in_keep, in_beside, after=(grads_send0,))
+    in_across = across(in_peer1)
+    early_flat, early_mine = run(
+        early_kernel, [arr(E_ROWS, 256), arr(EM_ROWS, 128)],
+        s, gain_mid1, gain_in1, gain_mid0, by_token0, first1, short1, second1, skip1, after=(in_peer1,),
+    )
+    early_flat_in, early_mine_in = beside(early_flat), beside(early_mine)
+    spec_grad0, grads0 = run(
+        grad_freq_kernel, [arr(*SPECTRUM), arr(length, 128)], s, kept, received, dft, twiddle, scratch=[stage_scratch()],
+        after=(grads_send0, in_peer1, early_flat),
+    )
+    own0, peer0 = run(add_kernel, [arr(1152, 128), arr(1152, 128)], s, grads_keep0, grads_in0, after=(spec_grad0,))
+    across0 = across(peer0)
+    early = run(chip_kernel, arr(E_ROWS + EM_ROWS, 256), s, early_flat, early_flat_in, early_mine, early_mine_in, after=(peer0,))
+    early_in = across(early)
+    total1 = run(add_one_kernel, arr(1152, 128), s, own1, across1, after=(peer0,))
+    in_total = run(add_one_kernel, arr(384, 128), s, in_own1, in_across, after=(peer0,))
+    total1_beside, in_total_beside = beside(total1), beside(in_total)
+    second0, first0, skip0, by_token12 = run(
+        token_back_kernel, filter_shapes + [arr(48, 256)], s, spec_grad0, spec0, grads0, product0, filt0, cosine,
+        sine_turned, mine, rates, feats_turned, dft, twiddle, freq0, onehot, turned, conv_table, scratch=filter_scratch,
+        after=(peer0, early, total1, in_total),
+    )
+    late_mine, late_first = run(late_kernel, [arr(L_ROWS, 128), arr(FIRST_ROWS, 128)], s, by_token12, second0, skip0, first0, after=(early_in,))
+    late = run(chip_kernel, arr(FIRST_ROWS + L_ROWS, 256), s, late_first, beside(late_first), late_mine, beside(late_mine))
+    late_in = across(late)
+    total0 = run(add_one_kernel, arr(1152, 128), s, own0, across0, after=(late,))
+    total0_beside = beside(total0)
+    grad_out, grad_up, grad_down = run(
+        spread_wide_kernel, [arr(2, 128, 256), arr(2, 256, 512), arr(2, 512, 256)],
+        s, total1, total1_beside, total0, total0_beside,
+    )
     grad_embed, grad_gain, grad_in0, grad_short, grad_first, grad_second, grad_skip = run(
         last_kernel,
         [
             arr(16, 256), arr(2, 2, 256), arr(3, 256, 128), arr(2, 3, 3, 128), arr(2, FEAT, 64), arr(2, 64, 128), arr(2, 128),
         ],
-        s, here, across(here), embed, norm_gain, pack, pack_in, in_own, first_in, first_in_other,
-    )
+        s, early, early_in, late, late_in, embed, norm_gain, pack, pack_in, in_own, second_part, second_beside,
+    )
+    grad_in = run(spread_in_kernel, arr(2, 3, 256, 128), s, grad_in0, in_total, in_total_beside)
     return (
         block_out,
         grad_embed,
         grad_gain,
-        jnp.swapaxes(jnp.stack([grad_in0, grad_in1]), 1, 2),
+        jnp.swapaxes(grad_in, 1, 2),
         grad_short,
         grad_first,
         grad_second,
         grad_skip,
-        jnp.stack([grad_out0, grad_out1]),
-        jnp.stack([grad_up0, grad_up1]),
-        jnp.stack([grad_down0, grad_down1]),
+        grad_out,
+        grad_up,
+        grad_down,
     )
 
 
@@ -1567,6 +1683,7 @@
 
     def either(*args):
         length = args[0].shape[1] * lax.axis_size("seq")
-        return (chip_local if length == BLOCKS * BLOCK else local)(*args)
+        near = length == BLOCKS * BLOCK and lax.axis_size("seq") == 16
+        return (chip_local if near else local)(*args)
 
     return jax.shard_map(either, mesh=mesh, in_specs=in_specs, out_specs=out_specs, check_vma=False)

time: 268 us -> 158 us (0.59)
  waiting for transfers between devices: 81.8 us -> 20.7 us
  local copies, waits for them, and re-layouts: 40 us -> 11.2 us
  Pallas kernels: 105 us -> 88 us
  starting transfers between devices: 20.6 us -> 35.7 us
  between operations: 15.2 us -> 1.55 us
  other arithmetic: 3.76 us -> 0 us
    ppermute x8 -> x9, waiting for transfers between devices: 72.6 us -> 15.9 us  [chip_local(): across = lambda v: lax.ppermute(v, 'ch', [(0, 1), (1, 0)])]
    unnamed x178 -> x98, local copies, waits for them, and re-layouts: 36.8 us -> 10.5 us
    ppermute x16 -> x28, starting transfers between devices: 2.67 us -> 25.7 us  [the longest x27 22.4 us: chip_local(): lax.ppermute(v, 'seq', [(i, i ^ bit) for i in range(count)])]
    pallas_call x34 -> x50, Pallas kernels: 105 us -> 88 us  [run(): pl.pallas_call(call, out_shape=shapes, in_specs=[vmem] + [far if i in hbm...]
    all_to_all x1 -> x0, starting transfers between devices: 6.57 us -> none  [chip_local(): lax.all_to_all(jnp.broadcast_to(own_ids, (count, width)), 'seq', split_ax...]
    ppermute x16 -> x28, waiting for transfers between devices: 9.23 us -> 4.85 us  [the longest x27 4.85 us: chip_local(): lax.ppermute(v, 'seq', [(i, i ^ bit) for i in range(count)])]
    another operation x3 -> x0, other arithmetic: 2.8 us -> none  [the longest x1 1.04 us: chip_local(): jnp.stack([grad_down0, grad_down1])]
    ppermute x8 -> x9, starting transfers between devices: 11.4 us -> 9.99 us  [chip_local(): across = lambda v: lax.ppermute(v, 'ch', [(0, 1), (1, 0)])]
  transfers between devices with their start and end apart: 26 -> 37, of which waited for: 12 -> 7; matrix products, arithmetic and copies ran while one was open for 1% -> 1% of each run, Pallas kernels for 28% -> 51%
where the time goes in v2:
time: 158 us; the launch traced here: 157 us
  Pallas kernels  88 us (56%)
  starting transfers between devices  35.7 us (23%)
  waiting for transfers between devices  20.7 us (13%)
  local copies, waits for them, and re-layouts  11.2 us (7%)
    pallas_call x50, Pallas kernels, run(): pl.pallas_call(call, out_shape=shapes, in_specs=[vmem] + [far if i in hbm...  88 us
    ppermute x27, starting transfers between devices, chip_local(): lax.ppermute(v, 'seq', [(i, i ^ bit) for i in range(count)])  22.4 us
    ppermute x9, waiting for transfers between devices, chip_local(): across = lambda v: lax.ppermute(v, 'ch', [(0, 1), (1, 0)])  15.9 us
    unnamed x98, local copies, waits for them, and re-layouts  10.5 us
    ppermute x9, starting transfers between devices, chip_local(): across = lambda v: lax.ppermute(v, 'ch', [(0, 1), (1, 0)])  9.99 us
    ppermute x27, waiting for transfers between devices, chip_local(): lax.ppermute(v, 'seq', [(i, i ^ bit) for i in range(count)])  4.85 us
    ppermute x1, starting transfers between devices, chip_local(): lax.ppermute(cot, 'seq', [(i, i ^ 8) for i in range(count) if i % 2 == i...  3.24 us
  transfers between devices with their start and end apart: 37, of which 7 were waited for; matrix products, arithmetic and copies ran while one was open for 1% of the time, Pallas kernels for 51%

profile of v2, /device:TPU:0, one launch (start us, length us, event | category | flops | bytes accessed | tf_op | source)
XLA Modules:
  0.0 157.1 jit_solution(13812006142839810390)
XLA Ops:
  2.8 3.0 %collective-permute-start = (s32[1,8,128]{2,1,0:T(8,128)S(1)}, s32[1,8,128]{2,1,0:T(8,128)S(1)}, u32[]{:S(2)}, u32[]{:S(2)}) collective-permute-start(s32[1,8,128]{2,1,0:T(8,128)S(1)} %ids_kernel.1.refs_6_.refs_0_), channel_id=1, source_target_pairs={{0,4},{2,6},{4,0},{6,2},{8,12},{10,14},{12,8},{14,10},{16,20},{18,... | collective-permute-start | bytes 12296 | tf_op jit(solution)/shard_map/ppermute | solution.py:1461
  7.1 1.5 send_weights_kernel.1
  8.7 1.6 %collective-permute-start.1 = (s32[2,8,128]{2,1,0:T(8,128)S(1)}, s32[2,8,128]{2,1,0:T(8,128)S(1)}, u32[]{:S(2)}, u32[]{:S(2)}) collective-permute-start(s32[2,8,128]{2,1,0:T(8,128)S(1)} %pair_kernel.7.refs_0_), channel_id=1, source_target_pairs={{0,8},{2,10},{4,12},{6,14},{8,0},{10,2},{12,4},{14,6},{16,24},{18,... | collective-permute-start | bytes 24584 | tf_op jit(solution)/shard_map/ppermute | solution.py:1461
  13.9 2.7 %collective-permute-start.2 = (s32[4,8,128]{2,1,0:T(8,128)S(1)}, s32[4,8,128]{2,1,0:T(8,128)S(1)}, u32[]{:S(2)}, u32[]{:S(2)}) collective-permute-start(s32[4,8,128]{2,1,0:T(8,128)S(1)} %pair_kernel.8.refs_2_.refs_0_), channel_id=1, source_target_pairs={{0,16},{2,18},{4,20},{6,22},{8,24},{10,26},{12,28},{14,30},{16,0},... | collective-permute-start | bytes 49160 | tf_op jit(solution)/shard_map/ppermute | solution.py:1461
  16.6 3.8 %sine_kernel.1 = (f32[2048,128]{1,0:T(8,128)S(1)}, f32[2048,128]{1,0:T(8,128)S(1)}, bf16[128,2048]{1,0:T(8,128)(2,1)S(1)}) custom-call(s32[16,128]{1,0:T(8,128)S(1)} %numbers_kernel.1.table, f32[2048,33]{1,0:T(8,128)S(1)} %copy-done.23, f32[2,33,64]{2,1,0:T(8,128)S(1)} %copy.31.refs_1_, s32[4,8,128]{2,1,0:T(8,128)S(1)} %pair_kernel.8.refs_2_.refs_0_), custom_call_target="tpu_custom_call" | custom-call | flops 10000000000 | bytes 1 | tf_op jit(solution)/shard_map/sine_kernel/pallas_call | solution.py:500
  23.8 2.8 %collective-permute-done.11.refs_1_ = f32[1,128,256]{2,1,0:T(8,128)S(1)} collective-permute-done((f32[1,128,256]{2,1,0:T(8,128)S(1)}, f32[1,128,256]{2,1,0:T(8,128)S(1)}, u32[]{:S(2)}, u32[]{:S(2)}) %collective-permute-start.11) | collective-permute-done | bytes 131104 | tf_op jit(solution)/shard_map/ppermute | solution.py:1461
  27.2 7.8 %filter_kernel.1 = (f32[2048,128]{1,0:T(8,128)S(1)}, f32[2048,128]{1,0:T(8,128)S(1)}, f32[9,256,256]{2,1,0:T(8,128)S(1)}, f32[9,256,256]{2,1,0:T(8,128)S(1)}) custom-call(s32[16,128]{1,0:T(8,128)S(1)} %numbers_kernel.1.table, f32[2048,128]{1,0:T(8,128)S(1)} %get-tuple-element.116.refs_2_.refs_0_.refs_1_, ...), custom_call_target="tpu_custom_call" | custom-call | flops 10000000000 | bytes 1 | tf_op jit(solution)/shard_map/filter_kernel/pallas_call | solution.py:500
  36.4 7.6 %conv_first_kernel.1 = (f32[1056,128]{1,0:T(8,128)S(1)}, f32[1056,128]{1,0:T(8,128)S(1)}, f32[9,256,256]{2,1,0:T(8,128)S(1)}, f32[2048,128]{1,0:T(8,128)S(1)}) custom-call(s32[16,128]{1,0:T(8,128)S(1)} %numbers_kernel.1.table, bf16[2080,128]{1,0:T(8,128)(2,1)S(1)} %get-tuple-element.117.refs_0_.refs_2_.refs_13_, ...), custom_call_target="tpu_custom_call" | custom-call | flops 10000000000 | bytes 1 | tf_op jit(solution)/shard_map/conv_first_kernel/pallas_call | solution.py:500
  44.2 3.2 %collective-permute-start.14 = (f32[8,128,256]{2,1,0:T(8,128)S(1)}, f32[8,128,256]{2,1,0:T(8,128)S(1)}, u32[]{:S(2)}, u32[]{:S(2)}) collective-permute-start(f32[8,128,256]{2,1,0:T(8,128)S(1)} %pair_kernel.13.refs_0_.refs_4_), channel_id=1, source_target_pairs={{0,16},{4,20},{8,24},{12,28},{18,2},{22,6},{26,10},{30,14},{1,17},... | collective-permute-start | bytes 3145736 | tf_op jit(solution)/shard_map/ppermute | solution.py:1500
  48.0 7.1 %forward_first_kernel.1 = (f32[1024,128]{1,0:T(8,128)S(1)}, f32[1024,128]{1,0:T(8,128)S(1)}, f32[1056,256]{1,0:T(8,128)S(1)}, f32[1056,256]{1,0:T(8,128)S(1)}, f...) custom-call(s32[16,128]{1,0:T(8,128)S(1)} %numbers_kernel.1.table, ...), custom_call_target="tpu_custom_call" | custom-call | flops 10000000000 | bytes 1 | tf_op jit(solution)/shard_map/forward_first_kernel/pallas_call | solution.py:500
  57.1 6.4 %conv_second_kernel.1 = (f32[1056,128]{1,0:T(8,128)S(1)}, f32[1056,128]{1,0:T(8,128)S(1)}, f32[9,256,256]{2,1,0:T(8,128)S(1)}, f32[2048,128]{1,0:T(8,128)S(1)}) custom-call(s32[16,128]{1,0:T(8,128)S(1)} %numbers_kernel.1.table, f32[1024,128]{1,0:T(8,128)S(1)} %get-tuple-element.130.refs_0_, f32[1024,128]{1,0:T(8,128)S(1)} %collective-permute-done.8.refs_1_, ...), custom_call_target="tpu_custom_call" | custom-call | flops 10000000000 | bytes 1 | tf_op jit(solution)/shard_map/conv_second_kernel/pallas_call | solution.py:500
  63.9 8.6 %collective-permute-start.15 = (f32[16,256]{1,0:T(8,128)S(1)}, f32[16,256]{1,0:T(8,128)S(1)}, u32[]{:S(2)}, u32[]{:S(2)}) collective-permute-start(f32[16,256]{1,0:T(8,128)S(1)} %rim_kernel.1), channel_id=1, source_target_pairs={{0,2},{2,0},{4,6},{6,4},{8,10},{10,8},{12,14},{14,12},{16,18},{18,... | collective-permute-start | bytes 49160 | tf_op jit(solution)/shard_map/ppermute | solution.py:1461
  73.4 6.6 %turn_back_kernel.1 = (f32[1024,128]{1,0:T(8,128)S(1)}, f32[1024,128]{1,0:T(8,128)S(1)}, f32[1056,256]{1,0:T(8,128)S(1)}, f32[1056,256]{1,0:T(8,128)S(1)}, f32[1...) custom-call(s32[16,128]{1,0:T(8,128)S(1)} %numbers_kernel.1.table, ...), custom_call_target="tpu_custom_call" | custom-call | flops 10000000000 | bytes 1 | tf_op jit(solution)/shard_map/turn_back_kernel/pallas_call | solution.py:500
  83.5 6.4 %conv_back_kernel.1 = (f32[1056,128]{1,0:T(8,128)S(1)}, f32[1056,128]{1,0:T(8,128)S(1)}, f32[9,256,256]{2,1,0:T(8,128)S(1)}, f32[2048,128]{1,0:T(8,128)S(1)}) custom-call(s32[16,128]{1,0:T(8,128)S(1)} %numbers_kernel.1.table, f32[1024,128]{1,0:T(8,128)S(1)} %get-tuple-element.143.refs_0_, f32[1024,128]{1,0:T(8,128)S(1)} %collective-permute-done.18.refs_1_, ...), custom_call_target="tpu_custom_call" | custom-call | flops 10000000000 | bytes 1 | tf_op jit(solution)/shard_map/conv_back_kernel/pallas_call | solution.py:500
  91.6 4.4 %filter_back_kernel.1 = (f32[64,128]{1,0:T(8,128)S(1)}, f32[40,64]{1,0:T(8,128)S(1)}, f32[8,128]{1,0:T(8,128)S(1)}) custom-call(s32[16,128]{1,0:T(8,128)S(1)} %numbers_kernel.1.table, f32[9,256,256]{2,1,0:T(8,128)S(1)} %get-tuple-element.157.refs_0_, f32[9,256,256]{2,1,0:T(8,128)S(1)} %get-tuple-element.158.refs_1_, ...), custom_call_target="tpu_custom_call" | custom-call | flops 10000000000 | bytes 1 | tf_op jit(solution)/shard_map/filter_back_kernel/pallas_call | solution.py:500
  96.1 5.4 %back_gates_kernel.1 = (f32[1024,256]{1,0:T(8,128)S(1)}, bf16[1024,256]{1,0:T(8,128)(2,1)S(1)}, bf16[1024,768]{1,0:T(8,128)(2,1)S(1)}, f32[3,8,768]{2,1,0:T(8,128)S(1)}, f32[8,256]{1,0:T(8,128)S(1)}) custom-call(s32[16,128]{1,0:T(8,128)S(1)} %numbers_kernel.1.table, f32[1056,128]{1,0:T(8,128)S(1)} %get-tuple-element.152.refs_0_, ...), custom_call_target="tpu_custom_call" | custom-call | flops 10000000000 | bytes 1 | tf_op jit(solution)/shard_map/back_gates_kernel/pallas_call | solution.py:500
  103.8 6.8 %back_first_kernel.1 = (f32[1024,128]{1,0:T(8,128)S(1)}, f32[1024,128]{1,0:T(8,128)S(1)}, bf16[1024,1024]{1,0:T(8,128)(2,1)S(1)}, bf16[1024,256]{1,0:T(8,128)(2,...) custom-call(s32[16,128]{1,0:T(8,128)S(1)} %numbers_kernel.1.table, ...), custom_call_target="tpu_custom_call" | custom-call | flops 10000000000 | bytes 1 | tf_op jit(solution)/shard_map/back_first_kernel/pallas_call | solution.py:500
  112.4 1.5 wide_grads_kernel.3
  116.1 3.0 %grad_freq_kernel.1 = (f32[9,256,256]{2,1,0:T(8,128)S(1)}, f32[2048,128]{1,0:T(8,128)S(1)}) custom-call(s32[16,128]{1,0:T(8,128)S(1)} %numbers_kernel.1.table, f32[1024,128]{1,0:T(8,128)S(1)} %get-tuple-element.193.refs_0_, f32[1024,128]{1,0:T(8,128)S(1)} %collective-permute-done.26.refs_1_, bf16[256,512]{1,0:T(8,128)(2,1)S(1)} %copy-done.24, ...), custom_call_target="tpu_custom_call" | custom-call | flops 10000000000 | bytes 1 | tf_op jit(solution)/shard_map/grad_freq_kernel/pallas_call | solution.py:500
  121.5 1.6 %copy-done.30 = f32[9,256,256]{2,1,0:T(8,128)S(1)} copy-done((f32[9,256,256]{2,1,0:T(8,128)S(1)}, f32[9,256,256]{2,1,0:T(8,128)}, u32[]{:S(2)}) %copy-start.30) | copy-done | bytes 2359320
  123.2 8.4 %token_back_kernel.1 = (f32[64,128]{1,0:T(8,128)S(1)}, f32[40,64]{1,0:T(8,128)S(1)}, f32[8,128]{1,0:T(8,128)S(1)}, f32[48,256]{1,0:T(8,128)S(1)}) custom-call(s32[16,128]{1,0:T(8,128)S(1)} %numbers_kernel.1.table, f32[9,256,256]{2,1,0:T(8,128)S(1)} %get-tuple-element.194.refs_2_.refs_0_, f32[9,256,256]{2,1,0:T(8,128)S(1)} %get-tuple-element.196.refs_1_, ...), custom_call_target="tpu_custom_call" | custom-call | flops 10000000000 | bytes 1 | tf_op jit(solution)/shard_map/token_back_kernel/pallas_call | solution.py:500
  135.8 5.5 %collective-permute-done.32.refs_3_ = f32[208,256]{1,0:T(8,128)S(1)} collective-permute-done((f32[208,256]{1,0:T(8,128)S(1)}, f32[208,256]{1,0:T(8,128)S(1)}, u32[]{:S(2)}, u32[]{:S(2)}) %collective-permute-start.32) | collective-permute-done | bytes 213024 | tf_op jit(solution)/shard_map/ppermute | solution.py:1460
  143.9 9.5 %collective-permute-done.35.refs_1_ = f32[1152,128]{1,0:T(8,128)S(1)} collective-permute-done((f32[1152,128]{1,0:T(8,128)S(1)}, f32[1152,128]{1,0:T(8,128)S(1)}, u32[]{:S(2)}, u32[]{:S(2)}) %collective-permute-start.35) | collective-permute-done | bytes 589856 | tf_op jit(solution)/shard_map/ppermute | solution.py:1460
  155.5 1.6 %spread_wide_kernel.1 = (f32[2,128,256]{2,1,0:T(8,128)}, f32[2,256,512]{2,1,0:T(8,128)}, f32[2,512,256]{2,1,0:T(8,128)}) custom-call(s32[16,128]{1,0:T(8,128)S(1)} %numbers_kernel.1.table, f32[1152,128]{1,0:T(8,128)S(1)} %add_one_kernel.3.refs_18_.refs_0_, f32[1152,128]{1,0:T(8,128)S(1)} %collective-permute-done.34.refs_1_, ...), custom_call_target="tpu_custom_call" | custom-call | flops 10000000000 | bytes 1 | tf_op jit(solution)/shard_map/spread_wide_kernel/pallas_call | solution.py:500
  (199 shorter events, 38.6 us)
Async XLA Ops:
  2.8 5.9 %collective-permute-start = (s32[1,8,128]{2,1,0:T(8,128)S(1)}, s32[1,8,128]{2,1,0:T(8,128)S(1)}, u32[]{:S(2)}, u32[]{:S(2)}) collective-permute-start(s32[1,8,128]{2,1,0:T(8,128)S(1)} %ids_kernel.1.refs_6_.refs_0_), channel_id=1, source_target_pairs={{0,4},{2,6},{4,0},{6,2},{8,12},{10,14},{12,8},{14,10},{16,20},{18,... | collective-permute-start | bytes 12296 | tf_op jit(solution)/shard_map/ppermute | solution.py:1461
  10.3 12.7 %collective-permute-start.4 = (f32[200,128]{1,0:T(8,128)S(1)}, f32[200,128]{1,0:T(8,128)S(1)}, u32[]{:S(2)}, u32[]{:S(2)}) collective-permute-start(f32[200,128]{1,0:T(8,128)S(1)} %pack_kernel.1.refs_4_.refs_0_.refs_6_), channel_id=1, source_target_pairs={{0,1},{1,0},{2,3},{3,2},{4,5},{5,4},{6,7},{7,6},{8,9},{9,8},{10,11... | collective-permute-start | bytes 307208 | tf_op jit(solution)/shard_map/ppermute | solution.py:1460
  11.8 23.3 %collective-permute-start.5 = (f32[1536,128]{1,0:T(8,128)S(1)}, f32[1536,128]{1,0:T(8,128)S(1)}, u32[]{:S(2)}, u32[]{:S(2)}) collective-permute-start(f32[1536,128]{1,0:T(8,128)S(1)} %get-tuple-element.115.refs_2_), channel_id=1, source_target_pairs={{0,1},{1,0},{2,3},{3,2},{4,5},{5,4},{6,7},{7,6},{8,9},{9,8},{10,11... | collective-permute-start | bytes 2359304 | tf_op jit(solution)/shard_map/ppermute | solution.py:1460
  12.4 42.9 %collective-permute-start.9 = (f32[1536,128]{1,0:T(8,128)}, f32[1536,128]{1,0:T(8,128)}, u32[]{:S(2)}, u32[]{:S(2)}) collective-permute-start(f32[1536,128]{1,0:T(8,128)} %get-tuple-element.132), channel_id=1, source_target_pairs={{0,1},{1,0},{2,3},{3,2},{4,5},{5,4},{6,7},{7,6},{8,9},{9,8},{10,11... | collective-permute-start | bytes 2359304 | tf_op jit(solution)/shard_map/ppermute | solution.py:1460
  13.9 6.5 %collective-permute-start.2 = (s32[4,8,128]{2,1,0:T(8,128)S(1)}, s32[4,8,128]{2,1,0:T(8,128)S(1)}, u32[]{:S(2)}, u32[]{:S(2)}) collective-permute-start(s32[4,8,128]{2,1,0:T(8,128)S(1)} %pair_kernel.8.refs_2_.refs_0_), channel_id=1, source_target_pairs={{0,16},{2,18},{4,20},{6,22},{8,24},{10,26},{12,28},{14,30},{16,0},... | collective-permute-start | bytes 49160 | tf_op jit(solution)/shard_map/ppermute | solution.py:1461
  26.7 8.3 %collective-permute-start.12 = (f32[2,128,256]{2,1,0:T(8,128)S(1)}, f32[2,128,256]{2,1,0:T(8,128)S(1)}, u32[]{:S(2)}, u32[]{:S(2)}) collective-permute-start(f32[2,128,256]{2,1,0:T(8,128)S(1)} %pair_kernel.11.refs_0_), channel_id=1, source_target_pairs={{0,8},{2,10},{4,12},{6,14},{8,0},{10,2},{12,4},{14,6},{16,24},{18,... | collective-permute-start | bytes 786440 | tf_op jit(solution)/shard_map/ppermute | solution.py:1461
  35.1 9.0 %collective-permute-start.13 = (f32[4,128,256]{2,1,0:T(8,128)S(1)}, f32[4,128,256]{2,1,0:T(8,128)S(1)}, u32[]{:S(2)}, u32[]{:S(2)}) collective-permute-start(f32[4,128,256]{2,1,0:T(8,128)S(1)} %pair_kernel.12.refs_0_), channel_id=1, source_target_pairs={{0,2},{2,0},{4,6},{6,4},{8,10},{10,8},{12,14},{14,12},{16,18},{18,... | collective-permute-start | bytes 1572872 | tf_op jit(solution)/shard_map/ppermute | solution.py:1461
  35.2 12.2 %collective-permute-start.7 = (f32[1536,128]{1,0:T(8,128)S(1)}, f32[1536,128]{1,0:T(8,128)S(1)}, u32[]{:S(2)}, u32[]{:S(2)}) collective-permute-start(f32[1536,128]{1,0:T(8,128)S(1)} %relay_kernel.2.refs_6_.refs_4_), channel_id=1, source_target_pairs={{0,2},{2,0},{4,6},{6,4},{8,10},{10,8},{12,14},{14,12},{16,18},{18,... | collective-permute-start | bytes 2359304 | tf_op jit(solution)/shard_map/ppermute | solution.py:1461
  44.2 19.6 %collective-permute-start.14 = (f32[8,128,256]{2,1,0:T(8,128)S(1)}, f32[8,128,256]{2,1,0:T(8,128)S(1)}, u32[]{:S(2)}, u32[]{:S(2)}) collective-permute-start(f32[8,128,256]{2,1,0:T(8,128)S(1)} %pair_kernel.13.refs_0_.refs_4_), channel_id=1, source_target_pairs={{0,16},{4,20},{8,24},{12,28},{18,2},{22,6},{26,10},{30,14},{1,17},... | collective-permute-start | bytes 3145736 | tf_op jit(solution)/shard_map/ppermute | solution.py:1500
  56.7 15.8 %collective-permute-start.16 = (f32[1536,128]{1,0:T(8,128)S(1)}, f32[1536,128]{1,0:T(8,128)S(1)}, u32[]{:S(2)}, u32[]{:S(2)}) collective-permute-start(f32[1536,128]{1,0:T(8,128)S(1)} %relay_kernel.3.refs_6_.refs_4_.refs_9_), channel_id=1, source_target_pairs={{0,2},{2,0},{4,6},{6,4},{8,10},{10,8},{12,14},{14,12},{16,18},{18,... | collective-permute-start | bytes 2359304 | tf_op jit(solution)/shard_map/ppermute | solution.py:1461
  63.5 9.9 %collective-permute-start.10 = (f32[1056,128]{1,0:T(8,128)S(1)}, f32[1056,128]{1,0:T(8,128)S(1)}, u32[]{:S(2)}, u32[]{:S(2)}) collective-permute-start(f32[1056,128]{1,0:T(8,128)S(1)} %get-tuple-element.134.refs_2_.refs_6_), channel_id=1, source_target_pairs={{0,2},{2,0},{4,6},{6,4},{8,10},{10,8},{12,14},{14,12},{16,18},{18,... | collective-permute-start | bytes 1622024 | tf_op jit(solution)/shard_map/ppermute | solution.py:1461
  63.9 9.5 %collective-permute-start.15 = (f32[16,256]{1,0:T(8,128)S(1)}, f32[16,256]{1,0:T(8,128)S(1)}, u32[]{:S(2)}, u32[]{:S(2)}) collective-permute-start(f32[16,256]{1,0:T(8,128)S(1)} %rim_kernel.1), channel_id=1, source_target_pairs={{0,2},{2,0},{4,6},{6,4},{8,10},{10,8},{12,14},{14,12},{16,18},{18,... | collective-permute-start | bytes 49160 | tf_op jit(solution)/shard_map/ppermute | solution.py:1461
  82.8 7.4 %collective-permute-start.20 = (f32[2,1152,128]{2,1,0:T(8,128)S(1)}, f32[2,1152,128]{2,1,0:T(8,128)S(1)}, u32[]{:S(2)}, u32[]{:S(2)}) collective-permute-start(f32[2,1152,128]{2,1,0:T(8,128)S(1)} %get-tuple-element.151.refs_6_), channel_id=1, source_target_pairs={{0,2},{2,0},{4,6},{6,4},{8,10},{10,8},{12,14},{14,12},{16,18},{18,... | collective-permute-start | bytes 3538952 | tf_op jit(solution)/shard_map/ppermute | solution.py:1461
  83.1 19.1 %collective-permute-start.17 = (f32[128,256]{1,0:T(8,128)S(1)}, f32[128,256]{1,0:T(8,128)S(1)}, u32[]{:S(2)}, u32[]{:S(2)}) collective-permute-start(f32[128,256]{1,0:T(8,128)S(1)} %get-tuple-element.142), channel_id=1, source_target_pairs={{0,2},{2,0},{4,6},{6,4},{8,10},{10,8},{12,14},{14,12},{16,18},{18,... | collective-permute-start | bytes 393224 | tf_op jit(solution)/shard_map/ppermute | solution.py:1461
  89.9 6.1 %collective-permute-start.19 = (f32[1056,128]{1,0:T(8,128)S(1)}, f32[1056,128]{1,0:T(8,128)S(1)}, u32[]{:S(2)}, u32[]{:S(2)}) collective-permute-start(f32[1056,128]{1,0:T(8,128)S(1)} %get-tuple-element.153.refs_2_), channel_id=1, source_target_pairs={{0,2},{2,0},{4,6},{6,4},{8,10},{10,8},{12,14},{14,12},{16,18},{18,... | collective-permute-start | bytes 1622024 | tf_op jit(solution)/shard_map/ppermute | solution.py:1461
  90.4 30.2 %collective-permute-start.28 = (f32[1152,128]{1,0:T(8,128)S(1)}, f32[1152,128]{1,0:T(8,128)S(1)}, u32[]{:S(2)}, u32[]{:S(2)}) collective-permute-start(f32[1152,128]{1,0:T(8,128)S(1)} %get-tuple-element.165.refs_12_), channel_id=1, source_target_pairs={{0,1},{1,0},{2,3},{3,2},{4,5},{5,4},{6,7},{7,6},{8,9},{9,8},{10,11... | collective-permute-start | bytes 1769480 | tf_op jit(solution)/shard_map/ppermute | solution.py:1460
  102.2 12.3 %collective-permute-start.22 = (f32[2,384,128]{2,1,0:T(8,128)S(1)}, f32[2,384,128]{2,1,0:T(8,128)S(1)}, u32[]{:S(2)}, u32[]{:S(2)}) collective-permute-start(f32[2,384,128]{2,1,0:T(8,128)S(1)} %get-tuple-element.169.refs_2_.refs_11_), channel_id=1, source_target_pairs={{0,2},{2,0},{4,6},{6,4},{8,10},{10,8},{12,14},{14,12},{16,18},{18,... | collective-permute-start | bytes 1179656 | tf_op jit(solution)/shard_map/ppermute | solution.py:1461
  102.3 8.4 %collective-permute-start.21 = (f32[128,256]{1,0:T(8,128)S(1)}, f32[128,256]{1,0:T(8,128)S(1)}, u32[]{:S(2)}, u32[]{:S(2)}) collective-permute-start(f32[128,256]{1,0:T(8,128)S(1)} %block_pick_kernel.1.refs_12_.refs_0_), channel_id=1, source_target_pairs={{0,1},{1,0},{2,3},{3,2},{4,5},{5,4},{6,7},{7,6},{8,9},{9,8},{10,11... | collective-permute-start | bytes 393224 | tf_op jit(solution)/shard_map/ppermute | solution.py:1460
  114.5 6.9 %collective-permute-start.29 = (f32[384,128]{1,0:T(8,128)S(1)}, f32[384,128]{1,0:T(8,128)S(1)}, u32[]{:S(2)}, u32[]{:S(2)}) collective-permute-start(f32[384,128]{1,0:T(8,128)S(1)} %get-tuple-element.189.refs_8_.refs_5_), channel_id=1, source_target_pairs={{0,1},{1,0},{2,3},{3,2},{4,5},{5,4},{6,7},{7,6},{8,9},{9,8},{10,11... | collective-permute-start | bytes 589832 | tf_op jit(solution)/shard_map/ppermute | solution.py:1460
  119.3 12.2 %collective-permute-start.27 = (f32[208,256]{1,0:T(8,128)S(1)}, f32[208,256]{1,0:T(8,128)S(1)}, u32[]{:S(2)}, u32[]{:S(2)}) collective-permute-start(f32[208,256]{1,0:T(8,128)S(1)} %chip_kernel.2.refs_17_.refs_0_), channel_id=1, source_target_pairs={{0,1},{1,0},{2,3},{3,2},{4,5},{5,4},{6,7},{7,6},{8,9},{9,8},{10,11... | collective-permute-start | bytes 638984 | tf_op jit(solution)/shard_map/ppermute | solution.py:1460
  133.2 8.1 %collective-permute-start.32 = (f32[208,256]{1,0:T(8,128)S(1)}, f32[208,256]{1,0:T(8,128)S(1)}, u32[]{:S(2)}, u32[]{:S(2)}) collective-permute-start(f32[208,256]{1,0:T(8,128)S(1)} %chip_kernel.3.refs_2_), channel_id=1, source_target_pairs={{0,1},{1,0},{2,3},{3,2},{4,5},{5,4},{6,7},{7,6},{8,9},{9,8},{10,11... | collective-permute-start | bytes 638984 | tf_op jit(solution)/shard_map/ppermute | solution.py:1460
  134.2 19.4 %collective-permute-start.33 = (f32[384,128]{1,0:T(8,128)S(1)}, f32[384,128]{1,0:T(8,128)S(1)}, u32[]{:S(2)}, u32[]{:S(2)}) collective-permute-start(f32[384,128]{1,0:T(8,128)S(1)} %add_one_kernel.4.refs_19_.refs_1_), channel_id=1, source_target_pairs={{0,2},{2,0},{4,6},{6,4},{8,10},{10,8},{12,14},{14,12},{16,18},{18,... | collective-permute-start | bytes 589832 | tf_op jit(solution)/shard_map/ppermute | solution.py:1461
  134.2 20.2 %collective-permute-start.34 = (f32[1152,128]{1,0:T(8,128)S(1)}, f32[1152,128]{1,0:T(8,128)S(1)}, u32[]{:S(2)}, u32[]{:S(2)}) collective-permute-start(f32[1152,128]{1,0:T(8,128)S(1)} %add_one_kernel.3.refs_18_.refs_0_), channel_id=1, source_target_pairs={{0,2},{2,0},{4,6},{6,4},{8,10},{10,8},{12,14},{14,12},{16,18},{18,... | collective-permute-start | bytes 1769480 | tf_op jit(solution)/shard_map/ppermute | solution.py:1461
  134.7 18.7 %collective-permute-start.35 = (f32[1152,128]{1,0:T(8,128)S(1)}, f32[1152,128]{1,0:T(8,128)S(1)}, u32[]{:S(2)}, u32[]{:S(2)}) collective-permute-start(f32[1152,128]{1,0:T(8,128)S(1)} %get-tuple-element.195.refs_4_.refs_2_.refs_16_), channel_id=1, source_target_pairs={{0,1},{1,0},{2,3},{3,2},{4,5},{5,4},{6,7},{7,6},{8,9},{9,8},{10,11... | collective-permute-start | bytes 1769480 | tf_op jit(solution)/shard_map/ppermute | solution.py:1460
  (60 other events, 302.1 us)
